TPU v7x, 32 devices: a whole 2x2x4 slice. The times are simulated.
32 devices in a mesh: wide: 8 (over y, x, core), narrow: 4 (over z).
Axes of the slice: x: 2, y: 2, z: 4, core: 2. Of those that a mesh axis runs over, the one named last changes fastest.
Arguments:
- tokens: bfloat16 [49152, 512], P(('wide', 'narrow')), may hold values from -20 to 20
- segment: int32 [49152], P(('wide', 'narrow')), may hold values from 0 to 1535, as said below
- w_query: bfloat16 [512, 512], P(('wide', 'narrow')), may hold values from -0.25 to 0.25
- w_key: bfloat16 [512, 512], P(('wide', 'narrow')), may hold values from -0.25 to 0.25
- w_value: bfloat16 [512, 512], P(('wide', 'narrow')), may hold values from -0.25 to 0.25
- w_output: bfloat16 [512, 512], P(('wide', 'narrow')), may hold values from -1 to 1
- gate_attn: bfloat16 [512, 512], P(('wide', 'narrow')), may hold values from -0.25 to 0.25
- gate_ffn: bfloat16 [512, 512], P(('wide', 'narrow')), may hold values from -0.25 to 0.25
- w_in: bfloat16 [512, 2048], P(('wide', 'narrow')), may hold values from -0.25 to 0.25
- w_out: bfloat16 [2048, 512], P(('wide', 'narrow')), may hold values from -0.125 to 0.125
- norm_attn: bfloat16 [512], P(('wide', 'narrow')), may hold values from 0.5 to 1.5
- norm_ffn: bfloat16 [512], P(('wide', 'narrow')), may hold values from 0.5 to 1.5
- bias_attn: bfloat16 [512], P(('wide', 'narrow')), may hold values from -3 to 3
- bias_ffn: bfloat16 [512], P(('wide', 'narrow')), may hold values from -3 to 3
- out_grad: bfloat16 [49152, 512], P(('wide', 'narrow')), may hold values from -6 to 6
Outputs:
- result: bfloat16 [49152, 512], P(('wide', 'narrow'))
- token_grad: float32 [49152, 512], P(('wide', 'narrow'))
- grad_query: float32 [512, 512], P(('wide', 'narrow'))
- grad_key: float32 [512, 512], P(('wide', 'narrow'))
- grad_value: float32 [512, 512], P(('wide', 'narrow'))
- grad_output: float32 [512, 512], P(('wide', 'narrow'))
- grad_gate_attn: float32 [512, 512], P(('wide', 'narrow'))
- grad_gate_ffn: float32 [512, 512], P(('wide', 'narrow'))
- grad_in: float32 [512, 2048], P(('wide', 'narrow'))
- grad_out: float32 [2048, 512], P(('wide', 'narrow'))
- grad_norm_attn: float32 [512], P(('wide', 'narrow'))
- grad_norm_ffn: float32 [512], P(('wide', 'narrow'))
- grad_bias_attn: float32 [512], P(('wide', 'narrow'))
- grad_bias_ffn: float32 [512], P(('wide', 'narrow'))
- gate_stats: float32 [4, 512], replicated
Inputs may be any that keep to these rules, and one draw needn't show every extreme that they name: `segment`: each token's number is the position, within its device's 1536 tokens, of the first token of its sequence; tokens with one number form one sequence of consecutive tokens; no sequence crosses a device; short sequences have at most 128 tokens, and some devices (at least one in every draw, which ones drawn) hold one sequence of exactly 1024 tokens, the longest.
All inputs are finite; a program needn't handle non-finite values.
Results may differ from a plain program's by a relative error of at most 0.015.
Values may be sent and summed in bfloat16 or wider, within the bound.
No kernel may reach another device: no remote copies, remote signals or barrier semaphores. Data moves between devices by JAX's collectives and lax.ppermute only.
A program may use at most 384 MiB of HBM per device.

v0:
```python
from functools import partial

import jax
import jax.numpy as jnp
from jax import lax
from jax.sharding import PartitionSpec as P

HEADS = 8
HEAD_DIM = 64


EPSILON = 1e-05
MASKED = -1000000000.0


def norm_rows(values, gain):
    center = jnp.mean(values, axis=-1, keepdims=True)
    offset = values - center
    spread = jnp.mean(offset * offset, axis=-1, keepdims=True)
    return offset * lax.rsqrt(spread + EPSILON) * gain


def fetch_forward(
    w_query,
    w_key,
    w_value,
    w_output,
    gate_attn,
    gate_ffn,
    w_in,
    w_out,
    norm_attn,
    norm_ffn,
    bias_attn,
    bias_ffn,
):
    return (
        lax.all_gather(w_query, ("wide", "narrow"), axis=0, tiled=True),
        lax.all_gather(w_key, ("wide", "narrow"), axis=0, tiled=True),
        lax.all_gather(w_value, ("wide", "narrow"), axis=0, tiled=True),
        lax.all_gather(w_output, ("wide", "narrow"), axis=0, tiled=True),
        lax.all_gather(gate_attn, ("wide", "narrow"), axis=0, tiled=True),
        lax.all_gather(gate_ffn, ("wide", "narrow"), axis=0, tiled=True),
        lax.all_gather(w_in, ("wide", "narrow"), axis=0, tiled=True),
        lax.all_gather(w_out, ("wide", "narrow"), axis=0, tiled=True),
        lax.all_gather(norm_attn, ("wide", "narrow"), axis=0, tiled=True),
        lax.all_gather(norm_ffn, ("wide", "narrow"), axis=0, tiled=True),
        lax.all_gather(bias_attn, ("wide", "narrow"), axis=0, tiled=True),
        lax.all_gather(bias_ffn, ("wide", "narrow"), axis=0, tiled=True),
    )


def fetch_backward(
    w_query,
    w_key,
    w_value,
    w_output,
    gate_attn,
    gate_ffn,
    w_in,
    w_out,
    norm_attn,
    norm_ffn,
    bias_attn,
    bias_ffn,
):
    return (
        lax.all_gather(w_query, ("wide", "narrow"), axis=0, tiled=True),
        lax.all_gather(w_key, ("wide", "narrow"), axis=0, tiled=True),
        lax.all_gather(w_value, ("wide", "narrow"), axis=0, tiled=True),
        lax.all_gather(w_output, ("wide", "narrow"), axis=0, tiled=True),
        lax.all_gather(gate_attn, ("wide", "narrow"), axis=0, tiled=True),
        lax.all_gather(gate_ffn, ("wide", "narrow"), axis=0, tiled=True),
        lax.all_gather(w_in, ("wide", "narrow"), axis=0, tiled=True),
        lax.all_gather(w_out, ("wide", "narrow"), axis=0, tiled=True),
        lax.all_gather(norm_attn, ("wide", "narrow"), axis=0, tiled=True),
        lax.all_gather(norm_ffn, ("wide", "narrow"), axis=0, tiled=True),
        lax.all_gather(bias_attn, ("wide", "narrow"), axis=0, tiled=True),
        lax.all_gather(bias_ffn, ("wide", "narrow"), axis=0, tiled=True),
    )


def reduce_grads(
    grad_query,
    grad_key,
    grad_value,
    grad_output,
    grad_gate_attn,
    grad_gate_ffn,
    grad_in,
    grad_out,
    grad_norm_attn,
    grad_norm_ffn,
    grad_bias_attn,
    grad_bias_ffn,
):
    return (
        lax.psum_scatter(grad_query, ("wide", "narrow"), scatter_dimension=0, tiled=True),
        lax.psum_scatter(grad_key, ("wide", "narrow"), scatter_dimension=0, tiled=True),
        lax.psum_scatter(grad_value, ("wide", "narrow"), scatter_dimension=0, tiled=True),
        lax.psum_scatter(grad_output, ("wide", "narrow"), scatter_dimension=0, tiled=True),
        lax.psum_scatter(grad_gate_attn, ("wide", "narrow"), scatter_dimension=0, tiled=True),
        lax.psum_scatter(grad_gate_ffn, ("wide", "narrow"), scatter_dimension=0, tiled=True),
        lax.psum_scatter(grad_in, ("wide", "narrow"), scatter_dimension=0, tiled=True),
        lax.psum_scatter(grad_out, ("wide", "narrow"), scatter_dimension=0, tiled=True),
        lax.psum_scatter(grad_norm_attn, ("wide", "narrow"), scatter_dimension=0, tiled=True),
        lax.psum_scatter(grad_norm_ffn, ("wide", "narrow"), scatter_dimension=0, tiled=True),
        lax.psum_scatter(grad_bias_attn, ("wide", "narrow"), scatter_dimension=0, tiled=True),
        lax.psum_scatter(grad_bias_ffn, ("wide", "narrow"), scatter_dimension=0, tiled=True),
    )


def make_mask(segment, offset, count):
    query_place = offset + jnp.arange(count, dtype=jnp.int32)
    key_place = jnp.arange(segment.shape[0], dtype=jnp.int32)
    own_segment = segment[offset : offset + count]
    return (query_place[:, None] >= key_place[None, :]) & (own_segment[:, None] == segment[None, :])


def block_scores(query_block, keys, segment, offset, half_rows):
    scaling = HEAD_DIM ** (-0.5)
    scores = (
        jnp.einsum("qhd,khd->hqk", query_block, keys, preferred_element_type=jnp.float32) * scaling
    )
    allowed = make_mask(segment, offset, half_rows)
    return jnp.where(allowed[None], scores, MASKED)


def attention_forward(queries, keys, values, segment):
    length = queries.shape[0]
    half_rows = length // 2
    outputs, row_peaks, row_totals = ([], [], [])
    for piece_index in range(2):
        offset = piece_index * half_rows
        query_block = queries[offset : offset + half_rows]
        scores = block_scores(query_block, keys, segment, offset, half_rows)
        row_peak = jnp.max(scores, axis=-1, keepdims=True)
        exponent = jnp.exp(scores - row_peak)
        row_total = jnp.sum(exponent, axis=-1, keepdims=True)
        probability = (exponent / row_total).astype(jnp.bfloat16)
        outputs.append(
            jnp.einsum("hqk,khd->qhd", probability, values, preferred_element_type=jnp.float32)
        )
        row_peaks.append(row_peak)
        row_totals.append(row_total)
    return (jnp.concatenate(outputs, axis=0), row_peaks, row_totals)


def attention_backward(queries, keys, values, segment, grad_mixed, row_peaks, row_totals):
    length = queries.shape[0]
    half_rows = length // 2
    scaling = HEAD_DIM ** (-0.5)
    grad_keys = jnp.zeros(keys.shape, jnp.float32)
    grad_values = jnp.zeros(values.shape, jnp.float32)
    grad_queries = []
    for piece_index in range(2):
        offset = piece_index * half_rows
        query_block = queries[offset : offset + half_rows]
        grad_block = grad_mixed[offset : offset + half_rows]
        scores = block_scores(query_block, keys, segment, offset, half_rows)
        probability = jnp.exp(scores - row_peaks[piece_index]) / row_totals[piece_index]
        grad_probs = jnp.einsum(
            "qhd,khd->hqk", grad_block, values, preferred_element_type=jnp.float32
        )
        inner_sum = jnp.sum(grad_probs * probability, axis=-1, keepdims=True)
        grad_scores = (probability * (grad_probs - inner_sum)).astype(jnp.bfloat16)
        grad_queries.append(
            jnp.einsum("hqk,khd->qhd", grad_scores, keys, preferred_element_type=jnp.float32)
            * scaling
        )
        grad_keys = (
            grad_keys
            + jnp.einsum(
                "hqk,qhd->khd", grad_scores, query_block, preferred_element_type=jnp.float32
            )
            * scaling
        )
        grad_values = grad_values + jnp.einsum(
            "hqk,qhd->khd",
            probability.astype(jnp.bfloat16),
            grad_block,
            preferred_element_type=jnp.float32,
        )
    return (jnp.concatenate(grad_queries, axis=0), grad_keys, grad_values)


def matmul(left, right):
    return jnp.dot(left, right, preferred_element_type=jnp.float32)


def left_product(left, right):
    return jnp.einsum("ti,tj->ij", left, right, preferred_element_type=jnp.float32)


def right_product(grad, weight):
    return jnp.einsum("tj,ij->ti", grad, weight, preferred_element_type=jnp.float32)


def per_device(
    tokens,
    segment,
    w_query,
    w_key,
    w_value,
    w_output,
    gate_attn,
    gate_ffn,
    w_in,
    w_out,
    norm_attn,
    norm_ffn,
    bias_attn,
    bias_ffn,
    out_grad,
):
    full = fetch_forward(
        w_query,
        w_key,
        w_value,
        w_output,
        gate_attn,
        gate_ffn,
        w_in,
        w_out,
        norm_attn,
        norm_ffn,
        bias_attn,
        bias_ffn,
    )
    length = tokens.shape[0]
    shaped = (length, HEADS, HEAD_DIM)
    inputs = tokens.astype(jnp.float32)
    gain_first = full[8].astype(jnp.float32)
    gain_second = full[9].astype(jnp.float32)
    normed = norm_rows(inputs, gain_first).astype(jnp.bfloat16)
    queries = matmul(normed, full[0]).astype(jnp.bfloat16).reshape(shaped)
    keys = matmul(normed, full[1]).astype(jnp.bfloat16).reshape(shaped)
    values = matmul(normed, full[2]).astype(jnp.bfloat16).reshape(shaped)
    mixed_raw, row_peaks, row_totals = attention_forward(queries, keys, values, segment)
    mixed = mixed_raw.reshape(length, HEADS * HEAD_DIM).astype(jnp.bfloat16)
    branch = matmul(mixed, full[3])
    gate_one = jax.nn.sigmoid(matmul(normed, full[4]) + full[10].astype(jnp.float32))
    middle = inputs + gate_one * branch
    second = norm_rows(middle, gain_second).astype(jnp.bfloat16)
    gate_two = jax.nn.sigmoid(matmul(second, full[5]) + full[11].astype(jnp.float32))
    inner = matmul(second, full[6])
    gelu_tanh = partial(jax.nn.gelu, approximate=True)
    hidden = gelu_tanh(inner).astype(jnp.bfloat16)
    feed = matmul(hidden, full[7])
    result = (middle + gate_two * feed).astype(jnp.bfloat16)
    moments = jnp.stack(
        [
            jnp.sum(gate_one, axis=0),
            jnp.sum(gate_one * gate_one, axis=0),
            jnp.sum(gate_two, axis=0),
            jnp.sum(gate_two * gate_two, axis=0),
        ]
    )
    summed = lax.psum(moments, ("wide", "narrow"))
    counted = length * lax.axis_size("wide") * lax.axis_size("narrow")
    mean_one = summed[0] / counted
    mean_two = summed[2] / counted
    gate_stats = jnp.stack(
        [
            mean_one,
            summed[1] / counted - mean_one * mean_one,
            mean_two,
            summed[3] / counted - mean_two * mean_two,
        ]
    )
    weights = fetch_backward(
        w_query,
        w_key,
        w_value,
        w_output,
        gate_attn,
        gate_ffn,
        w_in,
        w_out,
        norm_attn,
        norm_ffn,
        bias_attn,
        bias_ffn,
    )
    grad_result = out_grad.astype(jnp.float32)
    grad_feed = (grad_result * gate_two).astype(jnp.bfloat16)
    grad_zeta_two = grad_result * feed * gate_two * (1.0 - gate_two)
    grad_bias_ffn = jnp.sum(grad_zeta_two, axis=0)
    zeta_two_low = grad_zeta_two.astype(jnp.bfloat16)
    grad_out = left_product(hidden, grad_feed)
    grad_hidden = right_product(grad_feed, weights[7])
    gelu_pull = jax.vjp(gelu_tanh, inner)[1]
    grad_inner = gelu_pull(grad_hidden)[0].astype(jnp.bfloat16)
    grad_in = left_product(second, grad_inner)
    grad_gate_ffn = left_product(second, zeta_two_low)
    grad_second = right_product(grad_inner, weights[6]) + right_product(zeta_two_low, weights[5])
    norm_pull_second = jax.vjp(norm_rows, middle, weights[9].astype(jnp.float32))[1]
    grad_mid_norm, grad_norm_ffn = norm_pull_second(grad_second)
    grad_middle = grad_result + grad_mid_norm
    grad_branch = (grad_middle * gate_one).astype(jnp.bfloat16)
    grad_zeta_one = grad_middle * branch * gate_one * (1.0 - gate_one)
    grad_bias_attn = jnp.sum(grad_zeta_one, axis=0)
    zeta_one_low = grad_zeta_one.astype(jnp.bfloat16)
    grad_output = left_product(mixed, grad_branch)
    grad_gate_attn = left_product(normed, zeta_one_low)
    grad_mixed = right_product(grad_branch, weights[3]).astype(jnp.bfloat16).reshape(shaped)
    grad_queries, grad_keys, grad_values = attention_backward(
        queries, keys, values, segment, grad_mixed, row_peaks, row_totals
    )
    queries_low = grad_queries.reshape(length, HEADS * HEAD_DIM).astype(jnp.bfloat16)
    keys_low = grad_keys.reshape(length, HEADS * HEAD_DIM).astype(jnp.bfloat16)
    values_low = grad_values.reshape(length, HEADS * HEAD_DIM).astype(jnp.bfloat16)
    grad_query = left_product(normed, queries_low)
    grad_key = left_product(normed, keys_low)
    grad_value = left_product(normed, values_low)
    grad_normed = (
        right_product(queries_low, weights[0])
        + right_product(keys_low, weights[1])
        + right_product(values_low, weights[2])
        + right_product(zeta_one_low, weights[4])
    )
    norm_pull_first = jax.vjp(norm_rows, inputs, weights[8].astype(jnp.float32))[1]
    grad_input_norm, grad_norm_attn = norm_pull_first(grad_normed)
    token_grad = grad_middle + grad_input_norm
    owned = reduce_grads(
        grad_query,
        grad_key,
        grad_value,
        grad_output,
        grad_gate_attn,
        grad_gate_ffn,
        grad_in,
        grad_out,
        grad_norm_attn,
        grad_norm_ffn,
        grad_bias_attn,
        grad_bias_ffn,
    )
    return (
        result,
        token_grad,
        owned[0],
        owned[1],
        owned[2],
        owned[3],
        owned[4],
        owned[5],
        owned[6],
        owned[7],
        owned[8],
        owned[9],
        owned[10],
        owned[11],
        gate_stats,
    )


def solution(mesh):
    in_specs = (
        P(("wide", "narrow"), None),
        P(("wide", "narrow")),
        P(("wide", "narrow"), None),
        P(("wide", "narrow"), None),
        P(("wide", "narrow"), None),
        P(("wide", "narrow"), None),
        P(("wide", "narrow"), None),
        P(("wide", "narrow"), None),
        P(("wide", "narrow"), None),
        P(("wide", "narrow"), None),
        P(("wide", "narrow")),
        P(("wide", "narrow")),
        P(("wide", "narrow")),
        P(("wide", "narrow")),
        P(("wide", "narrow"), None),
    )
    out_specs = (
        P(("wide", "narrow"), None),
        P(("wide", "narrow"), None),
        P(("wide", "narrow"), None),
        P(("wide", "narrow"), None),
        P(("wide", "narrow"), None),
        P(("wide", "narrow"), None),
        P(("wide", "narrow"), None),
        P(("wide", "narrow"), None),
        P(("wide", "narrow"), None),
        P(("wide", "narrow"), None),
        P(("wide", "narrow")),
        P(("wide", "narrow")),
        P(("wide", "narrow")),
        P(("wide", "narrow")),
        P(),
    )
    return jax.shard_map(
        per_device, mesh=mesh, in_specs=in_specs, out_specs=out_specs, check_vma=False
    )
```

profile of v0, /device:TPU:0, one launch (start us, length us, event | category | flops | bytes accessed | tf_op | source)
XLA Modules:
  0.0 1714.4 jit_solution(17220396869776782733)
XLA Ops:
  12.2 42.0 %all-reduce.9 = (bf16[512]{0:T(512)(128)(2,1)S(1)}, bf16[512]{0:T(512)(128)(2,1)S(1)}, bf16[512]{0:T(512)(128)(2,1)S(1)}, bf16[512]{0:T(512)(128)(2,1)S(1)}) all-reduce(bf16[512]{0:T(512)(128)(2,1)S(1)} %dynamic-update-slice, bf16[512]{0:T(512)(128)(2,1)S(1)} %dynamic-update-slice.1, ...), channel_id=1, replica_groups=mesh['wide'=8,'narrow'=4] {'wide','narrow'}, use_global_device_ids=true, to_apply=%add | all-reduce | flops 2048 | bytes 8192
  54.2 2.0 convert_reduce_fusion
  56.2 2.1 fusion.46
  58.3 70.8 %all_gather.50 = bf16[512,512]{1,0:T(8,128)(2,1)S(1)} all-gather(bf16[16,512]{1,0:T(8,128)(2,1)S(1)} %copy-done.68), channel_id=1, replica_groups=mesh['wide'=8,'narrow'=4] {'wide','narrow'}, dimensions={0}, use_global_device_ids=true | all-gather | bytes 540672 | tf_op jit(solution)/shard_map/all_gather | solution.py:38
  129.2 68.4 %all_gather.51 = bf16[512,512]{1,0:T(8,128)(2,1)S(1)} all-gather(bf16[16,512]{1,0:T(8,128)(2,1)S(1)} %copy-done.69), channel_id=1, replica_groups=mesh['wide'=8,'narrow'=4] {'wide','narrow'}, dimensions={0}, use_global_device_ids=true | all-gather | bytes 540672 | tf_op jit(solution)/shard_map/all_gather | solution.py:39
  197.6 69.2 %all_gather.49 = bf16[512,512]{1,0:T(8,128)(2,1)S(1)} all-gather(bf16[16,512]{1,0:T(8,128)(2,1)S(1)} %copy-done.70), channel_id=1, replica_groups=mesh['wide'=8,'narrow'=4] {'wide','narrow'}, dimensions={0}, use_global_device_ids=true | all-gather | bytes 540672 | tf_op jit(solution)/shard_map/all_gather | solution.py:40
  266.8 73.3 %all_gather.52 = bf16[512,512]{1,0:T(8,128)(2,1)} all-gather(bf16[16,512]{1,0:T(8,128)(2,1)S(1)} %copy-done.71), channel_id=1, replica_groups=mesh['wide'=8,'narrow'=4] {'wide','narrow'}, dimensions={0}, use_global_device_ids=true | all-gather | bytes 540672 | tf_op jit(solution)/shard_map/all_gather | solution.py:41
  342.9 2.2 convolution_convert_fusion.3
  345.1 3.8 fusion.29
  348.9 18.7 %fusion.115 = (f32[8,768]{1,0:T(8,128)S(1)}, f32[8,768,1536]{2,1,0:T(8,128)}) fusion(pred[768,1536]{1,0:T(8,128)(4,1)} %get-tuple-element.56, bf16[768,8,64]{0,2,1:T(8,128)(2,1)S(1)} %bitcast.122, bf16[1536,8,64]{0,2,1:T(8,128)(2,1)S(1)} %bitcast.108), kind=kOutput, calls=%fused_computation.148 | convolution fusion | flops 1245709824 | bytes 41312256 | tf_op jit(solution)/shard_map/sub | solution.py:138
  367.6 16.5 fusion.67
  384.1 19.1 %fusion.114 = (f32[8,768]{1,0:T(8,128)S(1)}, f32[8,768,1536]{2,1,0:T(8,128)}) fusion(pred[768,1536]{1,0:T(8,128)(4,1)} %get-tuple-element.57, bf16[768,8,64]{0,2,1:T(8,128)(2,1)S(1)} %bitcast.126, bf16[1536,8,64]{0,2,1:T(8,128)(2,1)S(1)} %bitcast.110), kind=kOutput, calls=%fused_computation.147 | convolution fusion | flops 1245709824 | bytes 41312256 | tf_op jit(solution)/shard_map/sub | solution.py:138
  403.2 74.2 %all_gather.47 = bf16[512,512]{1,0:T(8,128)(2,1)} all-gather(bf16[16,512]{1,0:T(8,128)(2,1)S(1)} %copy-done.72), channel_id=1, replica_groups=mesh['wide'=8,'narrow'=4] {'wide','narrow'}, dimensions={0}, use_global_device_ids=true | all-gather | bytes 540672 | tf_op jit(solution)/shard_map/all_gather | solution.py:42
  477.5 16.5 fusion.64
  494.0 1.3 pad_maximum_fusion
  495.4 1.2 copy-done.16
  498.5 3.3 fusion.110
  502.6 73.3 %all_gather.54 = bf16[512,512]{1,0:T(8,128)(2,1)} all-gather(bf16[16,512]{1,0:T(8,128)(2,1)S(1)} %copy-done.73), channel_id=1, replica_groups=mesh['wide'=8,'narrow'=4] {'wide','narrow'}, dimensions={0}, use_global_device_ids=true | all-gather | bytes 540672 | tf_op jit(solution)/shard_map/all_gather | solution.py:43
  575.8 11.7 multiply_convert_fusion.2
  587.5 6.3 fusion.118
  593.8 5.2 fusion.105
  599.0 1.2 copy-done.43
  600.1 2.6 fusion.73
  602.8 14.4 fusion.16
  617.2 3.5 fusion.119
  620.7 2.4 multiply_reduce_fusion.4
  623.2 1.6 fusion.109
  625.6 2.1 copy-done.29
  627.7 2.4 fusion.104
  632.8 2.0 fusion.125
  634.9 28.8 %multiply_reduce_fusion = (f32[8,768]{1,0:T(8,128)}, f32[8,768,1536]{2,1,0:T(8,128)}) fusion(f32[8,768,1536]{2,1,0:T(8,128)} %get-tuple-element.61, f32[8,768]{1,0:T(8,128)S(1)} %get-tuple-element.60, bf16[768,8,64]{0,2,1:T(8,128)(2,1)S(1)} %bitcast.134, bf16[1536,8,64]{0,2,1:T(8,128)(2,1)} %bitcast.142), kind=kOutput, calls=%fused_computation.3 | convolution fusion | flops 1236264960 | bytes 77905920 | tf_op jit(solution)/shard_map/qhd,khd->hqk/dot_general | solution.py:162
  663.7 3.5 fusion.70
  667.3 16.6 fusion.17
  684.0 28.4 %multiply_reduce_fusion.1 = (f32[8,768]{1,0:T(8,128)S(1)}, f32[8,768,1536]{2,1,0:T(8,128)}) fusion(f32[8,768,1536]{2,1,0:T(8,128)} %get-tuple-element.63, f32[8,768]{1,0:T(8,128)S(1)} %copy-done.66, bf16[768,8,64]{0,2,1:T(8,128)(2,1)S(1)} %bitcast.133, bf16[1536,8,64]{0,2,1:T(8,128)(2,1)} %bitcast.143), kind=kOutput, calls=%fused_computation.5 | convolution fusion | flops 1236264960 | bytes 77905920 | tf_op jit(solution)/shard_map/qhd,khd->hqk/dot_general | solution.py:162
  712.4 31.2 %multiply_convert_fusion.1 = bf16[8,768,1536]{2,1,0:T(8,128)(2,1)} fusion(f32[8,768,1536]{2,1,0:T(8,128)} %get-tuple-element.72, f32[8,768]{1,0:T(8,128)S(1)} %get-tuple-element.71, f32[8,768,1536]{2,1,0:T(8,128)} %get-tuple-element.63, f32[8,768]{1,0:T(8,128)S(1)} %copy-done.66), kind=kLoop, calls=%fused_computation.4 | loop fusion | flops 37748736 | bytes 94420992 | tf_op jit(solution)/shard_map/convert_element_type | solution.py:166
  743.5 17.5 %add_convert_fusion = bf16[8,64,1536]{2,1,0:T(8,128)(2,1)} fusion(f32[8,64,1536]{2,1,0:T(8,128)} %fusion.17, bf16[768,8,64]{0,2,1:T(8,128)(2,1)} %bitcast.132, f32[8,768]{1,0:T(8,128)S(1)} %copy-done.66, pred[768,1536]{1,0:T(8,128)(4,1)} %get-tuple-element.56, bf16[768,8,64]{0,2,1:T(8,128)(2,1)} %bitcast.124, bf16[1536,8,64]{0,2,1:T(8,128)(2,1)S(1)} %bitcast.113), kind=kOutput, calls=%fused_computation.84 | convolution fusion | flops 2464685568 | bytes 9068544 | tf_op jit(solution)/shard_map/hqk,qhd->khd/dot_general | solution.py:178
  761.1 3.4 fusion.124
  764.5 11.7 fusion.121
  776.3 31.3 %multiply_convert_fusion = bf16[8,768,1536]{2,1,0:T(8,128)(2,1)} fusion(f32[8,768,1536]{2,1,0:T(8,128)} %get-tuple-element.70, f32[8,768]{1,0:T(8,128)S(1)} %copy-done.67, f32[8,768,1536]{2,1,0:T(8,128)} %get-tuple-element.61, f32[8,768]{1,0:T(8,128)S(1)} %get-tuple-element.60), kind=kLoop, calls=%fused_computation.2 | loop fusion | flops 37748736 | bytes 94420992 | tf_op jit(solution)/shard_map/convert_element_type | solution.py:166
  807.5 10.9 fusion.51
  818.4 1.2 copy-done.18
  819.6 2.1 fusion.123
  821.7 13.0 fusion.62
  835.0 13.1 fusion.63
  848.1 1.5 pad_maximum_fusion.1
  849.6 1.1 copy-done.14
  850.7 2.0 fusion.122
  852.9 9.2 fusion.84
  862.3 1.6 copy-done.1
  863.9 8.4 fusion.116
  873.9 1.0 fusion.120
  875.4 1.0 convolution_add_fusion.2
  877.0 1.1 convolution_add_fusion.1
  879.0 1.5 fusion.47
  880.6 1.6 copy-done.5
  882.2 1.8 fusion.45
  884.0 39.6 %all-reduce.8 = (f32[512]{0:T(512)S(1)}, f32[512]{0:T(512)S(1)}, f32[512]{0:T(512)S(1)}, f32[512]{0:T(512)S(1)}, f32[4,512]{1,0:T(4,128)S(1)}) all-reduce(f32[512]{0:T(512)S(1)} %get-tuple-element.17, f32[512]{0:T(512)S(1)} %copy-done.74, f32[512]{0:T(512)S(1)} %copy-done.75, ...), channel_id=10, replica_groups=mesh['wide'=8,'narrow'=4] {'wide','narrow'}, use_global_device_ids=true, to_apply=%region_23.24.clone | all-reduce | flops 4096 | bytes 32768
  926.6 4.7 add_add_fusion.2
  931.3 74.9 %reduce-scatter.17.cloned.1.call-done = f32[16,512]{1,0:T(8,128)} async-done(((f32[512,512]{1,0:T(8,128)}), f32[16,512]{1,0:T(8,128)}) %reduce-scatter.17.cloned.1.call-update) | async-done | bytes 32784 | tf_op jit(solution)/shard_map/reduce_scatter | solution.py:102
  1006.2 135.0 %reduce-scatter.13.cloned.1.call-done = f32[16,512]{1,0:T(8,128)} async-done(((f32[512,512]{1,0:T(8,128)}), f32[16,512]{1,0:T(8,128)}) %reduce-scatter.13.cloned.1.call-update) | async-done | bytes 32784 | tf_op jit(solution)/shard_map/reduce_scatter | solution.py:100
  1141.2 134.9 %reduce-scatter.11.cloned.1.call-done = f32[16,512]{1,0:T(8,128)} async-done(((f32[512,512]{1,0:T(8,128)}), f32[16,512]{1,0:T(8,128)}) %reduce-scatter.11.cloned.1.call-update) | async-done | bytes 32784 | tf_op jit(solution)/shard_map/reduce_scatter | solution.py:99
  1276.1 134.4 %reduce-scatter.9.cloned.1.call-done = f32[16,512]{1,0:T(8,128)} async-done(((f32[512,512]{1,0:T(8,128)}), f32[16,512]{1,0:T(8,128)}) %reduce-scatter.9.cloned.1.call-update) | async-done | bytes 32784 | tf_op jit(solution)/shard_map/reduce_scatter | solution.py:98
  1410.6 147.1 %reduce-scatter.23.cloned.1.call-done = f32[64,512]{1,0:T(8,128)} async-done(((f32[2048,512]{1,0:T(8,128)}), f32[64,512]{1,0:T(8,128)}) %reduce-scatter.23.cloned.1.call-update) | async-done | bytes 131088 | tf_op jit(solution)/shard_map/reduce_scatter | solution.py:105
  1557.7 149.6 %reduce-scatter.21.cloned.1.call-done = f32[16,2048]{1,0:T(8,128)} async-done(((f32[512,2048]{1,0:T(8,128)}), f32[16,2048]{1,0:T(8,128)}) %reduce-scatter.21.cloned.1.call-update) | async-done | bytes 131088 | tf_op jit(solution)/shard_map/reduce_scatter | solution.py:104
  (217 shorter events, 21.2 us)
Async XLA Ops:
  7.2 332.9 %copy-start.2 = (bf16[1536,512]{1,0:T(8,128)(2,1)S(1)}, bf16[1536,512]{1,0:T(8,128)(2,1)}, u32[]{:S(2)}) copy-start(bf16[1536,512]{1,0:T(8,128)(2,1)} %param.15) | copy-start | bytes 4718596
  7.2 51.1 %copy-start.64 = (s32[1536]{0:T(1024)S(1)}, s32[1536]{0:T(1024)}, u32[]{:S(2)}) copy-start(s32[1536]{0:T(1024)} %param.16) | copy-start | bytes 18436
  7.2 51.1 %copy-start.68 = (bf16[16,512]{1,0:T(8,128)(2,1)S(1)}, bf16[16,512]{1,0:T(8,128)(2,1)}, u32[]{:S(2)}) copy-start(bf16[16,512]{1,0:T(8,128)(2,1)} %param.17) | copy-start | bytes 49156
  7.2 122.0 %copy-start.69 = (bf16[16,512]{1,0:T(8,128)(2,1)S(1)}, bf16[16,512]{1,0:T(8,128)(2,1)}, u32[]{:S(2)}) copy-start(bf16[16,512]{1,0:T(8,128)(2,1)} %param.18) | copy-start | bytes 49156
  7.2 190.4 %copy-start.70 = (bf16[16,512]{1,0:T(8,128)(2,1)S(1)}, bf16[16,512]{1,0:T(8,128)(2,1)}, u32[]{:S(2)}) copy-start(bf16[16,512]{1,0:T(8,128)(2,1)} %param.19) | copy-start | bytes 49156
  7.2 259.6 %copy-start.71 = (bf16[16,512]{1,0:T(8,128)(2,1)S(1)}, bf16[16,512]{1,0:T(8,128)(2,1)}, u32[]{:S(2)}) copy-start(bf16[16,512]{1,0:T(8,128)(2,1)} %param.20) | copy-start | bytes 49156
  7.2 568.6 %all-gather.3.cloned.1.call-start = ((), (), s32[]{:S(2)}) async-start(), calls=%async_computation.8 | async-start | bytes 2162688 | tf_op jit(solution)/shard_map/all_gather | solution.py:44
  8.0 579.5 %all-gather.5.cloned.1.call-start = ((), (), s32[]{:S(2)}) async-start(), calls=%async_computation.9 | async-start | bytes 2162688 | tf_op jit(solution)/shard_map/all_gather | solution.py:45
  8.7 922.6 %reduce-scatter.19.cloned.1.call-start = ((), (), s32[]{:S(2)}) async-start(), calls=%async_computation.15 | async-start | bytes 1081344 | tf_op jit(solution)/shard_map/reduce_scatter | solution.py:103
  54.2 286.5 %copy-start.62 = (f32[512]{0:T(512)}, f32[512]{0:T(512)S(1)}, u32[]{:S(2)}) copy-start(f32[512]{0:T(512)S(1)} %convert_element_type.100) | copy-start | bytes 6148
  56.2 284.5 %copy-start.50 = (f32[1536]{0:T(1024)}, f32[1536]{0:T(1024)S(1)}, u32[]{:S(2)}) copy-start(f32[1536]{0:T(1024)S(1)} %broadcast_multiply_fusion.1) | copy-start | bytes 18436
  58.3 208.5 %copy-start.58 = (f32[1536]{0:T(1024)}, f32[1536]{0:T(1024)S(1)}, u32[]{:S(2)}) copy-start(f32[1536]{0:T(1024)S(1)} %fusion.46) | copy-start | bytes 18436
  58.3 282.4 %copy-start.54 = (f32[1536]{0:T(1024)}, f32[1536]{0:T(1024)S(1)}, u32[]{:S(2)}) copy-start(f32[1536]{0:T(1024)S(1)} %fusion.76) | copy-start | bytes 18436
  129.2 212.5 %copy-start.34 = (bf16[512,512]{1,0:T(8,128)(2,1)}, bf16[512,512]{1,0:T(8,128)(2,1)S(1)}, u32[]{:S(2)}) copy-start(bf16[512,512]{1,0:T(8,128)(2,1)S(1)} %all_gather.50) | copy-start | bytes 1572868
  197.6 144.2 %copy-start.32 = (bf16[512,512]{1,0:T(8,128)(2,1)}, bf16[512,512]{1,0:T(8,128)(2,1)S(1)}, u32[]{:S(2)}) copy-start(bf16[512,512]{1,0:T(8,128)(2,1)S(1)} %all_gather.51) | copy-start | bytes 1572868
  266.8 76.1 %copy-start.30 = (bf16[512,512]{1,0:T(8,128)(2,1)}, bf16[512,512]{1,0:T(8,128)(2,1)S(1)}, u32[]{:S(2)}) copy-start(bf16[512,512]{1,0:T(8,128)(2,1)S(1)} %all_gather.49) | copy-start | bytes 1572868
  340.7 2.2 copy-start.24
  341.8 135.7 %copy-start.9 = (bf16[1536,512]{0,1:T(8,128)(2,1)}, bf16[1536,512]{0,1:T(8,128)(2,1)S(1)}, u32[]{:S(2)}) copy-start(bf16[1536,512]{0,1:T(8,128)(2,1)S(1)} %convolution_convert_fusion.1) | copy-start | bytes 4718596
  342.9 24.7 %copy-start.27 = (bf16[768,512]{0,1:T(8,128)(2,1)}, bf16[768,512]{0,1:T(8,128)(2,1)S(1)}, u32[]{:S(2)}) copy-start(bf16[768,512]{0,1:T(8,128)(2,1)S(1)} %get-tuple-element.50) | copy-start | bytes 2359300
  342.9 134.5 %copy-start.28 = (bf16[768,512]{0,1:T(8,128)(2,1)}, bf16[768,512]{0,1:T(8,128)(2,1)S(1)}, u32[]{:S(2)}) copy-start(bf16[768,512]{0,1:T(8,128)(2,1)S(1)} %get-tuple-element.51) | copy-start | bytes 2359300
  367.6 16.5 copy-start.65
  384.1 19.1 %copy-start.72 = (bf16[16,512]{1,0:T(8,128)(2,1)S(1)}, bf16[16,512]{1,0:T(8,128)(2,1)}, u32[]{:S(2)}) copy-start(bf16[16,512]{1,0:T(8,128)(2,1)} %param.21) | copy-start | bytes 49156
  477.4 145.7 %copy-start.60 = (f32[512]{0:T(512)}, f32[512]{0:T(512)S(1)}, u32[]{:S(2)}) copy-start(f32[512]{0:T(512)S(1)} %convert_element_type.109) | copy-start | bytes 6148
  477.5 16.6 copy-start.47
  494.0 2.5 copy-start.40
  496.5 2.0 copy-start.36
  498.5 3.3 copy-start.7
  501.8 121.3 %copy-start = (f32[1536,512]{1,0:T(8,128)}, f32[1536,512]{1,0:T(8,128)S(1)}, u32[]{:S(2)}) copy-start(f32[1536,512]{1,0:T(8,128)S(1)} %get-tuple-element.39) | copy-start | bytes 9437188
  501.8 121.3 %copy-start.48 = (f32[1536]{0:T(1024)}, f32[1536]{0:T(1024)S(1)}, u32[]{:S(2)}) copy-start(f32[1536]{0:T(1024)S(1)} %broadcast_multiply_fusion) | copy-start | bytes 18436
  502.6 120.6 %copy-start.52 = (f32[1536]{0:T(1024)}, f32[1536]{0:T(1024)S(1)}, u32[]{:S(2)}) copy-start(f32[1536]{0:T(1024)S(1)} %fusion.77) | copy-start | bytes 18436
  587.5 6.3 copy-start.20
  587.5 6.3 copy-start.38
  602.7 328.6 %reduce-scatter.15.cloned.1.call-start = ((), (), s32[]{:S(2)}) async-start(), calls=%async_computation.13 | async-start | bytes 1081344 | tf_op jit(solution)/shard_map/reduce_scatter | solution.py:101
  602.8 14.4 copy-start.81
  617.2 3.5 copy-start.11
  617.2 3.5 copy-start.39
  617.2 3.5 copy-start.44
  623.2 2.4 copy-start.21
  623.2 4.5 copy-start.29
  624.8 5.3 copy-start.6
  624.9 5.2 copy-start.56
  627.7 2.4 copy-start.41
  630.1 33.6 %copy-start.12 = (bf16[1536,512]{1,0:T(8,128)(2,1)}, bf16[1536,512]{1,0:T(8,128)(2,1)S(1)}, u32[]{:S(2)}) copy-start(bf16[1536,512]{1,0:T(8,128)(2,1)S(1)} %get-tuple-element.44) | copy-start | bytes 4718596
  632.8 2.1 copy-start.46
  634.8 371.4 %reduce-scatter.17.cloned.1.call-start = ((), (), s32[]{:S(2)}) async-start(), calls=%async_computation.14 | async-start | bytes 1081344 | tf_op jit(solution)/shard_map/reduce_scatter | solution.py:102
  663.7 3.5 copy-start.10
  667.2 16.7 copy-start.45
  667.2 16.7 copy-start.66
  683.9 457.3 %reduce-scatter.13.cloned.1.call-start = ((), (), s32[]{:S(2)}) async-start(), calls=%async_computation.12 | async-start | bytes 1081344 | tf_op jit(solution)/shard_map/reduce_scatter | solution.py:100
  743.5 17.5 %copy-start.26 = (bf16[1536,512]{1,0:T(8,128)(2,1)S(1)}, bf16[1536,512]{1,0:T(8,128)(2,1)}, u32[]{:S(2)}) copy-start(bf16[1536,512]{1,0:T(8,128)(2,1)} %copy-done.24) | copy-start | bytes 4718596
  764.5 11.8 copy-start.67
  776.2 499.9 %reduce-scatter.11.cloned.1.call-start = ((), (), s32[]{:S(2)}) async-start(), calls=%async_computation.11 | async-start | bytes 1081344 | tf_op jit(solution)/shard_map/reduce_scatter | solution.py:99
  834.8 575.8 %reduce-scatter.9.cloned.1.call-start = ((), (), s32[]{:S(2)}) async-start(), calls=%async_computation.10 | async-start | bytes 1081344 | tf_op jit(solution)/shard_map/reduce_scatter | solution.py:98
  850.7 2.1 copy-start.22
  852.8 704.9 %reduce-scatter.23.cloned.1.call-start = ((), (), s32[]{:S(2)}) async-start(), calls=%async_computation.17 | async-start | bytes 4325376 | tf_op jit(solution)/shard_map/reduce_scatter | solution.py:105
  862.1 845.3 %reduce-scatter.21.cloned.1.call-start = ((), (), s32[]{:S(2)}) async-start(), calls=%async_computation.16 | async-start | bytes 4325376 | tf_op jit(solution)/shard_map/reduce_scatter | solution.py:104
  877.0 2.0 copy-start.37
  877.0 2.0 copy-start.51
  879.0 3.2 copy-start.55
  880.5 3.4 copy-start.74
  880.5 3.4 copy-start.75
  880.6 3.4 copy-start.78
  880.6 46.0 %copy-start.23 = (bf16[1536,512]{1,0:T(8,128)(2,1)S(1)}, bf16[1536,512]{1,0:T(8,128)(2,1)}, u32[]{:S(2)}) copy-start(bf16[1536,512]{1,0:T(8,128)(2,1)} %param.29) | copy-start | bytes 4718596
  880.6 46.0 %copy-start.57 = (f32[1536]{0:T(1024)S(1)}, f32[1536]{0:T(1024)}, u32[]{:S(2)}) copy-start(f32[1536]{0:T(1024)} %copy-done.56) | copy-start | bytes 18436
  (28 other events, 39.6 us)
Sparse Core Ops, SparseCore 0:
  11.0 59.3 all-gather.2
  73.4 55.9 all-gather.4
  602.8 133.8 reduce-scatter.18
  739.5 131.9 reduce-scatter.14
  874.2 131.9 reduce-scatter.16
  1009.0 132.1 reduce-scatter.12
  1144.0 132.0 reduce-scatter.10
  1279.0 131.4 reduce-scatter.8
  1413.4 144.2 reduce-scatter.22
  1560.4 146.8 reduce-scatter.20
where the time goes:
time: 1720 us; the launch traced here: 1710 us
  waiting for transfers between devices  778 us (45%)
  blocking collectives  511 us (30%)
  matrix products  302 us (18%)
  other arithmetic  85.4 us (5%)
  local copies, waits for them, and re-layouts  22.9 us (1%)
    reduce_scatter x1, waiting for transfers between devices, reduce_grads(): lax.psum_scatter(grad_in, ('wide', 'narrow'), scatter_dimension=0, tiled=...  150 us
    reduce_scatter x1, waiting for transfers between devices, reduce_grads(): lax.psum_scatter(grad_out, ('wide', 'narrow'), scatter_dimension=0, tiled...  147 us
    reduce_scatter x1, waiting for transfers between devices, reduce_grads(): lax.psum_scatter(grad_value, ('wide', 'narrow'), scatter_dimension=0, til...  135 us
    reduce_scatter x1, waiting for transfers between devices, reduce_grads(): lax.psum_scatter(grad_key, ('wide', 'narrow'), scatter_dimension=0, tiled...  135 us
    reduce_scatter x1, waiting for transfers between devices, reduce_grads(): lax.psum_scatter(grad_query, ('wide', 'narrow'), scatter_dimension=0, til...  134 us
    unnamed x2, blocking collectives  81.6 us
    reduce_scatter x1, waiting for transfers between devices, reduce_grads(): lax.psum_scatter(grad_gate_attn, ('wide', 'narrow'), scatter_dimension=0,...  74.9 us
    all_gather x1, blocking collectives, fetch_forward(): lax.all_gather(gate_attn, ('wide', 'narrow'), axis=0, tiled=True)  74.2 us
  transfers between devices with their start and end apart: 10, of which 6 were waited for; matrix products, arithmetic and copies ran while one was open for 22% of the time, Pallas kernels for 0%

commit v1 on v0

v1 whole, which is shorter than its diff:
```python
from functools import partial

import jax
import jax.numpy as jnp
from jax import lax
from jax.experimental import pallas as pl
from jax.experimental.pallas import tpu as pltpu
from jax.sharding import PartitionSpec as P

HEADS = 8
HEAD_DIM = 64
EPSILON = 1e-05
MASKED = -1000000000.0
AXES = ("wide", "narrow")
BF = jnp.bfloat16
F32 = jnp.float32
MIB = 1 << 20
VMEM = 60 * MIB
BLOCK = 256
ROWS = 16
BLOCKS = 32
FIRST = 1536 + 128
REST = 5632
SUMS = 384


def dot(left, right):
    return jnp.dot(left, right, preferred_element_type=F32)


def dot_t(left, right):
    return lax.dot_general(left, right, (((1,), (1,)), ((), ())), preferred_element_type=F32)


def t_dot(left, right):
    return lax.dot_general(left, right, (((0,), (0,)), ((), ())), preferred_element_type=F32)


def row_mean(values):
    return jnp.mean(values, axis=-1, keepdims=True)


def normalise(values):
    offset = values - row_mean(values)
    scale = lax.rsqrt(row_mean(offset * offset) + EPSILON)
    return offset * scale, scale


def sigmoid(values):
    return 1.0 / (1.0 + jnp.exp(-values))


def project_kernel(
    order, tokens, *refs
):
    pieces, refs = refs[:8], refs[8:]
    normed, normed_t, query, key, value, key_t, value_t, weights, small, held, sem = refs
    step = pl.program_id(0)

    @pl.when(step == 0)
    def _():
        for at in range(BLOCKS):
            place = pl.multiple_of(order[at] * ROWS, ROWS)
            pltpu.make_async_copy(
                pieces[at // 4].at[pl.ds(at % 4 * ROWS, ROWS)], held.at[pl.ds(place, ROWS)], sem
            ).start()

    unit, _ = normalise(tokens[...].astype(F32))

    @pl.when(step == 0)
    def _():
        pltpu.make_async_copy(held, held, sem).wait()
        total = jnp.zeros((ROWS, 128), F32)
        for at in range(BLOCKS):
            total = total + held[pl.ds(at * ROWS, ROWS), 1536:FIRST].astype(F32)
        for vector in range(4):
            for part in range(4):
                small[vector : vector + 1, part * 128 : (part + 1) * 128] = total[
                    vector * 4 + part : vector * 4 + part + 1
                ]
        weights[...] = held[:, :1536]

    low = (unit * small[0:1, :]).astype(BF)
    normed[...] = low
    normed_t[...] = low.T
    query[...] = (dot(low, held[:, :512]).astype(BF).astype(F32) * HEAD_DIM**-0.5).astype(BF)
    keys = dot(low, held[:, 512:1024]).astype(BF)
    key[...] = keys
    key_t[...] = keys.T
    values = dot(low, held[:, 1024:1536]).astype(BF)
    value[...] = values
    value_t[...] = values.T


def project(order, tokens, pieces):
    length, width = tokens.shape
    tile = 512
    by_rows = pl.BlockSpec((tile, width), lambda i: (i, 0))
    by_columns = pl.BlockSpec((width, tile), lambda i: (0, i))
    whole = lambda *shape: pl.BlockSpec(shape, lambda i: (0,) * len(shape))
    rows = jax.ShapeDtypeStruct((length, width), BF)
    columns = jax.ShapeDtypeStruct((width, length), BF)
    return pl.pallas_call(
        project_kernel,
        grid=(length // tile,),
        in_specs=[
            pl.BlockSpec(memory_space=pltpu.SMEM),
            by_rows,
        ] + [pl.BlockSpec(memory_space=pl.ANY)] * 8,
        out_specs=[
            by_rows, by_columns, by_rows, by_rows, by_rows, by_columns, by_columns,
            whole(width, 1536), whole(4, width),
        ],
        out_shape=[
            rows, columns, rows, rows, rows, columns, columns,
            jax.ShapeDtypeStruct((width, 1536), BF),
            jax.ShapeDtypeStruct((4, width), F32),
        ],
        scratch_shapes=[pltpu.VMEM((width, FIRST), BF), pltpu.SemaphoreType.DMA],
        compiler_params=pltpu.CompilerParams(vmem_limit_bytes=VMEM),
        cost_estimate=pl.CostEstimate(
            flops=6 * length * width * width, bytes_accessed=12 * MIB, transcendentals=length
        ),
        name="project",
    )(order, tokens, *pieces)


def bias_of(segment_row, key_block, query_block):
    key_at = key_block * BLOCK + lax.broadcasted_iota(jnp.int32, (BLOCK, BLOCK), 0)
    query_at = query_block * BLOCK + lax.broadcasted_iota(jnp.int32, (BLOCK, BLOCK), 1)
    return jnp.where((key_at >= segment_row) & (key_at <= query_at), 0.0, MASKED)


def keep_head(pair, head):
    lane = lax.broadcasted_iota(jnp.int32, pair.shape, 1)
    own = (lane >= HEAD_DIM) if head % 2 else (lane < HEAD_DIM)
    return jnp.where(own, pair, jnp.zeros_like(pair))


def attend_kernel(
    segment, segment_row, query, key, value_t, mixed, log_total, masked_query, peak, total, mix
):
    step = pl.program_id(0)
    for head in range(HEADS):
        pair = pl.ds(head // 2 * 128, 128)
        masked_query[head] = keep_head(query[:, pair], head)
    peak[...] = jnp.full(peak.shape, -1e30, F32)
    total[...] = jnp.zeros(total.shape, F32)
    mix[...] = jnp.zeros(mix.shape, F32)
    seen = segment_row[...]

    def visit(block, _):
        bias = bias_of(seen, block, step)
        rows = pl.ds(pl.multiple_of(block * BLOCK, BLOCK), BLOCK)
        heads = range(HEADS)
        pair = lambda head: pl.ds(head // 2 * 128, 128)
        own = lambda head: pl.ds(head * HEAD_DIM, HEAD_DIM)
        scores = [dot_t(key[rows, pair(h)], masked_query[h]) + bias for h in heads]
        old = [peak[h : h + 1, :] for h in heads]
        new = [jnp.maximum(o, jnp.max(s, axis=0, keepdims=True)) for o, s in zip(old, scores)]
        power = [jnp.exp(s - n) for s, n in zip(scores, new)]
        fade = [jnp.exp(o - n) for o, n in zip(old, new)]
        added = [jnp.sum(p, axis=0, keepdims=True) for p in power]
        high = [p.astype(BF) for p in power]
        rest = [(p - x.astype(F32)).astype(BF) for p, x in zip(power, high)]
        mixes = [
            mix[own(h), :] * fade[h] + dot(value_t[own(h), rows], high[h]) + dot(value_t[own(h), rows], rest[h])
            for h in heads
        ]
        for h in heads:
            peak[h : h + 1, :] = new[h]
            total[h : h + 1, :] = total[h : h + 1, :] * fade[h] + added[h]
            mix[own(h), :] = mixes[h]
        return 0

    first = lax.div(segment[step * BLOCK], BLOCK)
    lax.fori_loop(first, step + 1, visit, 0)
    log_total[...] = peak[...] + jnp.log(total[...])
    for head in range(HEADS):
        own = pl.ds(head * HEAD_DIM, HEAD_DIM)
        mix[own, :] = mix[own, :] / total[head : head + 1, :]
    mixed[...] = mix[...].T


def attend(segment, segment_row, query, key, value_t):
    length, width = query.shape
    whole = lambda *shape: pl.BlockSpec(shape, lambda i, s: (0,) * len(shape))
    return pl.pallas_call(
        attend_kernel,
        grid_spec=pltpu.PrefetchScalarGridSpec(
            num_scalar_prefetch=1,
            grid=(length // BLOCK,),
            in_specs=[
                pl.BlockSpec((1, BLOCK), lambda i, s: (0, i)),
                pl.BlockSpec((BLOCK, width), lambda i, s: (i, 0)),
                whole(length, width),
                whole(width, length),
            ],
            out_specs=[
                pl.BlockSpec((BLOCK, width), lambda i, s: (i, 0)),
                pl.BlockSpec((HEADS, BLOCK), lambda i, s: (0, i)),
            ],
            scratch_shapes=[
                pltpu.VMEM((HEADS, BLOCK, 128), BF),
                pltpu.VMEM((HEADS, BLOCK), F32),
                pltpu.VMEM((HEADS, BLOCK), F32),
                pltpu.VMEM((width, BLOCK), F32),
            ],
        ),
        out_shape=[
            jax.ShapeDtypeStruct((length, width), F32),
            jax.ShapeDtypeStruct((HEADS, length), F32),
        ],
        compiler_params=pltpu.CompilerParams(vmem_limit_bytes=VMEM),
        cost_estimate=pl.CostEstimate(
            flops=16 * length * length * width // 2, bytes_accessed=6 * MIB, transcendentals=8 * length * length // 2
        ),
        name="attend",
    )(segment, segment_row, query, key, value_t)


def attend_back_kernel(
    me, segment, segment_row, query, key, value, key_t, grad_mixed, log_total, inner_sum, normed_t, _after,
    grad_query, grad_key, grad_value, send, keep,
    masked_query, masked_grad, query_sum, key_sum, value_sum, whole_query, staged, sems,
    *, heads,
):
    step = pl.program_id(0)
    last = pl.num_programs(0) - 1
    width = heads * HEAD_DIM

    @pl.when(step == 0)
    def _():
        key_sum[...] = jnp.zeros(key_sum.shape, F32)
        value_sum[...] = jnp.zeros(value_sum.shape, F32)

    for head in range(heads):
        pair = pl.ds(head // 2 * 128, 128)
        masked_query[head] = keep_head(query[:, pair], head)
        masked_grad[head] = keep_head(grad_mixed[:, pair], head)
    query_sum[...] = jnp.zeros(query_sum.shape, F32)
    seen = segment_row[...]

    def visit(block, _):
        bias = bias_of(seen, block, step)
        rows = pl.ds(pl.multiple_of(block * BLOCK, BLOCK), BLOCK)
        every = range(heads)
        pair = lambda head: pl.ds(head // 2 * 128, 128)
        own = lambda head: pl.ds(head * HEAD_DIM, HEAD_DIM)
        scores = [dot_t(key[rows, pair(h)], masked_query[h]) for h in every]
        grad_probs = [dot_t(value[rows, pair(h)], masked_grad[h]) for h in every]
        probs = [jnp.exp((s + bias) - log_total[0, h : h + 1, :]) for h, s in enumerate(scores)]
        grad_scores = [
            (p * (g - inner_sum[0, h : h + 1, :])).astype(BF)
            for h, (p, g) in enumerate(zip(probs, grad_probs))
        ]
        to_value = [dot(p.astype(BF), masked_grad[h]) for h, p in enumerate(probs)]
        to_key = [dot(g, masked_query[h]) for h, g in enumerate(grad_scores)]
        to_query = [dot(key_t[own(h), rows], g) for h, g in enumerate(grad_scores)]
        for h in range(0, heads, 2):
            value_sum[rows, pair(h)] += to_value[h] + to_value[h + 1]
            key_sum[rows, pair(h)] += to_key[h] + to_key[h + 1]
        for h in every:
            query_sum[own(h), :] += to_query[h]
        return 0

    first = lax.div(segment[step * BLOCK], BLOCK)
    lax.fori_loop(first, step + 1, visit, 0)
    finished = (query_sum[...].T * HEAD_DIM**-0.5).astype(BF)
    grad_query[...] = finished
    whole_query[pl.ds(pl.multiple_of(step * BLOCK, BLOCK), BLOCK), :] = finished

    @pl.when(step == last)
    def _():
        low_key = key_sum[...].astype(BF)
        low_value = value_sum[...].astype(BF)
        grad_key[...] = low_key
        grad_value[...] = low_value
        staged[:, :width] = dot(normed_t[...], whole_query[...]).astype(BF)
        staged[:, width : 2 * width] = dot(normed_t[...], low_key).astype(BF)
        staged[:, 2 * width :] = dot(normed_t[...], low_value).astype(BF)
        hand_out(me[0], [(staged, 1, 0)], send, keep, sems)


def device_at(me, half, at):
    plane, line = at // 4, at % 4
    return jnp.bitwise_xor(me, (plane * 2 + half) * 4 + line)


def hand_out(me, parts, send, keep, sems):
    for half, target in enumerate((keep, send)):
        for at in range(BLOCKS // 2):
            owner = device_at(me, half, at)
            for source, groups, column in parts:
                wide = source.shape[1]
                if groups == 0:
                    pltpu.make_async_copy(
                        source, target.at[at, :, pl.ds(column, wide)], sems.at[half]
                    ).start()
                for group in range(groups):
                    place = pl.multiple_of(owner * (ROWS * groups) + group * ROWS, ROWS)
                    pltpu.make_async_copy(
                        source.at[pl.ds(place, ROWS)],
                        target.at[at, :, pl.ds(column + group * wide, wide)],
                        sems.at[half],
                    ).start()
    for half, target in enumerate((keep, send)):
        pltpu.make_async_copy(target, target, sems.at[half]).wait()


def attend_back(
    me, segment, segment_row, query, key, value, key_t, grad_mixed, log_total, inner_sum, normed_t,
    after, group, heads,
):
    length, full = query.shape
    width = heads * HEAD_DIM
    groups = HEADS // heads
    by_rows = pl.BlockSpec((BLOCK, width), lambda i, m, s: (i, group))
    columns = pl.BlockSpec((length, width), lambda i, m, s: (0, group))
    per_head = pl.BlockSpec((1, heads, BLOCK), lambda i, m, s: (group, 0, i))
    flat = jax.ShapeDtypeStruct((length, width), BF)
    packet = jax.ShapeDtypeStruct((BLOCKS // 2, ROWS, 3 * width), BF)
    return pl.pallas_call(
        partial(attend_back_kernel, heads=heads),
        grid_spec=pltpu.PrefetchScalarGridSpec(
            num_scalar_prefetch=2,
            grid=(length // BLOCK,),
            in_specs=[
                pl.BlockSpec((1, BLOCK), lambda i, m, s: (0, i)),
                by_rows,
                columns,
                columns,
                pl.BlockSpec((width, length), lambda i, m, s: (group, 0)),
                by_rows,
                per_head,
                per_head,
                pl.BlockSpec((full, length), lambda i, m, s: (0, 0)),
                pl.BlockSpec(memory_space=pl.ANY),
            ],
            out_specs=[
                pl.BlockSpec((BLOCK, width), lambda i, m, s: (i, 0)),
                pl.BlockSpec((length, width), lambda i, m, s: (0, 0)),
                pl.BlockSpec((length, width), lambda i, m, s: (0, 0)),
                pl.BlockSpec(memory_space=pl.ANY),
                pl.BlockSpec(memory_space=pl.ANY),
            ],
            scratch_shapes=[
                pltpu.VMEM((heads, BLOCK, 128), BF),
                pltpu.VMEM((heads, BLOCK, 128), BF),
                pltpu.VMEM((width, BLOCK), F32),
                pltpu.VMEM((length, width), F32),
                pltpu.VMEM((length, width), F32),
                pltpu.VMEM((length, width), BF),
                pltpu.VMEM((full, 3 * width), BF),
                pltpu.SemaphoreType.DMA((2,)),
            ],
        ),
        out_shape=[flat, flat, flat, packet, packet],
        compiler_params=pltpu.CompilerParams(vmem_limit_bytes=VMEM),
        cost_estimate=pl.CostEstimate(
            flops=40 * length * length * width // 2, bytes_accessed=8 * MIB, transcendentals=heads * length * length // 2
        ),
        name=f"attend_back_{group}",
    )(
        me, segment, segment_row, query, key, value, key_t, grad_mixed,
        log_total.reshape(groups, heads, length), inner_sum.reshape(groups, heads, length), normed_t, after,
    )


def feed_kernel(
    me, order, tokens, normed, mixed, out_grad, small, *refs
):
    pieces, refs = refs[:8], refs[8:]
    result, grad_middle, zeta_one_low, grad_mixed, inner_sum, gate_attn_out, send, keep, *refs = refs
    held, held_out, sum_held, sum_out, staged, staged_out, hidden, slope, sums, sums_tile, sems = refs
    step = pl.program_id(0)
    last = pl.num_programs(0) - 1
    features = tokens.shape[1]
    chunks = held_out.shape[0] // features
    straight = 3 * features + chunks * features

    @pl.when(step == 0)
    def _():
        for at in range(BLOCKS):
            source = pieces[at // 4].at[pl.ds(at % 4 * ROWS, ROWS)]
            place = pl.multiple_of(order[at] * ROWS, ROWS)
            pltpu.make_async_copy(
                source.at[:, pl.ds(0, straight)], held.at[pl.ds(place, ROWS)], sems.at[0]
            ).start()
            for group in range(4):
                pltpu.make_async_copy(
                    source.at[:, pl.ds(straight + group * features, features)],
                    held_out.at[pl.ds(place * 4 + group * ROWS, ROWS)],
                    sems.at[1],
                ).start()
        sums[...] = jnp.zeros(sums.shape, F32)
        sum_held[...] = jnp.zeros(sum_held.shape, F32)
        sum_out[...] = jnp.zeros(sum_out.shape, F32)
        pltpu.make_async_copy(held, held, sems.at[0]).wait()
        pltpu.make_async_copy(held_out, held_out, sems.at[1]).wait()
        gate_attn_out[...] = held[:, features : 2 * features]

    w_output = held.at[:, pl.ds(0, features)]
    gate_attn = held.at[:, pl.ds(features, features)]
    gate_ffn = held.at[:, pl.ds(2 * features, features)]
    gain, bias_one, bias_two = small[1:2, :], small[2:3, :], small[3:4, :]

    exact = mixed[...]
    mix = exact.astype(BF)
    branch = dot(mix, w_output[...])
    gate_one = sigmoid(dot(normed[...], gate_attn[...]) + bias_one)
    middle = tokens[...].astype(F32) + gate_one * branch
    unit, scale = normalise(middle)
    second = (unit * gain).astype(BF)
    gate_two = sigmoid(dot(second, gate_ffn[...]) + bias_two)

    feed = jnp.zeros(middle.shape, F32)
    for chunk in range(chunks):
        at = pl.ds(chunk * features, features)
        inner = dot(second, held[:, pl.ds((3 + chunk) * features, features)])
        root = (2.0 / jnp.pi) ** 0.5
        square = inner * inner
        turn = jnp.tanh(inner * (root + (root * 0.044715) * square))
        rise = 0.5 + 0.5 * turn
        value = inner * rise
        slope[:, at] = rise + value * (1.0 - turn) * (root + (3.0 * root * 0.044715) * square)
        low = value.astype(BF)
        hidden[:, at] = low
        feed = feed + dot(low, held_out[at, :])
    result[...] = (middle + gate_two * feed).astype(BF)

    grad = out_grad[...].astype(F32)
    grad_feed = (grad * gate_two).astype(BF)
    zeta_two = grad * feed * gate_two * (1.0 - gate_two)
    zeta_two_low = zeta_two.astype(BF)
    grad_second = dot_t(zeta_two_low, gate_ffn[...])
    sum_held[:, pl.ds(2 * features, features)] += t_dot(second, zeta_two_low)
    for chunk in range(chunks):
        at = pl.ds(chunk * features, features)
        columns = pl.ds((3 + chunk) * features, features)
        grad_hidden = dot_t(grad_feed, held_out[at, :])
        grad_inner = (slope[:, at] * grad_hidden).astype(BF)
        sum_out[at, :] += t_dot(hidden[:, at], grad_feed)
        sum_held[:, columns] += t_dot(second, grad_inner)
        grad_second = grad_second + dot_t(grad_inner, held[:, columns])

    grad_unit = grad_second * gain
    grad_mid = grad + scale * (
        grad_unit - row_mean(grad_unit) - unit * row_mean(grad_unit * unit)
    )
    grad_middle[...] = grad_mid
    grad_branch = (grad_mid * gate_one).astype(BF)
    zeta_one = grad_mid * branch * gate_one * (1.0 - gate_one)
    low_one = zeta_one.astype(BF)
    zeta_one_low[...] = low_one
    sum_held[:, pl.ds(0, features)] += t_dot(mix, grad_branch)
    sum_held[:, pl.ds(features, features)] += t_dot(normed[...], low_one)
    back = dot_t(grad_branch, w_output[...]).astype(BF)
    grad_mixed[...] = back
    product = back.astype(F32) * exact
    high = product.astype(BF)
    rest = (product - high.astype(F32)).astype(BF)
    head_of = lax.broadcasted_iota(jnp.int32, (HEADS, features), 1) // HEAD_DIM
    own = (head_of == lax.broadcasted_iota(jnp.int32, (HEADS, features), 0)).astype(BF)
    inner_sum[...] = dot_t(own, high) + dot_t(own, rest)

    total = lambda v: jnp.sum(v, axis=0, keepdims=True)
    sums[0:1, :] += total(gate_one)
    sums[1:2, :] += total(gate_one * gate_one)
    sums[2:3, :] += total(gate_two)
    sums[3:4, :] += total(gate_two * gate_two)
    sums[4:5, :] += total(zeta_one)
    sums[5:6, :] += total(zeta_two)

    @pl.when(step == last)
    def _():
        staged[...] = sum_held[...].astype(BF)
        staged_out[...] = sum_out[...].astype(BF)
        write_sums(sums[...], sums_tile)
        hand_out(me[0], [(staged, 1, 0), (staged_out, 4, straight), (sums_tile, 0, REST)], send, keep, sems)


def write_sums(sums, tile):
    high = sums[0:6].astype(BF)
    low = (sums[0:6] - high.astype(F32)).astype(BF)
    rows = jnp.concatenate([high.astype(F32), low.astype(F32)], axis=0)
    spill = [
        jnp.concatenate([rows[3 * r + k : 3 * r + k + 1, SUMS:] for k in range(3)], axis=1)
        for r in range(4)
    ]
    tile[...] = jnp.concatenate([rows[:, :SUMS]] + spill, axis=0).astype(BF)


def read_sums(tile):
    tile = tile.astype(F32)
    spill = jnp.concatenate(
        [tile[12 + r : 13 + r, k * 128 : (k + 1) * 128] for r in range(4) for k in range(3)], axis=0
    )
    rows = jnp.concatenate([tile[:12], spill], axis=1)
    return rows[0:6] + rows[6:12]


def feed_forward(me, order, tokens, normed, mixed, out_grad, small, pieces):
    length, width = tokens.shape
    hidden = REST - 3 * width
    hidden = hidden // 2
    tile = 512
    by_rows = pl.BlockSpec((tile, width), lambda i: (i, 0))
    anywhere = pl.BlockSpec(memory_space=pl.ANY)
    rows = jax.ShapeDtypeStruct((length, width), BF)
    half = jax.ShapeDtypeStruct((BLOCKS // 2, ROWS, REST + SUMS), BF)
    straight = 3 * width + hidden
    return pl.pallas_call(
        feed_kernel,
        grid=(length // tile,),
        in_specs=[
            pl.BlockSpec(memory_space=pltpu.SMEM),
            pl.BlockSpec(memory_space=pltpu.SMEM),
            by_rows, by_rows, by_rows, by_rows,
            pl.BlockSpec((4, width), lambda i: (0, 0)),
        ] + [anywhere] * 8,
        out_specs=[
            by_rows, by_rows, by_rows, by_rows,
            pl.BlockSpec((HEADS, tile), lambda i: (0, i)),
            pl.BlockSpec((width, width), lambda i: (0, 0)),
            anywhere, anywhere,
        ],
        out_shape=[
            rows,
            jax.ShapeDtypeStruct((length, width), F32),
            rows,
            rows,
            jax.ShapeDtypeStruct((HEADS, length), F32),
            jax.ShapeDtypeStruct((width, width), BF),
            half,
            half,
        ],
        scratch_shapes=[
            pltpu.VMEM((width, straight), BF),
            pltpu.VMEM((hidden, width), BF),
            pltpu.VMEM((width, straight), F32),
            pltpu.VMEM((hidden, width), F32),
            pltpu.VMEM((width, straight), BF),
            pltpu.VMEM((hidden, width), BF),
            pltpu.VMEM((tile, hidden), BF),
            pltpu.VMEM((tile, hidden), F32),
            pltpu.VMEM((8, width), F32),
            pltpu.VMEM((ROWS, SUMS), BF),
            pltpu.SemaphoreType.DMA((2,)),
        ],
        compiler_params=pltpu.CompilerParams(vmem_limit_bytes=VMEM),
        cost_estimate=pl.CostEstimate(
            flops=6 * length * width * (3 * width + 2 * hidden), bytes_accessed=24 * MIB, transcendentals=length * hidden
        ),
        name="feed_forward",
    )(me, order, tokens, normed, mixed, out_grad, small, *pieces)


def finish_kernel(tokens, zeta_one_low, grad_middle, weights, gate_attn, small, *refs):
    *grads, _after, token_grad = refs
    groups = len(grads) // 3
    width = tokens.shape[1]
    part = width // groups
    total = dot_t(zeta_one_low[...], gate_attn[...])
    for at, grad in enumerate(grads):
        which, group = at % 3, at // 3
        columns = pl.ds(which * width + group * part, part)
        total = total + dot_t(grad[...], weights[:, columns])
    unit, scale = normalise(tokens[...].astype(F32))
    grad_unit = total * small[0:1, :]
    token_grad[...] = grad_middle[...] + scale * (
        grad_unit - row_mean(grad_unit) - unit * row_mean(grad_unit * unit)
    )


def finish(tokens, zeta_one_low, grad_middle, weights, gate_attn, small, grads, after):
    length, width = tokens.shape
    tile = 512
    by_rows = pl.BlockSpec((tile, width), lambda i: (i, 0))
    return pl.pallas_call(
        finish_kernel,
        grid=(length // tile,),
        in_specs=[
            by_rows, by_rows, by_rows,
            pl.BlockSpec((width, 3 * width), lambda i: (0, 0)),
            pl.BlockSpec((width, width), lambda i: (0, 0)),
            pl.BlockSpec((4, width), lambda i: (0, 0)),
        ] + [pl.BlockSpec((tile, g.shape[1]), lambda i: (i, 0)) for g in grads]
        + [pl.BlockSpec(memory_space=pl.ANY)],
        out_specs=by_rows,
        out_shape=jax.ShapeDtypeStruct((length, width), F32),
        compiler_params=pltpu.CompilerParams(vmem_limit_bytes=VMEM),
        cost_estimate=pl.CostEstimate(
            flops=8 * length * width * width, bytes_accessed=16 * MIB, transcendentals=length
        ),
        name="finish",
    )(tokens, zeta_one_low, grad_middle, weights, gate_attn, small, *grads, after)


def row_sum(weight, grad):
    return jnp.sum(weight.astype(F32) * grad, axis=1, keepdims=True)


def close_kernel(
    query, key, value, gate_attn, gate_ffn, w_in, *refs
):
    *parts, _after, grad_query, grad_key, grad_value, grad_output, grad_gate_attn, grad_gate_ffn, grad_in, grad_out, norms, summed = refs
    width = query.shape[1]
    wide = w_in.shape[1]
    add = lambda four, columns: sum(p[:, columns].astype(F32) for p in four)
    late, early = parts[:4], parts[4:]
    total = jnp.zeros((ROWS, 1), F32)
    for k, (weight, out) in enumerate(((query, grad_query), (key, grad_key), (value, grad_value))):
        grad = add(late, pl.ds(k * width, width))
        out[...] = grad
        total = total + row_sum(weight[...], grad)
    grad_output[...] = add(early, pl.ds(0, width))
    grad = add(early, pl.ds(width, width))
    grad_gate_attn[...] = grad
    total = total + row_sum(gate_attn[...], grad)
    grad = add(early, pl.ds(2 * width, width))
    grad_gate_ffn[...] = grad
    other = row_sum(gate_ffn[...], grad)
    grad = add(early, pl.ds(3 * width, wide))
    grad_in[...] = grad
    other = other + row_sum(w_in[...], grad)
    for group in range(4):
        grad_out[pl.ds(group * ROWS, ROWS), :] = add(early, pl.ds(3 * width + wide + group * width, width))
    lane = lax.broadcasted_iota(jnp.int32, (ROWS, 128), 1)
    norms[...] = jnp.where(lane == 0, total, jnp.where(lane == 1, other, 0.0))
    gathered = sum(read_sums(p[:, pl.ds(REST, SUMS)]) for p in early)
    summed[...] = jnp.concatenate([gathered, jnp.zeros((2, width), F32)], axis=0)


def close(query, key, value, gate_attn, gate_ffn, w_in, late, early, after):
    width, wide = query.shape[1], w_in.shape[1]
    vmem = pl.BlockSpec(memory_space=pltpu.VMEM)
    square = jax.ShapeDtypeStruct((ROWS, width), F32)
    return pl.pallas_call(
        close_kernel,
        in_specs=[vmem] * 14 + [pl.BlockSpec(memory_space=pl.ANY)],
        out_shape=[square] * 6 + [
            jax.ShapeDtypeStruct((ROWS, wide), F32),
            jax.ShapeDtypeStruct((4 * ROWS, width), F32),
            jax.ShapeDtypeStruct((ROWS, 128), F32),
            jax.ShapeDtypeStruct((8, width), F32),
        ],
        compiler_params=pltpu.CompilerParams(vmem_limit_bytes=VMEM),
        name="close",
    )(query, key, value, gate_attn, gate_ffn, w_in, *late, *early, after)


def swap(values, axis, bits):
    count = lax.axis_size(axis)
    return lax.ppermute(values, axis, [(i, i ^ bits) for i in range(count)])


def gather_pieces(values):
    line = jnp.concatenate([values] + [swap(values, "narrow", k) for k in (1, 2, 3)])
    return [line] + [swap(line, "wide", 2 * k) for k in (1, 2, 3)]


def both_cores(near):
    return list(near) + [swap(piece, "wide", 1) for piece in near]


def hold_kernel(*refs):
    pass


def hold(arrays, *after):
    count = len(arrays)
    anywhere = pl.BlockSpec(memory_space=pl.ANY)
    return pl.pallas_call(
        hold_kernel,
        in_specs=[anywhere] * (count + len(after)),
        out_specs=[anywhere] * count,
        out_shape=[jax.ShapeDtypeStruct(a.shape, a.dtype) for a in arrays],
        input_output_aliases={k: k for k in range(count)},
        name="hold",
    )(*arrays, *after)


def add_kernel(*refs, terms, each, sums):
    sources, targets = refs[:terms], refs[terms + 1 :]
    columns = targets[0].shape[-1]
    main = columns - SUMS if sums else columns
    for at, target in enumerate(targets):
        for block in range(each):
            index = at * each + block
            total = sources[0][index, :, :main].astype(F32)
            for source in sources[1:]:
                total = total + source[index, :, :main].astype(F32)
            target[block, :, :main] = total.astype(BF)
    if sums:
        gathered = sum(read_sums(source[0, :, main:]) for source in sources)
        write_sums(gathered, targets[0].at[0, :, pl.ds(main, SUMS)])
        tile = targets[0][0, :, main:]
        for target in targets:
            for block in range(each):
                target[block, :, main:] = tile


def add_split(arrays, sums, after):
    blocks, _, columns = arrays[0].shape
    each = blocks // 4
    vmem = pl.BlockSpec(memory_space=pltpu.VMEM)
    return pl.pallas_call(
        partial(add_kernel, terms=len(arrays), each=each, sums=sums),
        in_specs=[vmem] * len(arrays) + [pl.BlockSpec(memory_space=pl.ANY)],
        out_specs=[vmem] * 4,
        out_shape=[jax.ShapeDtypeStruct((each, ROWS, columns), BF)] * 4,
        compiler_params=pltpu.CompilerParams(vmem_limit_bytes=VMEM),
        name="add_split",
    )(*arrays, after)


def add_core(send, keep, sums, after):
    return add_split([keep, swap(send, "wide", 1)], sums, after)


def swap_plane(plane):
    return [swap(plane[k], "wide", 2 * k) for k in (1, 2, 3)]


def along_line(line):
    return [line[0][0]] + [swap(line[k], "narrow", k)[0] for k in (1, 2, 3)]


def natural(send, keep):
    columns = keep.shape[-1]
    halves = jnp.stack([keep, send]).reshape(2, 4, 4, ROWS, columns)
    return halves.transpose(1, 0, 2, 3, 4).reshape(BLOCKS * ROWS, columns)


def pack_kernel(device, vectors, *refs):
    *shards, first, rest = refs
    own = vectors.shape[1]
    column, row = lax.rem(device[0] * own, 128), lax.div(device[0] * own, 128)
    at = 0
    for shard in shards[:3]:
        first[:, at : at + shard.shape[1]] = shard[...]
        at += shard.shape[1]
    values = vectors[...].astype(F32)
    wide = pltpu.roll(jnp.concatenate([values, jnp.zeros((4, 128 - own), F32)], axis=1), column, 1)
    place = lax.broadcasted_iota(jnp.int32, (ROWS, 128), 0)
    tile = jnp.zeros((ROWS, 128), F32)
    for vector in range(4):
        tile = jnp.where(place == vector * 4 + row, wide[vector : vector + 1], tile)
    first[:, at:] = tile.astype(BF)
    at = 0
    for shard in shards[3:7]:
        rest[:, at : at + shard.shape[1]] = shard[...]
        at += shard.shape[1]
    tall = shards[7]
    for group in range(4):
        wide = tall.shape[1]
        rest[:, at : at + wide] = tall[group * ROWS : (group + 1) * ROWS]
        at += wide


def pack(device, vectors, *shards):
    return pl.pallas_call(
        pack_kernel,
        in_specs=[pl.BlockSpec(memory_space=pltpu.SMEM)]
        + [pl.BlockSpec(memory_space=pltpu.VMEM)] * (1 + len(shards)),
        out_shape=[
            jax.ShapeDtypeStruct((ROWS, FIRST), BF),
            jax.ShapeDtypeStruct((ROWS, REST), BF),
        ],
        compiler_params=pltpu.CompilerParams(vmem_limit_bytes=VMEM),
        name="pack",
    )(device, vectors, *shards)


def per_device(
    tokens, segment, w_query, w_key, w_value, w_output, gate_attn, gate_ffn, w_in, w_out,
    norm_attn, norm_ffn, bias_attn, bias_ffn, out_grad,
):
    wide, narrow = lax.axis_size("wide"), lax.axis_size("narrow")
    devices = wide * narrow
    length, width = tokens.shape
    hidden = w_in.shape[1]
    own_rows = w_query.shape[0]
    device = lax.axis_index("wide") * narrow + lax.axis_index("narrow")
    direct = wide == 8 and narrow == 4 and own_rows == ROWS
    vectors = (norm_attn, norm_ffn, bias_attn, bias_ffn)

    def gather(values):
        return lax.all_gather(values, AXES, axis=0, tiled=True)

    if direct:
        me = device.astype(jnp.int32).reshape(1)
        first, rest = pack(
            me, jnp.stack(vectors), w_query, w_key, w_value, w_output, gate_attn, gate_ffn, w_in, w_out
        )
        pieces = both_cores(gather_pieces(first))
        rest_near = gather_pieces(rest)
        order = jnp.concatenate(
            [
                jnp.bitwise_xor(device, (jnp.arange(16) // 4 * 2 + half) * 4 + jnp.arange(16) % 4)
                for half in range(2)
            ]
        ).astype(jnp.int32)
    else:
        full = gather(jnp.stack(vectors, axis=1))
        tile = jnp.zeros((BLOCKS, ROWS, 128), BF).at[0].set(full.T.reshape(ROWS, 128))
        first = jnp.concatenate(
            [gather(w_query), gather(w_key), gather(w_value), tile.reshape(BLOCKS * ROWS, 128)], axis=1
        )
        out_blocks = gather(w_out).reshape(BLOCKS, 4, ROWS, width).transpose(0, 2, 1, 3)
        packet = jnp.concatenate(
            [gather(w_output), gather(gate_attn), gather(gate_ffn), gather(w_in),
             out_blocks.reshape(BLOCKS * ROWS, 4 * width)], axis=1
        )
        pieces = [first[k * 64 : (k + 1) * 64] for k in range(8)]
        rest_pieces = [packet[k * 64 : (k + 1) * 64] for k in range(8)]
        me = jnp.zeros((1,), jnp.int32)
        order = jnp.arange(BLOCKS, dtype=jnp.int32)

    segment_row = segment.reshape(1, length)
    normed, normed_t, query, key, value, key_t, value_t, weights, small = project(order, tokens, pieces)
    mixed, log_total = attend(segment, segment_row, query, key, value_t)
    if direct:
        rest_pieces = both_cores(rest_near[:1] + list(hold(rest_near[1:], mixed)))
    result, grad_middle, zeta_one_low, grad_mixed, inner_sum, whole_gate, send, keep = feed_forward(
        me, order, tokens, normed, mixed, out_grad, small, rest_pieces
    )
    plane = add_core(send, keep, True, me) if direct else [me]
    *grads, late_send, late_keep = attend_back(
        me, segment, segment_row, query, key, value, key_t, grad_mixed, log_total, inner_sum,
        normed_t, plane[0], 0, HEADS,
    )
    if direct:
        received = swap_plane(plane)
        (late_send,) = hold([late_send], *received)
        line = add_split([plane[0]] + received, True, late_send)
        late_plane = add_core(late_send, late_keep, False, line[0])
    else:
        late_plane = [me]
    token_grad = finish(
        tokens, zeta_one_low, grad_middle, weights, whole_gate, small, grads, late_plane[0]
    )

    straight = 3 * width + hidden
    if direct:
        early = along_line(line)
        late = along_line(add_split([late_plane[0]] + swap_plane(late_plane), False, token_grad))
        *owned, norms, summed = close(
            w_query, w_key, w_value, gate_attn, gate_ffn, w_in, late, early, token_grad
        )
        norm_one, norm_two = norms[:, 0], norms[:, 1]
    else:

        def scatter(values):
            return lax.psum_scatter(values, AXES, scatter_dimension=0, tiled=True)

        tile = keep[0, :, REST:].astype(F32)
        spill = tile[12:].reshape(12, 128)
        rows = jnp.concatenate([tile[:12], spill], axis=1)
        own_sums = rows[:6] + rows[6:]
        whole = natural(send, keep)[:, :REST].astype(F32)
        out_whole = whole[:, straight:].reshape(BLOCKS, ROWS, 4, width).transpose(0, 2, 1, 3)
        first = scatter(natural(late_send, late_keep).astype(F32))
        second = scatter(whole[:, :straight])
        owned = [first[:, k * width : (k + 1) * width] for k in range(3)]
        owned += [second[:, k * width : (k + 1) * width] for k in range(3)]
        owned += [second[:, 3 * width :], scatter(out_whole.reshape(hidden, width))]
        shards = (w_query, w_key, w_value, gate_attn)
        norm_one = sum(row_sum(w, g)[:, 0] for w, g in zip(shards, owned[:3] + owned[4:5]))
        norm_two = (row_sum(gate_ffn, owned[5]) + row_sum(w_in, owned[6]))[:, 0]
        summed = lax.psum(own_sums, AXES)

    grad_norm_attn = norm_one / norm_attn.astype(F32)
    grad_norm_ffn = norm_two / norm_ffn.astype(F32)
    counted = length * devices
    mean_one = summed[0] / counted
    mean_two = summed[2] / counted
    gate_stats = jnp.stack(
        [
            mean_one,
            summed[1] / counted - mean_one * mean_one,
            mean_two,
            summed[3] / counted - mean_two * mean_two,
        ]
    )
    own = lax.dynamic_slice(summed, (4, device * own_rows), (2, own_rows))
    return (result, token_grad, *owned, grad_norm_attn, grad_norm_ffn, own[0], own[1], gate_stats)


def solution(mesh):
    rows = P(AXES, None)
    flat = P(AXES)
    in_specs = (rows, flat) + (rows,) * 8 + (flat,) * 4 + (rows,)
    out_specs = (rows,) * 10 + (flat,) * 4 + (P(),)
    return jax.shard_map(
        per_device, mesh=mesh, in_specs=in_specs, out_specs=out_specs, check_vma=False
    )
```

time: 1720 us -> 221 us (0.13)
  waiting for transfers between devices: 778 us -> 20 us
  blocking collectives: 511 us -> 0 us
  matrix products: 302 us -> 0 us
  Pallas kernels: 0 us -> 144 us
  other arithmetic: 85.4 us -> 4.4 us
  starting transfers between devices: 0.79 us -> 37.7 us
    reduce_scatter x8 -> x0, waiting for transfers between devices: 776 us -> none  [the longest x1 150 us: reduce_grads(): lax.psum_scatter(grad_in, ('wide', 'narrow'), scatter_dimension=0, tiled=...]
    all_gather x6 -> x0, blocking collectives: 429 us -> none  [the longest x1 74.2 us: fetch_forward(): lax.all_gather(gate_attn, ('wide', 'narrow'), axis=0, tiled=True)]
    dot_general x34 -> x0, matrix products: 264 us -> none  [the longest x2 57.2 us: attention_backward(): jnp.einsum('qhd,khd->hqk', grad_block, values, preferred_element_type=jnp...]
    pallas_call x0 -> x13, Pallas kernels: none -> 144 us  [the longest x1 44.6 us: feed_forward(): pl.pallas_call(feed_kernel, grid=(length // tile,), in_specs=[pl.BlockSpe...]
    unnamed x2 -> x0, blocking collectives: 81.6 us -> none
    convert_element_type x7 -> x0, other arithmetic: 63 us -> none  [the longest x2 62.4 us: attention_backward(): grad_scores = (probability * (grad_probs - inner_sum)).astype(jnp.bfloat16)]
    sub x2 -> x0, matrix products: 37.8 us -> none  [attention_forward(): exponent = jnp.exp(scores - row_peak)]
    ppermute x0 -> x34, starting transfers between devices: none -> 37.7 us  [swap(): return lax.ppermute(values, axis, [(i, i ^ bits) for i in range(count)])]
  transfers between devices with their start and end apart: 10 -> 34, of which waited for: 6 -> 10; matrix products, arithmetic and copies ran while one was open for 22% -> 2% of each run, Pallas kernels for 0% -> 40%
where the time goes in v1:
time: 221 us
  Pallas kernels  144 us (65%)
  starting transfers between devices  37.7 us (17%)
  waiting for transfers between devices  20 us (9%)
  local copies, waits for them, and re-layouts  14.2 us (6%)
  other arithmetic  4.4 us (2%)
    pallas_call x1, Pallas kernels, feed_forward(): pl.pallas_call(feed_kernel, grid=(length // tile,), in_specs=[pl.BlockSpe...  44.6 us
    pallas_call x1, Pallas kernels, attend_back(): pl.pallas_call(partial(attend_back_kernel, heads=heads), grid_spec=pltpu....  39 us
    ppermute x34, starting transfers between devices, swap(): return lax.ppermute(values, axis, [(i, i ^ bits) for i in range(count)])  37.7 us
    pallas_call x1, Pallas kernels, attend(): pl.pallas_call(attend_kernel, grid_spec=pltpu.PrefetchScalarGridSpec(num_...  26.1 us
    ppermute x34, waiting for transfers between devices, swap(): return lax.ppermute(values, axis, [(i, i ^ bits) for i in range(count)])  20 us
    pallas_call x4, Pallas kernels, add_split(): pl.pallas_call(partial(add_kernel, terms=len(arrays), each=each, sums=sum...  12.2 us
    unnamed x68, local copies, waits for them, and re-layouts  10.6 us
    pallas_call x1, Pallas kernels, finish(): pl.pallas_call(finish_kernel, grid=(length // tile,), in_specs=[by_rows,...  9.46 us
  transfers between devices with their start and end apart: 34, of which 10 were waited for; matrix products, arithmetic and copies ran while one was open for 2% of the time, Pallas kernels for 40%

profile of v1, /device:TPU:0, one launch (start us, length us, event | category | flops | bytes accessed | tf_op | source)
XLA Modules:
  0.0 221.0 jit_solution(29931784972859530)
XLA Ops:
  0.7 1.3 pad_maximum_fusion.1.vectors
  1.9 1.7 pack.1
  3.6 3.0 %collective-permute-start = (bf16[16,1664]{1,0:T(8,128)(2,1)}, bf16[16,1664]{1,0:T(8,128)(2,1)S(1)}, u32[]{:S(2)}, u32[]{:S(2)}) collective-permute-start(bf16[16,1664]{1,0:T(8,128)(2,1)} %get-tuple-element.70), channel_id=1, source_target_pairs={{0,1},{1,0},{2,3},{3,2},{4,5},{5,4},{6,7},{7,6},{8,9},{9,8},{10,11... | collective-permute-start | bytes 159752 | tf_op jit(solution)/shard_map/ppermute | solution.py:655
  6.6 2.6 %collective-permute-start.1 = (bf16[16,1664]{1,0:T(8,128)(2,1)}, bf16[16,1664]{1,0:T(8,128)(2,1)S(1)}, u32[]{:S(2)}, u32[]{:S(2)}) collective-permute-start(bf16[16,1664]{1,0:T(8,128)(2,1)} %get-tuple-element.70), channel_id=1, source_target_pairs={{0,2},{1,3},{2,0},{3,1},{4,6},{5,7},{6,4},{7,5},{8,10},{9,11},{10,... | collective-permute-start | bytes 159752 | tf_op jit(solution)/shard_map/ppermute | solution.py:655
  9.2 0.9 collective-permute-start.10
  10.1 3.5 %collective-permute-start.11 = (bf16[16,5632]{1,0:T(8,128)(2,1)}, bf16[16,5632]{1,0:T(8,128)(2,1)S(1)}, u32[]{:S(2)}, u32[]{:S(2)}) collective-permute-start(bf16[16,5632]{1,0:T(8,128)(2,1)} %get-tuple-element.77), channel_id=1, source_target_pairs={{0,2},{1,3},{2,0},{3,1},{4,6},{5,7},{6,4},{7,5},{8,10},{9,11},{10,... | collective-permute-start | bytes 540680 | tf_op jit(solution)/shard_map/ppermute | solution.py:655
  13.6 0.8 constant_dynamic-update-slice_fusion.3
  14.4 0.9 constant_dynamic-update-slice_fusion.7
  15.4 0.6 pad_add_fusion.order
  16.0 1.3 reshape.43.segment_row
  17.3 1.8 collective-permute-start.3
  19.1 1.5 collective-permute-start.4
  20.6 1.9 collective-permute-start.5
  22.5 4.9 %collective-permute-done.11 = bf16[16,5632]{1,0:T(8,128)(2,1)S(1)} collective-permute-done((bf16[16,5632]{1,0:T(8,128)(2,1)}, bf16[16,5632]{1,0:T(8,128)(2,1)S(1)}, u32[]{:S(2)}, u32[]{:S(2)}) %collective-permute-start.11) | collective-permute-done | bytes 180256 | tf_op jit(solution)/shard_map/ppermute | solution.py:655
  27.4 0.6 collective-permute-start.7
  28.0 1.2 collective-permute-done.4.refs_2_
  29.2 0.5 collective-permute-start.9
  30.2 2.0 collective-permute-start.14
  32.2 1.1 collective-permute-start.15
  33.3 0.7 copy-done.27
  34.0 8.3 %project.1 = (bf16[1536,512]{1,0:T(8,128)(2,1)}, bf16[512,1536]{1,0:T(8,128)(2,1)}, bf16[1536,512]{1,0:T(8,128)(2,1)}, bf16[1536,512]{1,0:T(8,128)(2,1)}, bf16[1...) custom-call(s32[32]{0:T(128)} %pad_add_fusion.order, ...), custom_call_target="tpu_custom_call" | custom-call | flops 2415919104 | bytes 12582912 | tf_op jit(solution)/shard_map/project/pallas_call | solution.py:103
  42.4 26.1 %attend.1 = (f32[1536,512]{1,0:T(8,128)}, f32[8,1536]{1,0:T(8,128)}) custom-call(s32[1536]{0:T(1024)} %segment.3, s32[1,1536]{1,0:T(1,128)} %reshape.43.segment_row, bf16[1536,512]{1,0:T(8,128)(2,1)} %get-tuple-element.72.query, bf16[1536,512]{1,0:T(8,128)(2,1)} %get-tuple-element.73.key, bf16[512,1536]{1,0:T(8,128)(2,1)} %get-tuple-element.74.value_t), custom_call_target="tpu_custom_call" | custom-call | flops 9663676416 | bytes 6291456 | tf_op jit(solution)/shard_map/attend/pallas_call | solution.py:188
  68.6 0.8 copy-done.5
  70.0 0.5 collective-permute-start.17
  70.5 0.5 collective-permute-start.19
  71.0 1.5 collective-permute-done.17.refs_5_
  72.5 1.0 collective-permute-done.18.refs_6_
  73.5 1.0 collective-permute-done.19.refs_7_
  74.6 0.9 copy-done.23
  75.4 44.6 %feed_forward.1 = (bf16[1536,512]{1,0:T(8,128)(2,1)}, f32[1536,512]{1,0:T(8,128)}, bf16[1536,512]{1,0:T(8,128)(2,1)}, bf16[1536,512]{1,0:T(8,128)(2,1)}, f32[8,1...) custom-call(s32[1]{0:T(128)} %bitcast.device.me.refs_2_, ...), custom_call_target="tpu_custom_call" | custom-call | flops 26575110144 | bytes 25165824 | tf_op jit(solution)/shard_map/feed_forward/pallas_call | solution.py:513
  120.5 5.4 %collective-permute-done.20.refs_1_ = bf16[16,16,6016]{2,1,0:T(8,128)(2,1)S(1)} collective-permute-done((bf16[16,16,6016]{2,1,0:T(8,128)(2,1)}, bf16[16,16,6016]{2,1,0:T(8,128)(2,1)S(1)}, u32[]{:S(2)}, u32[]{:S(2)}) %collective-permute-start.20) | collective-permute-done | bytes 3080224 | tf_op jit(solution)/shard_map/ppermute | solution.py:655
  125.9 1.6 copy-done
  127.5 4.9 %add_split.4 = (bf16[4,16,6016]{2,1,0:T(8,128)(2,1)}, bf16[4,16,6016]{2,1,0:T(8,128)(2,1)}, bf16[4,16,6016]{2,1,0:T(8,128)(2,1)}, bf16[4,16,6016]{2,1,0:T(8,128)(2,1)}) custom-call(bf16[16,16,6016]{2,1,0:T(8,128)(2,1)} %get-tuple-element.92.refs_0_, bf16[16,16,6016]{2,1,0:T(8,128)(2,1)} %copy-done, s32[1]{0:T(128)} %bitcast.device.me.refs_2_), custom_call_target="tpu_custom_call" | custom-call | tf_op jit(solution)/shard_map/add_split/pallas_call | solution.py:708
  132.4 0.5 collective-permute-start.21
  132.9 2.0 collective-permute-start.22
  134.8 1.1 collective-permute-start.23
  135.9 39.0 %attend_back_0.1 = (bf16[1536,512]{1,0:T(8,128)(2,1)}, bf16[1536,512]{1,0:T(8,128)(2,1)}, bf16[1536,512]{1,0:T(8,128)(2,1)}, bf16[16,16,1536]{2,1,0:T(8,128)(2,1)}, bf16[16,16,1536]{2,1,0:T(8,128)(2,1)}) custom-call(s32[1]{0:T(128)} %bitcast.device.me.refs_2_, s32[1536]{0:T(1024)} %segment.3, s32[1,1536]{1,0:T(1,128)} %reshape.43.segment_row, ...), custom_call_target="tpu_custom_call" | custom-call | flops 24159191040 | bytes 8388608 | tf_op jit(solution)/shard_map/attend_back_0/pallas_call | solution.py:323
  175.0 0.8 copy-done.1
  176.4 3.1 %add_split.5 = (bf16[1,16,6016]{2,1,0:T(8,128)(2,1)}, bf16[1,16,6016]{2,1,0:T(8,128)(2,1)}, bf16[1,16,6016]{2,1,0:T(8,128)(2,1)}, bf16[1,16,6016]{2,1,0:T(8,128)(2,1)}) custom-call(bf16[4,16,6016]{2,1,0:T(8,128)(2,1)} %get-tuple-element.94._after.refs_0_, bf16[4,16,6016]{2,1,0:T(8,128)(2,1)} %copy-done.1, bf16[4,16,6016]{2,1,0:T(8,128)(2,1)} %copy-done.2, ...), custom_call_target="tpu_custom_call" | custom-call | tf_op jit(solution)/shard_map/add_split/pallas_call | solution.py:708
  179.4 0.9 copy-done.4
  180.3 2.3 %add_split.6 = (bf16[4,16,1536]{2,1,0:T(8,128)(2,1)}, bf16[4,16,1536]{2,1,0:T(8,128)(2,1)}, bf16[4,16,1536]{2,1,0:T(8,128)(2,1)}, bf16[4,16,1536]{2,1,0:T(8,128)(2,1)}) custom-call(bf16[16,16,1536]{2,1,0:T(8,128)(2,1)} %get-tuple-element.98.refs_0_, bf16[16,16,1536]{2,1,0:T(8,128)(2,1)} %copy-done.4, bf16[1,16,6016]{2,1,0:T(8,128)(2,1)} %get-tuple-element.103.refs_2_), custom_call_target="tpu_custom_call" | custom-call | tf_op jit(solution)/shard_map/add_split/pallas_call | solution.py:708
  182.8 1.8 collective-permute-start.31
  184.6 2.5 %collective-permute-start.32 = (bf16[1,16,6016]{2,1,0:T(8,128)(2,1)S(1)}, bf16[1,16,6016]{2,1,0:T(8,128)(2,1)S(1)}, u32[]{:S(2)}, u32[]{:S(2)}) collective-permute-start(bf16[1,16,6016]{2,1,0:T(8,128)(2,1)S(1)} %copy-done.29), channel_id=1, source_target_pairs={{0,2},{1,3},{2,0},{3,1},{4,6},{5,7},{6,4},{7,5},{8,10},{9,11},{10,... | collective-permute-start | bytes 577544 | tf_op jit(solution)/shard_map/ppermute | solution.py:655
  187.2 2.2 %collective-permute-start.26 = (bf16[4,16,1536]{2,1,0:T(8,128)(2,1)}, bf16[4,16,1536]{2,1,0:T(8,128)(2,1)S(1)}, u32[]{:S(2)}, u32[]{:S(2)}) collective-permute-start(bf16[4,16,1536]{2,1,0:T(8,128)(2,1)} %get-tuple-element.106), channel_id=1, source_target_pairs={{0,16},{4,20},{8,24},{12,28},{16,0},{20,4},{24,8},{28,12},{1,17},{... | collective-permute-start | bytes 589832 | tf_op jit(solution)/shard_map/ppermute | solution.py:655
  189.5 0.7 collective-permute-done.25.refs_1_
  190.2 1.8 collective-permute-start.27
  192.0 9.5 %finish.1.refs_4_.refs_8_ = f32[1536,512]{1,0:T(8,128)} custom-call(bf16[1536,512]{1,0:T(8,128)(2,1)} %tokens.5, bf16[1536,512]{1,0:T(8,128)(2,1)} %get-tuple-element.82.zeta_one_low, f32[1536,512]{1,0:T(8,128)} %get-tuple-element.83.grad_middle, bf16[512,1536]{1,0:T(8,128)(2,1)} %get-tuple-element.84.weights, bf16[512,512]{1,0:T(8,128)(2,1)} %get-tuple-element.85.gate_attn, ...), custom_call_target="tpu_custom_call" | custom-call | flops 3221225472 | bytes 16777216 | tf_op jit(solution)/shard_map/finish/pallas_call | solution.py:580
  201.5 0.7 copy-done.9
  202.2 0.7 copy-done.10
  202.9 2.0 add_split.7
  204.8 3.3 %collective-permute-start.30 = (bf16[1,16,1536]{2,1,0:T(8,128)(2,1)}, bf16[1,16,1536]{2,1,0:T(8,128)(2,1)S(1)}, u32[]{:S(2)}, u32[]{:S(2)}) collective-permute-start(bf16[1,16,1536]{2,1,0:T(8,128)(2,1)} %get-tuple-element.111), channel_id=1, source_target_pairs={{0,3},{1,2},{2,1},{3,0},{4,7},{5,6},{6,5},{7,4},{8,11},{9,10},{10,... | collective-permute-start | bytes 147464 | tf_op jit(solution)/shard_map/ppermute | solution.py:655
  208.2 1.1 collective-permute-start.29
  209.2 1.8 collective-permute-done.30
  211.0 1.4 collective-permute-done.28
  212.4 1.0 collective-permute-done.29
  213.4 0.6 copy-done.16
  214.0 2.2 close.1
  216.2 0.9 slice_multiply_fusion.1
  217.1 0.8 constant_dynamic-slice_fusion
  217.8 0.5 slice_bitcast_fusion
  218.3 1.0 slice_reduce_fusion
  219.3 0.5 convert_divide_fusion
  219.8 0.5 convert_divide_fusion.1
  220.4 0.6 pad_maximum_fusion
  (98 shorter events, 2.5 us)
Async XLA Ops:
  3.6 13.6 %collective-permute-start = (bf16[16,1664]{1,0:T(8,128)(2,1)}, bf16[16,1664]{1,0:T(8,128)(2,1)S(1)}, u32[]{:S(2)}, u32[]{:S(2)}) collective-permute-start(bf16[16,1664]{1,0:T(8,128)(2,1)} %get-tuple-element.70), channel_id=1, source_target_pairs={{0,1},{1,0},{2,3},{3,2},{4,5},{5,4},{6,7},{7,6},{8,9},{9,8},{10,11... | collective-permute-start | bytes 159752 | tf_op jit(solution)/shard_map/ppermute | solution.py:655
  6.6 10.6 %collective-permute-start.1 = (bf16[16,1664]{1,0:T(8,128)(2,1)}, bf16[16,1664]{1,0:T(8,128)(2,1)S(1)}, u32[]{:S(2)}, u32[]{:S(2)}) collective-permute-start(bf16[16,1664]{1,0:T(8,128)(2,1)} %get-tuple-element.70), channel_id=1, source_target_pairs={{0,2},{1,3},{2,0},{3,1},{4,6},{5,7},{6,4},{7,5},{8,10},{9,11},{10,... | collective-permute-start | bytes 159752 | tf_op jit(solution)/shard_map/ppermute | solution.py:655
  9.2 8.1 %collective-permute-start.2 = (bf16[16,1664]{1,0:T(8,128)(2,1)}, bf16[16,1664]{1,0:T(8,128)(2,1)S(1)}, u32[]{:S(2)}, u32[]{:S(2)}) collective-permute-start(bf16[16,1664]{1,0:T(8,128)(2,1)} %get-tuple-element.70), channel_id=1, source_target_pairs={{0,3},{1,2},{2,1},{3,0},{4,7},{5,6},{6,5},{7,4},{8,11},{9,10},{10,... | collective-permute-start | bytes 159752 | tf_op jit(solution)/shard_map/ppermute | solution.py:655
  9.2 11.4 %collective-permute-start.10 = (bf16[16,5632]{1,0:T(8,128)(2,1)}, bf16[16,5632]{1,0:T(8,128)(2,1)S(1)}, u32[]{:S(2)}, u32[]{:S(2)}) collective-permute-start(bf16[16,5632]{1,0:T(8,128)(2,1)} %get-tuple-element.77), channel_id=1, source_target_pairs={{0,1},{1,0},{2,3},{3,2},{4,5},{5,4},{6,7},{7,6},{8,9},{9,8},{10,11... | collective-permute-start | bytes 540680 | tf_op jit(solution)/shard_map/ppermute | solution.py:655
  10.1 17.2 %collective-permute-start.11 = (bf16[16,5632]{1,0:T(8,128)(2,1)}, bf16[16,5632]{1,0:T(8,128)(2,1)S(1)}, u32[]{:S(2)}, u32[]{:S(2)}) collective-permute-start(bf16[16,5632]{1,0:T(8,128)(2,1)} %get-tuple-element.77), channel_id=1, source_target_pairs={{0,2},{1,3},{2,0},{3,1},{4,6},{5,7},{6,4},{7,5},{8,10},{9,11},{10,... | collective-permute-start | bytes 540680 | tf_op jit(solution)/shard_map/ppermute | solution.py:655
  17.3 12.4 %collective-permute-start.12 = (bf16[16,5632]{1,0:T(8,128)(2,1)}, bf16[16,5632]{1,0:T(8,128)(2,1)S(1)}, u32[]{:S(2)}, u32[]{:S(2)}) collective-permute-start(bf16[16,5632]{1,0:T(8,128)(2,1)} %get-tuple-element.77), channel_id=1, source_target_pairs={{0,3},{1,2},{2,1},{3,0},{4,7},{5,6},{6,5},{7,4},{8,11},{9,10},{10,... | collective-permute-start | bytes 540680 | tf_op jit(solution)/shard_map/ppermute | solution.py:655
  17.3 16.6 %copy-start.18 = (bf16[64,1664]{1,0:T(8,128)(2,1)}, bf16[64,1664]{1,0:T(8,128)(2,1)S(1)}, u32[]{:S(2)}) copy-start(bf16[64,1664]{1,0:T(8,128)(2,1)S(1)} %constant_dynamic-update-slice_fusion.refs_0_) | copy-start | bytes 638980
  17.3 10.0 %collective-permute-start.3 = (bf16[64,1664]{1,0:T(8,128)(2,1)S(1)}, bf16[64,1664]{1,0:T(8,128)(2,1)S(1)}, u32[]{:S(2)}, u32[]{:S(2)}) collective-permute-start(bf16[64,1664]{1,0:T(8,128)(2,1)S(1)} %constant_dynamic-update-slice_fusion.refs_0_), channel_id=1, source_target_pairs={{0,8},{4,12},{8,0},{12,4},{16,24},{20,28},{24,16},{28,20},{1,9},{5... | collective-permute-start | bytes 638984 | tf_op jit(solution)/shard_map/ppermute | solution.py:655
  19.1 10.0 %collective-permute-start.4 = (bf16[64,1664]{1,0:T(8,128)(2,1)S(1)}, bf16[64,1664]{1,0:T(8,128)(2,1)S(1)}, u32[]{:S(2)}, u32[]{:S(2)}) collective-permute-start(bf16[64,1664]{1,0:T(8,128)(2,1)S(1)} %constant_dynamic-update-slice_fusion.refs_0_), channel_id=1, source_target_pairs={{0,16},{4,20},{8,24},{12,28},{16,0},{20,4},{24,8},{28,12},{1,17},{... | collective-permute-start | bytes 638984 | tf_op jit(solution)/shard_map/ppermute | solution.py:655
  20.6 8.5 %collective-permute-start.5 = (bf16[64,1664]{1,0:T(8,128)(2,1)S(1)}, bf16[64,1664]{1,0:T(8,128)(2,1)S(1)}, u32[]{:S(2)}, u32[]{:S(2)}) collective-permute-start(bf16[64,1664]{1,0:T(8,128)(2,1)S(1)} %constant_dynamic-update-slice_fusion.refs_0_), channel_id=1, source_target_pairs={{0,24},{4,28},{8,16},{12,20},{16,8},{20,12},{24,0},{28,4},{1,25},{... | collective-permute-start | bytes 638984 | tf_op jit(solution)/shard_map/ppermute | solution.py:655
  27.4 2.8 %collective-permute-start.6 = (bf16[64,1664]{1,0:T(8,128)(2,1)S(1)}, bf16[64,1664]{1,0:T(8,128)(2,1)}, u32[]{:S(2)}, u32[]{:S(2)}) collective-permute-start(bf16[64,1664]{1,0:T(8,128)(2,1)S(1)} %constant_dynamic-update-slice_fusion.refs_0_), channel_id=1, source_target_pairs={{0,4},{4,0},{8,12},{12,8},{16,20},{20,16},{24,28},{28,24},{1,5},{5... | collective-permute-start | bytes 638984 | tf_op jit(solution)/shard_map/ppermute | solution.py:655
  27.4 6.6 %copy-start.24 = (bf16[64,1664]{1,0:T(8,128)(2,1)}, bf16[64,1664]{1,0:T(8,128)(2,1)S(1)}, u32[]{:S(2)}) copy-start(bf16[64,1664]{1,0:T(8,128)(2,1)S(1)} %collective-permute-done.3.refs_1_) | copy-start | bytes 638980
  27.4 4.8 %collective-permute-start.7 = (bf16[64,1664]{1,0:T(8,128)(2,1)S(1)}, bf16[64,1664]{1,0:T(8,128)(2,1)}, u32[]{:S(2)}, u32[]{:S(2)}) collective-permute-start(bf16[64,1664]{1,0:T(8,128)(2,1)S(1)} %collective-permute-done.3.refs_1_), channel_id=1, source_target_pairs={{0,4},{4,0},{8,12},{12,8},{16,20},{20,16},{24,28},{28,24},{1,5},{5... | collective-permute-start | bytes 638984 | tf_op jit(solution)/shard_map/ppermute | solution.py:655
  29.2 4.8 %copy-start.25 = (bf16[64,1664]{1,0:T(8,128)(2,1)}, bf16[64,1664]{1,0:T(8,128)(2,1)S(1)}, u32[]{:S(2)}) copy-start(bf16[64,1664]{1,0:T(8,128)(2,1)S(1)} %collective-permute-done.4.refs_2_) | copy-start | bytes 638980
  29.2 4.1 %collective-permute-start.8 = (bf16[64,1664]{1,0:T(8,128)(2,1)S(1)}, bf16[64,1664]{1,0:T(8,128)(2,1)S(1)}, u32[]{:S(2)}, u32[]{:S(2)}) collective-permute-start(bf16[64,1664]{1,0:T(8,128)(2,1)S(1)} %collective-permute-done.4.refs_2_), channel_id=1, source_target_pairs={{0,4},{4,0},{8,12},{12,8},{16,20},{20,16},{24,28},{28,24},{1,5},{5... | collective-permute-start | bytes 638984 | tf_op jit(solution)/shard_map/ppermute | solution.py:655
  29.2 4.8 %copy-start.26 = (bf16[64,1664]{1,0:T(8,128)(2,1)}, bf16[64,1664]{1,0:T(8,128)(2,1)S(1)}, u32[]{:S(2)}) copy-start(bf16[64,1664]{1,0:T(8,128)(2,1)S(1)} %collective-permute-done.5.refs_3_) | copy-start | bytes 638980
  29.2 4.8 %collective-permute-start.9 = (bf16[64,1664]{1,0:T(8,128)(2,1)S(1)}, bf16[64,1664]{1,0:T(8,128)(2,1)}, u32[]{:S(2)}, u32[]{:S(2)}) collective-permute-start(bf16[64,1664]{1,0:T(8,128)(2,1)S(1)} %collective-permute-done.5.refs_3_), channel_id=1, source_target_pairs={{0,4},{4,0},{8,12},{12,8},{16,20},{20,16},{24,28},{28,24},{1,5},{5... | collective-permute-start | bytes 638984 | tf_op jit(solution)/shard_map/ppermute | solution.py:655
  29.7 12.7 %copy-start.17 = (bf16[64,5632]{1,0:T(8,128)(2,1)}, bf16[64,5632]{1,0:T(8,128)(2,1)S(1)}, u32[]{:S(2)}) copy-start(bf16[64,5632]{1,0:T(8,128)(2,1)S(1)} %constant_dynamic-update-slice_fusion.4.refs_0_) | copy-start | bytes 2162692
  29.7 38.8 %collective-permute-start.13 = (bf16[64,5632]{1,0:T(8,128)(2,1)S(1)}, bf16[64,5632]{1,0:T(8,128)(2,1)S(1)}, u32[]{:S(2)}, u32[]{:S(2)}) collective-permute-start(bf16[64,5632]{1,0:T(8,128)(2,1)S(1)} %constant_dynamic-update-slice_fusion.4.refs_0_), channel_id=1, source_target_pairs={{0,8},{4,12},{8,0},{12,4},{16,24},{20,28},{24,16},{28,20},{1,9},{5... | collective-permute-start | bytes 2162696 | tf_op jit(solution)/shard_map/ppermute | solution.py:655
  30.2 38.4 %collective-permute-start.14 = (bf16[64,5632]{1,0:T(8,128)(2,1)S(1)}, bf16[64,5632]{1,0:T(8,128)(2,1)S(1)}, u32[]{:S(2)}, u32[]{:S(2)}) collective-permute-start(bf16[64,5632]{1,0:T(8,128)(2,1)S(1)} %constant_dynamic-update-slice_fusion.4.refs_0_), channel_id=1, source_target_pairs={{0,16},{4,20},{8,24},{12,28},{16,0},{20,4},{24,8},{28,12},{1,17},{... | collective-permute-start | bytes 2162696 | tf_op jit(solution)/shard_map/ppermute | solution.py:655
  32.2 36.4 %collective-permute-start.15 = (bf16[64,5632]{1,0:T(8,128)(2,1)S(1)}, bf16[64,5632]{1,0:T(8,128)(2,1)S(1)}, u32[]{:S(2)}, u32[]{:S(2)}) collective-permute-start(bf16[64,5632]{1,0:T(8,128)(2,1)S(1)} %constant_dynamic-update-slice_fusion.4.refs_0_), channel_id=1, source_target_pairs={{0,24},{4,28},{8,16},{12,20},{16,8},{20,12},{24,0},{28,4},{1,25},{... | collective-permute-start | bytes 2162696 | tf_op jit(solution)/shard_map/ppermute | solution.py:655
  33.3 0.7 copy-start.27
  34.0 37.0 %collective-permute-start.16 = (bf16[64,5632]{1,0:T(8,128)(2,1)S(1)}, bf16[64,5632]{1,0:T(8,128)(2,1)}, u32[]{:S(2)}, u32[]{:S(2)}) collective-permute-start(bf16[64,5632]{1,0:T(8,128)(2,1)S(1)} %constant_dynamic-update-slice_fusion.4.refs_0_), channel_id=1, source_target_pairs={{0,4},{4,0},{8,12},{12,8},{16,20},{20,16},{24,28},{28,24},{1,5},{5... | collective-permute-start | bytes 2162696 | tf_op jit(solution)/shard_map/ppermute | solution.py:655
  68.5 0.9 copy-start.5
  68.5 1.1 copy-start.6
  68.6 1.4 copy-start.7
  70.0 2.5 %collective-permute-start.17 = (bf16[64,5632]{1,0:T(8,128)(2,1)}, bf16[64,5632]{1,0:T(8,128)(2,1)S(1)}, u32[]{:S(2)}, u32[]{:S(2)}) collective-permute-start(bf16[64,5632]{1,0:T(8,128)(2,1)} %get-tuple-element.78.refs_1_), channel_id=1, source_target_pairs={{0,4},{4,0},{8,12},{12,8},{16,20},{20,16},{24,28},{28,24},{1,5},{5... | collective-permute-start | bytes 2162696 | tf_op jit(solution)/shard_map/ppermute | solution.py:655
  70.5 3.1 %collective-permute-start.18 = (bf16[64,5632]{1,0:T(8,128)(2,1)}, bf16[64,5632]{1,0:T(8,128)(2,1)S(1)}, u32[]{:S(2)}, u32[]{:S(2)}) collective-permute-start(bf16[64,5632]{1,0:T(8,128)(2,1)} %get-tuple-element.79.refs_2_), channel_id=1, source_target_pairs={{0,4},{4,0},{8,12},{12,8},{16,20},{20,16},{24,28},{28,24},{1,5},{5... | collective-permute-start | bytes 2162696 | tf_op jit(solution)/shard_map/ppermute | solution.py:655
  70.5 4.1 %collective-permute-start.19 = (bf16[64,5632]{1,0:T(8,128)(2,1)}, bf16[64,5632]{1,0:T(8,128)(2,1)S(1)}, u32[]{:S(2)}, u32[]{:S(2)}) collective-permute-start(bf16[64,5632]{1,0:T(8,128)(2,1)} %get-tuple-element.80.refs_3_), channel_id=1, source_target_pairs={{0,4},{4,0},{8,12},{12,8},{16,20},{20,16},{24,28},{28,24},{1,5},{5... | collective-permute-start | bytes 2162696 | tf_op jit(solution)/shard_map/ppermute | solution.py:655
  72.5 2.1 copy-start.21
  73.5 1.0 copy-start.22
  74.5 0.9 copy-start.23
  120.0 5.8 %collective-permute-start.20 = (bf16[16,16,6016]{2,1,0:T(8,128)(2,1)}, bf16[16,16,6016]{2,1,0:T(8,128)(2,1)S(1)}, u32[]{:S(2)}, u32[]{:S(2)}) collective-permute-start(bf16[16,16,6016]{2,1,0:T(8,128)(2,1)} %get-tuple-element.93), channel_id=1, source_target_pairs={{0,4},{4,0},{8,12},{12,8},{16,20},{20,16},{24,28},{28,24},{1,5},{5... | collective-permute-start | bytes 9240584 | tf_op jit(solution)/shard_map/ppermute | solution.py:655
  125.9 1.6 copy-start
  132.4 42.5 %collective-permute-start.21 = (bf16[4,16,6016]{2,1,0:T(8,128)(2,1)}, bf16[4,16,6016]{2,1,0:T(8,128)(2,1)S(1)}, u32[]{:S(2)}, u32[]{:S(2)}) collective-permute-start(bf16[4,16,6016]{2,1,0:T(8,128)(2,1)} %get-tuple-element.100), channel_id=1, source_target_pairs={{0,8},{4,12},{8,0},{12,4},{16,24},{20,28},{24,16},{28,20},{1,9},{5... | collective-permute-start | bytes 2310152 | tf_op jit(solution)/shard_map/ppermute | solution.py:655
  132.9 42.1 %collective-permute-start.22 = (bf16[4,16,6016]{2,1,0:T(8,128)(2,1)}, bf16[4,16,6016]{2,1,0:T(8,128)(2,1)S(1)}, u32[]{:S(2)}, u32[]{:S(2)}) collective-permute-start(bf16[4,16,6016]{2,1,0:T(8,128)(2,1)} %get-tuple-element.101), channel_id=1, source_target_pairs={{0,16},{4,20},{8,24},{12,28},{16,0},{20,4},{24,8},{28,12},{1,17},{... | collective-permute-start | bytes 2310152 | tf_op jit(solution)/shard_map/ppermute | solution.py:655
  134.8 40.1 %collective-permute-start.23 = (bf16[4,16,6016]{2,1,0:T(8,128)(2,1)}, bf16[4,16,6016]{2,1,0:T(8,128)(2,1)S(1)}, u32[]{:S(2)}, u32[]{:S(2)}) collective-permute-start(bf16[4,16,6016]{2,1,0:T(8,128)(2,1)} %get-tuple-element.102), channel_id=1, source_target_pairs={{0,24},{4,28},{8,16},{12,20},{16,8},{20,12},{24,0},{28,4},{1,25},{... | collective-permute-start | bytes 2310152 | tf_op jit(solution)/shard_map/ppermute | solution.py:655
  174.9 0.9 copy-start.1
  175.0 1.1 copy-start.2
  175.0 1.4 copy-start.3
  176.3 3.1 %collective-permute-start.24 = (bf16[16,16,1536]{2,1,0:T(8,128)(2,1)}, bf16[16,16,1536]{2,1,0:T(8,128)(2,1)S(1)}, u32[]{:S(2)}, u32[]{:S(2)}) collective-permute-start(bf16[16,16,1536]{2,1,0:T(8,128)(2,1)} %hold.3.refs_4_), channel_id=1, source_target_pairs={{0,4},{4,0},{8,12},{12,8},{16,20},{20,16},{24,28},{28,24},{1,5},{5... | collective-permute-start | bytes 2359304 | tf_op jit(solution)/shard_map/ppermute | solution.py:655
  179.4 3.4 %copy-start.30 = (bf16[1,16,6016]{2,1,0:T(8,128)(2,1)S(1)}, bf16[1,16,6016]{2,1,0:T(8,128)(2,1)}, u32[]{:S(2)}) copy-start(bf16[1,16,6016]{2,1,0:T(8,128)(2,1)} %get-tuple-element.112) | copy-start | bytes 577540
  179.4 5.2 %copy-start.29 = (bf16[1,16,6016]{2,1,0:T(8,128)(2,1)S(1)}, bf16[1,16,6016]{2,1,0:T(8,128)(2,1)}, u32[]{:S(2)}) copy-start(bf16[1,16,6016]{2,1,0:T(8,128)(2,1)} %get-tuple-element.113) | copy-start | bytes 577540
  179.4 7.7 %copy-start.28 = (bf16[1,16,6016]{2,1,0:T(8,128)(2,1)S(1)}, bf16[1,16,6016]{2,1,0:T(8,128)(2,1)}, u32[]{:S(2)}) copy-start(bf16[1,16,6016]{2,1,0:T(8,128)(2,1)} %get-tuple-element.114) | copy-start | bytes 577540
  179.4 0.9 copy-start.4
  182.7 7.5 %collective-permute-start.25 = (bf16[4,16,1536]{2,1,0:T(8,128)(2,1)}, bf16[4,16,1536]{2,1,0:T(8,128)(2,1)S(1)}, u32[]{:S(2)}, u32[]{:S(2)}) collective-permute-start(bf16[4,16,1536]{2,1,0:T(8,128)(2,1)} %get-tuple-element.105), channel_id=1, source_target_pairs={{0,8},{4,12},{8,0},{12,4},{16,24},{20,28},{24,16},{28,20},{1,9},{5... | collective-permute-start | bytes 589832 | tf_op jit(solution)/shard_map/ppermute | solution.py:655
  182.8 25.3 %collective-permute-start.31 = (bf16[1,16,6016]{2,1,0:T(8,128)(2,1)S(1)}, bf16[1,16,6016]{2,1,0:T(8,128)(2,1)S(1)}, u32[]{:S(2)}, u32[]{:S(2)}) collective-permute-start(bf16[1,16,6016]{2,1,0:T(8,128)(2,1)S(1)} %copy-done.30), channel_id=1, source_target_pairs={{0,1},{1,0},{2,3},{3,2},{4,5},{5,4},{6,7},{7,6},{8,9},{9,8},{10,11... | collective-permute-start | bytes 577544 | tf_op jit(solution)/shard_map/ppermute | solution.py:655
  184.6 24.6 %collective-permute-start.32 = (bf16[1,16,6016]{2,1,0:T(8,128)(2,1)S(1)}, bf16[1,16,6016]{2,1,0:T(8,128)(2,1)S(1)}, u32[]{:S(2)}, u32[]{:S(2)}) collective-permute-start(bf16[1,16,6016]{2,1,0:T(8,128)(2,1)S(1)} %copy-done.29), channel_id=1, source_target_pairs={{0,2},{1,3},{2,0},{3,1},{4,6},{5,7},{6,4},{7,5},{8,10},{9,11},{10,... | collective-permute-start | bytes 577544 | tf_op jit(solution)/shard_map/ppermute | solution.py:655
  187.1 22.1 %collective-permute-start.33 = (bf16[1,16,6016]{2,1,0:T(8,128)(2,1)S(1)}, bf16[1,16,6016]{2,1,0:T(8,128)(2,1)S(1)}, u32[]{:S(2)}, u32[]{:S(2)}) collective-permute-start(bf16[1,16,6016]{2,1,0:T(8,128)(2,1)S(1)} %copy-done.28), channel_id=1, source_target_pairs={{0,3},{1,2},{2,1},{3,0},{4,7},{5,6},{6,5},{7,4},{8,11},{9,10},{10,... | collective-permute-start | bytes 577544 | tf_op jit(solution)/shard_map/ppermute | solution.py:655
  187.2 14.3 %collective-permute-start.26 = (bf16[4,16,1536]{2,1,0:T(8,128)(2,1)}, bf16[4,16,1536]{2,1,0:T(8,128)(2,1)S(1)}, u32[]{:S(2)}, u32[]{:S(2)}) collective-permute-start(bf16[4,16,1536]{2,1,0:T(8,128)(2,1)} %get-tuple-element.106), channel_id=1, source_target_pairs={{0,16},{4,20},{8,24},{12,28},{16,0},{20,4},{24,8},{28,12},{1,17},{... | collective-permute-start | bytes 589832 | tf_op jit(solution)/shard_map/ppermute | solution.py:655
  190.2 11.3 %copy-start.8 = (bf16[4,16,1536]{2,1,0:T(8,128)(2,1)}, bf16[4,16,1536]{2,1,0:T(8,128)(2,1)S(1)}, u32[]{:S(2)}) copy-start(bf16[4,16,1536]{2,1,0:T(8,128)(2,1)S(1)} %collective-permute-done.25.refs_1_) | copy-start | bytes 589828
  190.2 11.3 %collective-permute-start.27 = (bf16[4,16,1536]{2,1,0:T(8,128)(2,1)}, bf16[4,16,1536]{2,1,0:T(8,128)(2,1)S(1)}, u32[]{:S(2)}, u32[]{:S(2)}) collective-permute-start(bf16[4,16,1536]{2,1,0:T(8,128)(2,1)} %get-tuple-element.107), channel_id=1, source_target_pairs={{0,24},{4,28},{8,16},{12,20},{16,8},{20,12},{24,0},{28,4},{1,25},{... | collective-permute-start | bytes 589832 | tf_op jit(solution)/shard_map/ppermute | solution.py:655
  201.5 0.7 copy-start.9
  202.2 0.7 copy-start.10
  204.8 6.2 %collective-permute-start.30 = (bf16[1,16,1536]{2,1,0:T(8,128)(2,1)}, bf16[1,16,1536]{2,1,0:T(8,128)(2,1)S(1)}, u32[]{:S(2)}, u32[]{:S(2)}) collective-permute-start(bf16[1,16,1536]{2,1,0:T(8,128)(2,1)} %get-tuple-element.111), channel_id=1, source_target_pairs={{0,3},{1,2},{2,1},{3,0},{4,7},{5,6},{6,5},{7,4},{8,11},{9,10},{10,... | collective-permute-start | bytes 147464 | tf_op jit(solution)/shard_map/ppermute | solution.py:655
  208.1 4.3 %collective-permute-start.28 = (bf16[1,16,1536]{2,1,0:T(8,128)(2,1)}, bf16[1,16,1536]{2,1,0:T(8,128)(2,1)S(1)}, u32[]{:S(2)}, u32[]{:S(2)}) collective-permute-start(bf16[1,16,1536]{2,1,0:T(8,128)(2,1)} %get-tuple-element.109), channel_id=1, source_target_pairs={{0,1},{1,0},{2,3},{3,2},{4,5},{5,4},{6,7},{7,6},{8,9},{9,8},{10,11... | collective-permute-start | bytes 147464 | tf_op jit(solution)/shard_map/ppermute | solution.py:655
  208.1 5.3 %copy-start.11 = (bf16[1,16,6016]{2,1,0:T(8,128)(2,1)}, bf16[1,16,6016]{2,1,0:T(8,128)(2,1)S(1)}, u32[]{:S(2)}) copy-start(bf16[1,16,6016]{2,1,0:T(8,128)(2,1)S(1)} %collective-permute-done.31) | copy-start | bytes 577540
  208.2 5.3 %collective-permute-start.29 = (bf16[1,16,1536]{2,1,0:T(8,128)(2,1)}, bf16[1,16,1536]{2,1,0:T(8,128)(2,1)S(1)}, u32[]{:S(2)}, u32[]{:S(2)}) collective-permute-start(bf16[1,16,1536]{2,1,0:T(8,128)(2,1)} %get-tuple-element.110), channel_id=1, source_target_pairs={{0,2},{1,3},{2,0},{3,1},{4,6},{5,7},{6,4},{7,5},{8,10},{9,11},{10,... | collective-permute-start | bytes 147464 | tf_op jit(solution)/shard_map/ppermute | solution.py:655
  209.2 4.2 %copy-start.12 = (bf16[1,16,6016]{2,1,0:T(8,128)(2,1)}, bf16[1,16,6016]{2,1,0:T(8,128)(2,1)S(1)}, u32[]{:S(2)}) copy-start(bf16[1,16,6016]{2,1,0:T(8,128)(2,1)S(1)} %collective-permute-done.32) | copy-start | bytes 577540
  209.2 4.2 %copy-start.13 = (bf16[1,16,6016]{2,1,0:T(8,128)(2,1)}, bf16[1,16,6016]{2,1,0:T(8,128)(2,1)S(1)}, u32[]{:S(2)}) copy-start(bf16[1,16,6016]{2,1,0:T(8,128)(2,1)S(1)} %collective-permute-done.33) | copy-start | bytes 577540
  211.0 2.4 %copy-start.14 = (bf16[1,16,1536]{2,1,0:T(8,128)(2,1)}, bf16[1,16,1536]{2,1,0:T(8,128)(2,1)S(1)}, u32[]{:S(2)}) copy-start(bf16[1,16,1536]{2,1,0:T(8,128)(2,1)S(1)} %collective-permute-done.30) | copy-start | bytes 147460
  212.4 1.0 copy-start.15
  214.0 5.3 %copy-start.19 = (bf16[16]{0:T(256)(128)(2,1)S(1)}, bf16[16]{0:T(256)(128)(2,1)}, u32[]{:S(2)}) copy-start(bf16[16]{0:T(256)(128)(2,1)} %param.26) | copy-start | bytes 100
  214.0 5.8 %copy-start.20 = (bf16[16]{0:T(256)(128)(2,1)S(1)}, bf16[16]{0:T(256)(128)(2,1)}, u32[]{:S(2)}) copy-start(bf16[16]{0:T(256)(128)(2,1)} %param.25) | copy-start | bytes 100
  (1 other events, 0.6 us)

commit v2 on v1

v2 whole, which is shorter than its diff:
```python
from functools import partial

import jax
import jax.numpy as jnp
from jax import lax
from jax.experimental import pallas as pl
from jax.experimental.pallas import tpu as pltpu
from jax.sharding import PartitionSpec as P

HEADS = 8
HEAD_DIM = 64
EPSILON = 1e-05
MASKED = -1000000000.0
AXES = ("wide", "narrow")
BF = jnp.bfloat16
F32 = jnp.float32
MIB = 1 << 20
VMEM = 60 * MIB
ANYWHERE = pl.BlockSpec(memory_space=pl.ANY)
BLOCK = 256
ROWS = 16
BLOCKS = 32
FIRST = 1536 + 128
TILES = 11
PARTS = 1


def dot(left, right):
    return jnp.dot(left, right, preferred_element_type=F32)


def dot_t(left, right):
    return lax.dot_general(left, right, (((1,), (1,)), ((), ())), preferred_element_type=F32)


def t_dot(left, right):
    return lax.dot_general(left, right, (((0,), (0,)), ((), ())), preferred_element_type=F32)


def row_mean(values):
    return jnp.mean(values, axis=-1, keepdims=True)


def normalise(values):
    offset = values - row_mean(values)
    scale = lax.rsqrt(row_mean(offset * offset) + EPSILON)
    return offset * scale, scale


def sigmoid(values):
    return 1.0 / (1.0 + jnp.exp(-values))


def project_kernel(
    order, tokens, *refs
):
    pieces, refs = refs[:8], refs[8:]
    normed, normed_t, query, key, value, key_t, value_t, weights, small, held, sem = refs
    step = pl.program_id(0)

    @pl.when(step == 0)
    def _():
        for at in range(BLOCKS):
            place = pl.multiple_of(order[at] * ROWS, ROWS)
            pltpu.make_async_copy(
                pieces[at // 4].at[pl.ds(at % 4 * ROWS, ROWS)], held.at[pl.ds(place, ROWS)], sem
            ).start()

    unit, _ = normalise(tokens[...].astype(F32))

    @pl.when(step == 0)
    def _():
        pltpu.make_async_copy(held, held, sem).wait()
        total = jnp.zeros((ROWS, 128), F32)
        for at in range(BLOCKS):
            total = total + held[pl.ds(at * ROWS, ROWS), 1536:FIRST].astype(F32)
        for vector in range(4):
            for part in range(4):
                small[vector : vector + 1, part * 128 : (part + 1) * 128] = total[
                    vector * 4 + part : vector * 4 + part + 1
                ]
        weights[...] = held[:, :1536]

    low = (unit * small[0:1, :]).astype(BF)
    normed[...] = low
    normed_t[...] = low.T
    query[...] = (dot(low, held[:, :512]).astype(BF).astype(F32) * HEAD_DIM**-0.5).astype(BF)
    keys = dot(low, held[:, 512:1024]).astype(BF)
    key[...] = keys
    key_t[...] = keys.T
    values = dot(low, held[:, 1024:1536]).astype(BF)
    value[...] = values
    value_t[...] = values.T


def project(order, tokens, pieces):
    length, width = tokens.shape
    tile = 512
    by_rows = pl.BlockSpec((tile, width), lambda i: (i, 0))
    by_columns = pl.BlockSpec((width, tile), lambda i: (0, i))
    whole = lambda *shape: pl.BlockSpec(shape, lambda i: (0,) * len(shape))
    rows = jax.ShapeDtypeStruct((length, width), BF)
    columns = jax.ShapeDtypeStruct((width, length), BF)
    return pl.pallas_call(
        project_kernel,
        grid=(length // tile,),
        in_specs=[
            pl.BlockSpec(memory_space=pltpu.SMEM),
            by_rows,
        ] + [pl.BlockSpec(memory_space=pl.ANY)] * 8,
        out_specs=[
            by_rows, by_columns, by_rows, by_rows, by_rows, by_columns, by_columns,
            whole(width, 1536), whole(4, width),
        ],
        out_shape=[
            rows, columns, rows, rows, rows, columns, columns,
            jax.ShapeDtypeStruct((width, 1536), BF),
            jax.ShapeDtypeStruct((4, width), F32),
        ],
        scratch_shapes=[pltpu.VMEM((width, FIRST), BF), pltpu.SemaphoreType.DMA],
        compiler_params=pltpu.CompilerParams(vmem_limit_bytes=VMEM),
        cost_estimate=pl.CostEstimate(
            flops=6 * length * width * width, bytes_accessed=12 * MIB, transcendentals=length
        ),
        name="project",
    )(order, tokens, *pieces)


def bias_of(segment_row, key_block, query_block):
    key_at = key_block * BLOCK + lax.broadcasted_iota(jnp.int32, (BLOCK, BLOCK), 0)
    query_at = query_block * BLOCK + lax.broadcasted_iota(jnp.int32, (BLOCK, BLOCK), 1)
    return jnp.where((key_at >= segment_row) & (key_at <= query_at), 0.0, MASKED)


def keep_heads(source, target):
    for head in range(target.shape[0]):
        target[head, :, pl.ds(head % 2 * HEAD_DIM, HEAD_DIM)] = source[:, pl.ds(head * HEAD_DIM, HEAD_DIM)]


def attend_kernel(
    segment, segment_row, query_in, key_in, value_t_in, mixed_out, log_total,
    query, key, value_t, mixed, masked_query, peak, total, mix, in_sems, out_sems,
):
    length, width = query.shape
    steps = length // BLOCK
    heads = range(HEADS)

    def loads(step):
        part = pl.ds(pl.multiple_of(step * BLOCK, BLOCK), BLOCK)
        return [
            pltpu.make_async_copy(query_in.at[part], query.at[part], in_sems.at[0, step]),
            pltpu.make_async_copy(key_in.at[part], key.at[part], in_sems.at[1, step]),
            pltpu.make_async_copy(value_t_in.at[:, part], value_t.at[:, part], in_sems.at[2, step]),
        ]

    def store(step):
        part = pl.ds(pl.multiple_of(step * BLOCK, BLOCK), BLOCK)
        return pltpu.make_async_copy(mixed.at[part], mixed_out.at[part], out_sems.at[step])

    for step in range(steps):
        for copy in loads(step):
            copy.start()
    masked_query[...] = jnp.zeros(masked_query.shape, BF)
    pair = lambda head: pl.ds(head // 2 * 128, 128)
    own = lambda head: pl.ds(head * HEAD_DIM, HEAD_DIM)

    def of_queries(step, _):
        for copy in loads(step):
            copy.wait()
        here = pl.ds(pl.multiple_of(step * BLOCK, BLOCK), BLOCK)
        keep_heads(query.at[here], masked_query)
        peak[...] = jnp.full(peak.shape, -1e30, F32)
        total[...] = jnp.zeros(total.shape, F32)
        mix[...] = jnp.zeros(mix.shape, F32)
        seen = segment_row[:, here]

        def visit(block, _):
            bias = bias_of(seen, block, step)
            rows = pl.ds(pl.multiple_of(block * BLOCK, BLOCK), BLOCK)
            scores = [dot_t(key[rows, pair(h)], masked_query[h]) + bias for h in heads]
            old = [peak[h : h + 1, :] for h in heads]
            new = [jnp.maximum(o, jnp.max(s, axis=0, keepdims=True)) for o, s in zip(old, scores)]
            power = [jnp.exp(s - n) for s, n in zip(scores, new)]
            fade = [jnp.exp(o - n) for o, n in zip(old, new)]
            added = [jnp.sum(p, axis=0, keepdims=True) for p in power]
            high = [p.astype(BF) for p in power]
            rest = [(p - x.astype(F32)).astype(BF) for p, x in zip(power, high)]
            mixes = [
                mix[own(h), :] * fade[h] + dot(value_t[own(h), rows], high[h]) + dot(value_t[own(h), rows], rest[h])
                for h in heads
            ]
            for h in heads:
                peak[h : h + 1, :] = new[h]
                total[h : h + 1, :] = total[h : h + 1, :] * fade[h] + added[h]
                mix[own(h), :] = mixes[h]
            return 0

        first = lax.div(segment[step * BLOCK], BLOCK)
        lax.fori_loop(first, step + 1, visit, 0)
        log_total[:, here] = peak[...] + jnp.log(total[...])
        for head in heads:
            mix[own(head), :] = mix[own(head), :] / total[head : head + 1, :]
        mixed[here, :] = mix[...].T
        store(step).start()
        return 0

    lax.fori_loop(0, steps, of_queries, 0)
    for step in range(steps):
        store(step).wait()


def attend(segment, segment_row, query, key, value_t):
    length, width = query.shape
    steps = length // BLOCK
    smem = pl.BlockSpec(memory_space=pltpu.SMEM)
    vmem = pl.BlockSpec(memory_space=pltpu.VMEM)
    rows = pltpu.VMEM((length, width), BF)
    return pl.pallas_call(
        attend_kernel,
        in_specs=[smem, vmem, ANYWHERE, ANYWHERE, ANYWHERE],
        out_specs=[ANYWHERE, vmem],
        out_shape=[
            jax.ShapeDtypeStruct((length, width), F32),
            jax.ShapeDtypeStruct((HEADS, length), F32),
        ],
        scratch_shapes=[
            rows,
            rows,
            pltpu.VMEM((width, length), BF),
            pltpu.VMEM((length, width), F32),
            pltpu.VMEM((HEADS, BLOCK, 128), BF),
            pltpu.VMEM((HEADS, BLOCK), F32),
            pltpu.VMEM((HEADS, BLOCK), F32),
            pltpu.VMEM((width, BLOCK), F32),
            pltpu.SemaphoreType.DMA((3, steps)),
            pltpu.SemaphoreType.DMA((steps,)),
        ],
        compiler_params=pltpu.CompilerParams(vmem_limit_bytes=VMEM),
        cost_estimate=pl.CostEstimate(
            flops=8 * length * length * width, bytes_accessed=6 * MIB, transcendentals=4 * length * length
        ),
        name="attend",
    )(segment, segment_row, query, key, value_t)


def attend_back_kernel(
    me, segment, segment_row, query_in, key_in, value_in, key_t_in, grad_in, log_total, inner_sum, normed_t_in, _after,
    grad_query, grad_key, grad_value, send, keep,
    query, key, value, grad_mixed, key_t, normed_t,
    masked_query, masked_grad, query_sum, key_sum, value_sum, low_query, low_key, low_value, staged,
    in_sems, out_sems, sems,
):
    length, width = query.shape
    steps = length // BLOCK
    heads = range(HEADS)
    by_rows = ((query_in, query), (key_in, key), (value_in, value), (grad_in, grad_mixed))

    def loads(step):
        part = pl.ds(pl.multiple_of(step * BLOCK, BLOCK), BLOCK)
        copies = [
            pltpu.make_async_copy(source.at[part], target.at[part], in_sems.at[k, step])
            for k, (source, target) in enumerate(by_rows)
        ]
        return copies + [
            pltpu.make_async_copy(key_t_in.at[:, part], key_t.at[:, part], in_sems.at[4, step])
        ]

    for step in range(steps):
        for copy in loads(step):
            copy.start()
    last_load = pltpu.make_async_copy(normed_t_in, normed_t, out_sems.at[3])
    last_load.start()
    key_sum[...] = jnp.zeros(key_sum.shape, F32)
    value_sum[...] = jnp.zeros(value_sum.shape, F32)
    masked_query[...] = jnp.zeros(masked_query.shape, BF)
    masked_grad[...] = jnp.zeros(masked_grad.shape, BF)
    pair = lambda head: pl.ds(head // 2 * 128, 128)
    own = lambda head: pl.ds(head * HEAD_DIM, HEAD_DIM)

    def of_queries(step, _):
        for copy in loads(step):
            copy.wait()
        here = pl.ds(pl.multiple_of(step * BLOCK, BLOCK), BLOCK)
        keep_heads(query.at[here], masked_query)
        keep_heads(grad_mixed.at[here], masked_grad)
        query_sum[...] = jnp.zeros(query_sum.shape, F32)
        seen = segment_row[:, here]

        def visit(block, _):
            bias = bias_of(seen, block, step)
            rows = pl.ds(pl.multiple_of(block * BLOCK, BLOCK), BLOCK)
            scores = [dot_t(key[rows, pair(h)], masked_query[h]) for h in heads]
            grad_probs = [dot_t(value[rows, pair(h)], masked_grad[h]) for h in heads]
            probs = [jnp.exp((scores[h] + bias) - log_total[h : h + 1, here]) for h in heads]
            grad_scores = [
                (probs[h] * (grad_probs[h] - inner_sum[h : h + 1, here])).astype(BF) for h in heads
            ]
            to_value = [dot(probs[h].astype(BF), masked_grad[h]) for h in heads]
            to_key = [dot(grad_scores[h], masked_query[h]) for h in heads]
            to_query = [dot(key_t[own(h), rows], grad_scores[h]) for h in heads]
            for h in heads[::2]:
                value_sum[rows, pair(h)] += to_value[h] + to_value[h + 1]
                key_sum[rows, pair(h)] += to_key[h] + to_key[h + 1]
            for h in heads:
                query_sum[own(h), :] += to_query[h]
            return 0

        first = lax.div(segment[step * BLOCK], BLOCK)
        lax.fori_loop(first, step + 1, visit, 0)
        low_query[here, :] = (query_sum[...] * HEAD_DIM**-0.5).astype(BF).T
        return 0

    lax.fori_loop(0, steps, of_queries, 0)
    low_key[...] = key_sum[...].astype(BF)
    low_value[...] = value_sum[...].astype(BF)
    results = ((low_query, grad_query), (low_key, grad_key), (low_value, grad_value))
    stores = [
        pltpu.make_async_copy(source, target, out_sems.at[k])
        for k, (source, target) in enumerate(results)
    ]
    for store in stores:
        store.start()
    last_load.wait()
    for k, (source, _) in enumerate(results):
        staged[:, k * width : (k + 1) * width] = dot(normed_t[...], source[...]).astype(BF)
    hand_out(
        me[0], lambda row: staged.at[pl.ds(row, ROWS)], lambda out, at: out.at[at], send, keep, sems
    )
    wait_out(send, keep, sems)
    for store in stores:
        store.wait()


def device_at(me, half, at):
    plane, line = at // 4, at % 4
    return jnp.bitwise_xor(me, (plane * 2 + half) * 4 + line)


def hand_out(me, source_at, target_at, send, keep, sems):
    for half, target in enumerate((keep, send)):
        for at in range(BLOCKS // 2):
            place = pl.multiple_of(device_at(me, half, at) * ROWS, ROWS)
            pltpu.make_async_copy(source_at(place), target_at(target, at), sems.at[half]).start()


def wait_out(send, keep, sems):
    for half, target in enumerate((keep, send)):
        pltpu.make_async_copy(target, target, sems.at[half]).wait()


def attend_back(
    me, segment, segment_row, query, key, value, key_t, grad_mixed, log_total, inner_sum, normed_t, after
):
    length, width = query.shape
    steps = length // BLOCK
    smem = pl.BlockSpec(memory_space=pltpu.SMEM)
    vmem = pl.BlockSpec(memory_space=pltpu.VMEM)
    flat = jax.ShapeDtypeStruct((length, width), BF)
    packet = jax.ShapeDtypeStruct((BLOCKS // 2, ROWS, 3 * width), BF)
    rows, columns = pltpu.VMEM((length, width), BF), pltpu.VMEM((width, length), BF)
    return pl.pallas_call(
        attend_back_kernel,
        in_specs=[smem, smem, vmem] + [ANYWHERE] * 5 + [vmem, vmem, ANYWHERE, ANYWHERE],
        out_specs=[ANYWHERE] * 5,
        out_shape=[flat, flat, flat, packet, packet],
        scratch_shapes=[rows] * 4 + [columns] * 2 + [
            pltpu.VMEM((HEADS, BLOCK, 128), BF),
            pltpu.VMEM((HEADS, BLOCK, 128), BF),
            pltpu.VMEM((width, BLOCK), F32),
            pltpu.VMEM((length, width), F32),
            pltpu.VMEM((length, width), F32),
        ] + [rows] * 3 + [
            pltpu.VMEM((width, 3 * width), BF),
            pltpu.SemaphoreType.DMA((5, steps)),
            pltpu.SemaphoreType.DMA((4,)),
            pltpu.SemaphoreType.DMA((2,)),
        ],
        compiler_params=pltpu.CompilerParams(vmem_limit_bytes=VMEM),
        cost_estimate=pl.CostEstimate(
            flops=20 * length * length * width, bytes_accessed=8 * MIB, transcendentals=4 * length * length
        ),
        name="attend_back",
    )(
        me, segment, segment_row, query, key, value, key_t, grad_mixed, log_total, inner_sum, normed_t, after
    )


def feed_kernel(
    me, order, tokens, normed, normed_t, mixed, out_grad, small, *refs
):
    pieces, refs = refs[:8], refs[8:]
    result, grad_middle, zeta_one_low, grad_mixed, inner_sum, gate_attn_out, send, keep, *refs = refs
    held, held_out, grads, staged, hidden, slope, sums, *refs = refs
    mix, second, grad_feed, zeta_two_low, grad_branch, grad_inner, sems, out_sems = refs
    step = pl.program_id(0)
    last = pl.num_programs(0) - 1
    features = tokens.shape[1]
    chunks = 4
    tile = lambda k: pl.ds(k * features, features)
    w_output, gate_attn, gate_ffn, *w_in = (held.at[:, tile(k)] for k in range(3 + chunks))
    w_out = [held_out.at[k] for k in range(chunks)]
    spans = (pl.ds(0, 3 * features), pl.ds(3 * features, chunks * features))

    @pl.when(step == 0)
    def _():
        for part in range(2 + chunks):
            for at in range(BLOCKS):
                place = pl.multiple_of(order[at] * ROWS, ROWS)
                source = pieces[at // 4].at[pl.ds(at % 4 * ROWS, ROWS)]
                here = pl.ds(place, ROWS)
                if part < 2:
                    copy = (source.at[:, spans[part]], held.at[here, spans[part]])
                else:
                    copy = (source.at[:, tile(3 + chunks + part - 2)], held_out.at[part - 2, here])
                pltpu.make_async_copy(*copy, sems.at[min(part, 2)]).start()
        sums[...] = jnp.zeros(sums.shape, F32)
        grads[...] = jnp.zeros(grads.shape, F32)
        pltpu.make_async_copy(held.at[:, spans[0]], held.at[:, spans[0]], sems.at[0]).wait()
        gate_attn_out[...] = gate_attn[...]

    gain, bias_one, bias_two = small[1:2, :], small[2:3, :], small[3:4, :]

    size = tokens.shape[0] // PARTS
    parts = range(PARTS)
    rows = [pl.ds(k * size, size) for k in parts]
    total = lambda vs: sum(jnp.sum(v, axis=0, keepdims=True) for v in vs)

    exact = [mixed[r, :] for r in rows]
    for k in parts:
        mix[rows[k], :] = exact[k].astype(BF)
    branch = [dot(mix[r, :], w_output[...]) for r in rows]
    gate_one = [sigmoid(dot(normed[r, :], gate_attn[...]) + bias_one) for r in rows]
    middle = [tokens[r, :].astype(F32) + g * b for r, g, b in zip(rows, gate_one, branch)]
    unit, scale = zip(*(normalise(m) for m in middle))
    for k in parts:
        second[rows[k], :] = (unit[k] * gain).astype(BF)
    gate_two = [sigmoid(dot(second[r, :], gate_ffn[...]) + bias_two) for r in rows]

    @pl.when(step == 0)
    def _():
        pltpu.make_async_copy(held.at[:, spans[1]], held.at[:, spans[1]], sems.at[1]).wait()
        pltpu.make_async_copy(held_out, held_out, sems.at[2]).wait()

    root = (2.0 / jnp.pi) ** 0.5
    feed = [jnp.zeros((size, features), F32) for _ in parts]
    for chunk in range(chunks):
        at = pl.ds(chunk * features, features)
        inner = [dot(second[r, :], w_in[chunk][...]) for r in rows]
        for k in parts:
            square = inner[k] * inner[k]
            turn = jnp.tanh(inner[k] * (root + (root * 0.044715) * square))
            rise = 0.5 + 0.5 * turn
            value = inner[k] * rise
            slope[rows[k], at] = rise + value * (1.0 - turn) * (
                root + (3.0 * root * 0.044715) * square
            )
            low = value.astype(BF)
            hidden[rows[k], at] = low
            feed[k] = feed[k] + dot(low, w_out[chunk][...])

    grad = [out_grad[r, :].astype(F32) for r in rows]
    zeta_two = []
    for k in parts:
        result[rows[k], :] = (middle[k] + gate_two[k] * feed[k]).astype(BF)
        gated = grad[k] * gate_two[k]
        grad_feed[rows[k], :] = gated.astype(BF)
        zeta_two.append(gated * feed[k] * (1.0 - gate_two[k]))
        zeta_two_low[rows[k], :] = zeta_two[k].astype(BF)
    second_t = second[...].T
    grad_second = [dot_t(zeta_two_low[r, :], gate_ffn[...]) for r in rows]
    grads[2] += dot(second_t, zeta_two_low[...])
    for chunk in range(chunks):
        at = pl.ds(chunk * features, features)
        for k in parts:
            grad_hidden = dot_t(grad_feed[rows[k], :], w_out[chunk][...])
            grad_inner[rows[k], :] = (slope[rows[k], at] * grad_hidden).astype(BF)
            grad_second[k] = grad_second[k] + dot_t(grad_inner[rows[k], :], w_in[chunk][...])
        grads[7 + chunk] += t_dot(hidden[:, at], grad_feed[...])
        grads[3 + chunk] += dot(second_t, grad_inner[...])

    @pl.when(step == last)
    def _():
        ready = pl.ds(2, TILES - 2)
        staged[ready] = grads[ready].astype(BF)
        hand_out(
            me[0], lambda row: staged.at[ready, pl.ds(row, ROWS)], lambda out, at: out.at[at, ready],
            send, keep, out_sems,
        )

    zeta_one = []
    for k in parts:
        grad_unit = grad_second[k] * gain
        grad_mid = grad[k] + scale[k] * (
            grad_unit - row_mean(grad_unit) - unit[k] * row_mean(grad_unit * unit[k])
        )
        grad_middle[rows[k], :] = grad_mid
        gated = grad_mid * gate_one[k]
        grad_branch[rows[k], :] = gated.astype(BF)
        zeta_one.append(gated * branch[k] * (1.0 - gate_one[k]))
        zeta_one_low[rows[k], :] = zeta_one[k].astype(BF)
    head_of = lax.broadcasted_iota(jnp.int32, (HEADS, features), 1) // HEAD_DIM
    own = (head_of == lax.broadcasted_iota(jnp.int32, (HEADS, features), 0)).astype(BF)
    for k in parts:
        back = dot_t(grad_branch[rows[k], :], w_output[...]).astype(BF)
        grad_mixed[rows[k], :] = back
        product = back.astype(F32) * exact[k]
        high = product.astype(BF)
        rest = (product - high.astype(F32)).astype(BF)
        inner_sum[:, rows[k]] = dot_t(own, high) + dot_t(own, rest)
    grads[0] += t_dot(mix[...], grad_branch[...])
    grads[1] += dot(normed_t[...], zeta_one_low[...])

    sums[0:1, :] += total(gate_one)
    sums[1:2, :] += total(g * g for g in gate_one)
    sums[2:3, :] += total(gate_two)
    sums[3:4, :] += total(g * g for g in gate_two)
    sums[4:5, :] += total(zeta_one)
    sums[5:6, :] += total(zeta_two)

    @pl.when(step == last)
    def _():
        sums_tile = write_sums(sums[0:6])
        for part, (first, count) in enumerate(((0, 2), (TILES, 1))):
            ready = pl.ds(first, count)
            if part == 0:
                staged[ready] = grads[ready].astype(BF)
            else:
                staged[TILES] = jnp.concatenate([sums_tile] * BLOCKS, axis=0)
            hand_out(
                me[0], lambda row: staged.at[ready, pl.ds(row, ROWS)], lambda out, at: out.at[at, ready],
                send, keep, out_sems,
            )
        wait_out(send, keep, out_sems)


def write_sums(sums):
    high = sums.astype(BF).astype(F32)
    rows = jnp.concatenate([high, sums - high, jnp.zeros((4, sums.shape[1]), F32)], axis=0)
    return rows.astype(BF)


def read_sums(tile):
    rows = tile.astype(F32)
    return rows[0:6] + rows[6:12]


def feed_forward(me, order, tokens, normed, normed_t, mixed, out_grad, small, pieces):
    length, width = tokens.shape
    hidden = 4 * width
    tile = 512
    by_rows = pl.BlockSpec((tile, width), lambda i: (i, 0))
    anywhere = pl.BlockSpec(memory_space=pl.ANY)
    rows = jax.ShapeDtypeStruct((length, width), BF)
    half = jax.ShapeDtypeStruct((BLOCKS // 2, TILES + 1, ROWS, width), BF)
    return pl.pallas_call(
        feed_kernel,
        grid=(length // tile,),
        in_specs=[
            pl.BlockSpec(memory_space=pltpu.SMEM),
            pl.BlockSpec(memory_space=pltpu.SMEM),
            by_rows, by_rows,
            pl.BlockSpec((width, tile), lambda i: (0, i)),
            by_rows, by_rows,
            pl.BlockSpec((4, width), lambda i: (0, 0)),
        ] + [anywhere] * 8,
        out_specs=[
            by_rows, by_rows, by_rows, by_rows,
            pl.BlockSpec((HEADS, tile), lambda i: (0, i)),
            pl.BlockSpec((width, width), lambda i: (0, 0)),
            anywhere, anywhere,
        ],
        out_shape=[
            rows,
            jax.ShapeDtypeStruct((length, width), F32),
            rows,
            rows,
            jax.ShapeDtypeStruct((HEADS, length), F32),
            jax.ShapeDtypeStruct((width, width), BF),
            half,
            half,
        ],
        scratch_shapes=[
            pltpu.VMEM((width, 7 * width), BF),
            pltpu.VMEM((4, width, width), BF),
            pltpu.VMEM((TILES, width, width), F32),
            pltpu.VMEM((TILES + 1, width, width), BF),
            pltpu.VMEM((tile, hidden), BF),
            pltpu.VMEM((tile, hidden), F32),
            pltpu.VMEM((8, width), F32),
        ] + [pltpu.VMEM((tile, width), BF)] * 6 + [
            pltpu.SemaphoreType.DMA((3,)),
            pltpu.SemaphoreType.DMA((2,)),
        ],
        compiler_params=pltpu.CompilerParams(vmem_limit_bytes=VMEM),
        cost_estimate=pl.CostEstimate(
            flops=6 * length * width * (3 * width + 2 * hidden), bytes_accessed=24 * MIB, transcendentals=length * hidden
        ),
        name="feed_forward",
    )(me, order, tokens, normed, normed_t, mixed, out_grad, small, *pieces)


def finish_kernel(tokens, zeta_one_low, grad_middle, weights, gate_attn, small, *refs):
    *grads, _after, token_grad, finished = refs
    finished[...] = jnp.zeros(finished.shape, F32)
    groups = len(grads) // 3
    width = tokens.shape[1]
    part = width // groups
    total = dot_t(zeta_one_low[...], gate_attn[...])
    for at, grad in enumerate(grads):
        which, group = at % 3, at // 3
        columns = pl.ds(which * width + group * part, part)
        total = total + dot_t(grad[...], weights[:, columns])
    unit, scale = normalise(tokens[...].astype(F32))
    grad_unit = total * small[0:1, :]
    token_grad[...] = grad_middle[...] + scale * (
        grad_unit - row_mean(grad_unit) - unit * row_mean(grad_unit * unit)
    )


def finish(tokens, zeta_one_low, grad_middle, weights, gate_attn, small, grads, after):
    length, width = tokens.shape
    tile = 512
    by_rows = pl.BlockSpec((tile, width), lambda i: (i, 0))
    return pl.pallas_call(
        finish_kernel,
        grid=(length // tile,),
        in_specs=[
            by_rows, by_rows, by_rows,
            pl.BlockSpec((width, 3 * width), lambda i: (0, 0)),
            pl.BlockSpec((width, width), lambda i: (0, 0)),
            pl.BlockSpec((4, width), lambda i: (0, 0)),
        ] + [pl.BlockSpec((tile, g.shape[1]), lambda i: (i, 0)) for g in grads]
        + [pl.BlockSpec(memory_space=pl.ANY)],
        out_specs=[by_rows, pl.BlockSpec((8, 128), lambda i: (0, 0))],
        out_shape=[
            jax.ShapeDtypeStruct((length, width), F32),
            jax.ShapeDtypeStruct((8, 128), F32),
        ],
        compiler_params=pltpu.CompilerParams(vmem_limit_bytes=VMEM),
        cost_estimate=pl.CostEstimate(
            flops=8 * length * width * width, bytes_accessed=16 * MIB, transcendentals=length
        ),
        name="finish",
    )(tokens, zeta_one_low, grad_middle, weights, gate_attn, small, *grads, after)


def row_sum(weight, grad):
    return jnp.sum(weight.astype(F32) * grad, axis=1, keepdims=True)


def in_order(features):
    unit = lax.broadcasted_iota(jnp.int32, (features, features), 0)
    column = lax.broadcasted_iota(jnp.int32, (features, features), 1)
    group, inside = column // 128, column % 128
    return (unit == inside // ROWS * 64 + group * ROWS + inside % ROWS).astype(BF)


def close_kernel(device, query, key, value, gate_attn, gate_ffn, w_in, gain_one, gain_two, *refs):
    late, early, refs = refs[:4], refs[4:8], refs[9:]
    *square_grads, grad_in, grad_out, norm_one, norm_two, bias_one, bias_two, stats = refs
    grad_query, grad_key, grad_value, grad_output, grad_gate_attn, grad_gate_ffn = square_grads
    width = query.shape[1]
    tile = lambda k: sum(p[pl.ds(k * ROWS, ROWS), :].astype(F32) for p in early)
    total = jnp.zeros((ROWS, 1), F32)
    for k, (weight, out) in enumerate(((query, grad_query), (key, grad_key), (value, grad_value))):
        grad = sum(p[:, pl.ds(k * width, width)].astype(F32) for p in late)
        out[...] = grad
        total = total + row_sum(weight[...], grad)
    grad_output[...] = tile(0)
    grad = tile(1)
    grad_gate_attn[...] = grad
    total = total + row_sum(gate_attn[...], grad)
    grad = tile(2)
    grad_gate_ffn[...] = grad
    other = row_sum(gate_ffn[...], grad)
    order = in_order(width)
    tiles = [tile(3 + k) for k in range(4)]
    for part in range(4):
        columns = pl.ds(part * width, width)
        grad = jnp.concatenate([t[:, part * 128 : (part + 1) * 128] for t in tiles], axis=1)
        high = grad.astype(BF)
        grad = dot_t(high, order) + dot_t((grad - high.astype(F32)).astype(BF), order)
        grad_in[:, columns] = grad
        other = other + row_sum(w_in[:, columns], grad)
    for group in range(4):
        grad_out[pl.ds(group * ROWS, ROWS), :] = tile(7 + group)

    def as_row(column, gain):
        eye = lax.broadcasted_iota(jnp.int32, (ROWS, ROWS), 0) == lax.broadcasted_iota(
            jnp.int32, (ROWS, ROWS), 1
        )
        return jnp.sum(jnp.where(eye, column, 0.0), axis=0, keepdims=True) / gain

    norm_one[...] = as_row(total, gain_one[...].astype(F32)[None, :])
    norm_two[...] = as_row(other, gain_two[...].astype(F32)[None, :])
    summed = sum(read_sums(p[pl.ds(TILES * ROWS, ROWS), :]) for p in early)
    mean = summed / device[1].astype(F32)
    stats[0:1, :] = mean[0:1]
    stats[1:2, :] = mean[1:2] - mean[0:1] * mean[0:1]
    stats[2:3, :] = mean[2:3]
    stats[3:4, :] = mean[3:4] - mean[2:3] * mean[2:3]
    both = jnp.concatenate([summed[4:6], jnp.zeros((6, width), F32)], axis=0)
    moved = pltpu.roll(both, lax.rem(width - device[0] * ROWS, width), 1)
    bias_one[...] = moved[0:1, :ROWS]
    bias_two[...] = moved[1:2, :ROWS]


def close(device, query, key, value, gate_attn, gate_ffn, w_in, gain_one, gain_two, late, early, after):
    width, wide = query.shape[1], w_in.shape[1]
    vmem = pl.BlockSpec(memory_space=pltpu.VMEM)
    square = jax.ShapeDtypeStruct((ROWS, width), F32)
    vector = jax.ShapeDtypeStruct((1, ROWS), F32)
    outs = [square] * 6 + [
        jax.ShapeDtypeStruct((ROWS, wide), F32),
        jax.ShapeDtypeStruct((4 * ROWS, width), F32),
    ] + [vector] * 4 + [jax.ShapeDtypeStruct((4, width), F32)]
    whole = lambda array: pl.BlockSpec(array.shape, lambda i: (0,) * len(array.shape))
    return pl.pallas_call(
        close_kernel,
        grid=(1,),
        in_specs=[pl.BlockSpec(memory_space=pltpu.SMEM)]
        + [whole(a) for a in (query, key, value, gate_attn, gate_ffn, w_in)]
        + [vmem] * 10
        + [ANYWHERE],
        out_specs=[whole(a) for a in outs],
        out_shape=outs,
        compiler_params=pltpu.CompilerParams(vmem_limit_bytes=VMEM),
        name="close",
    )(device, query, key, value, gate_attn, gate_ffn, w_in, gain_one, gain_two, *late, *early, after)


def swap(values, axis, bits):
    count = lax.axis_size(axis)
    return lax.ppermute(values, axis, [(i, i ^ bits) for i in range(count)])


def gather_pieces(values):
    line = jnp.concatenate([values] + [swap(values, "narrow", k) for k in (1, 2, 3)])
    return [line] + [swap(line, "wide", 2 * k) for k in (1, 2, 3)]


def both_cores(near):
    return list(near) + [swap(piece, "wide", 1) for piece in near]


def hold_kernel(*refs):
    pass


def hold(arrays, after):
    count = len(arrays)
    return pl.pallas_call(
        hold_kernel,
        in_specs=[ANYWHERE] * (count + len(after)),
        out_specs=[ANYWHERE] * count,
        out_shape=[jax.ShapeDtypeStruct(a.shape, a.dtype) for a in arrays],
        input_output_aliases={k: k for k in range(count)},
        name="hold",
    )(*arrays, *after)


def add_kernel(own, *refs, terms, sums):
    arrived, targets, (held, sems) = refs[: terms - 1], refs[terms : terms + 4], refs[terms + 4 :]
    each, rows, _ = targets[0].shape
    copies = []
    for part in range(4):
        here = pl.ds(part * each, each)
        copies.append(pltpu.make_async_copy(own.at[here], held.at[here], sems.at[part]))
        copies[-1].start()
    tile = pl.ds(rows - ROWS, ROWS)
    for part, target in enumerate(targets):
        copies[part].wait()
        for block in range(each):
            at = part * each + block
            target[block] = sum((a[at].astype(F32) for a in arrived), held[at].astype(F32)).astype(BF)
        if sums and part == 0:
            added = write_sums(sum((read_sums(a[0, tile, :]) for a in arrived), read_sums(held[0, tile, :])))
        if sums:
            for block in range(each):
                target[block, tile, :] = added


def add_split(own, arrived, sums, limit, after):
    blocks, rows, columns = own.shape
    vmem = pl.BlockSpec(memory_space=pltpu.VMEM)
    return pl.pallas_call(
        partial(add_kernel, terms=1 + len(arrived), sums=sums),
        in_specs=[ANYWHERE] + [vmem] * len(arrived) + [ANYWHERE],
        out_specs=[vmem] * 4,
        out_shape=[jax.ShapeDtypeStruct((blocks // 4, rows, columns), BF)] * 4,
        scratch_shapes=[pltpu.VMEM(own.shape, BF), pltpu.SemaphoreType.DMA((4,))],
        compiler_params=pltpu.CompilerParams(vmem_limit_bytes=int(limit * MIB)),
        name="add_split",
    )(own, *arrived, after)


def add_core(send, keep, sums, limit, after):
    return add_split(keep, [swap(send, "wide", 1)], sums, limit, after)


def swap_plane(plane):
    return [swap(plane[k], "wide", 2 * k) for k in (1, 2, 3)]


def along_line(line):
    return [line[0][0]] + [swap(line[k], "narrow", k)[0] for k in (1, 2, 3)]


def natural(send, keep):
    halves = jnp.stack([keep, send]).reshape(2, 4, 4, *keep.shape[1:])
    return halves.swapaxes(0, 1).reshape(BLOCKS, *keep.shape[1:])


def pack_first(device, vectors, shards, first):
    own = vectors[0].shape[0]
    column, row = lax.rem(device[0] * own, 128), lax.div(device[0] * own, 128)
    at = 0
    for shard in shards:
        first[:, at : at + shard.shape[1]] = shard[...]
        at += shard.shape[1]
    values = jnp.concatenate([v[...].astype(F32)[None, :] for v in vectors], axis=0)
    wide = pltpu.roll(jnp.concatenate([values, jnp.zeros((4, 128 - own), F32)], axis=1), column, 1)
    place = lax.broadcasted_iota(jnp.int32, (ROWS, 128), 0)
    tile = jnp.zeros((ROWS, 128), F32)
    for vector in range(4):
        tile = jnp.where(place == vector * 4 + row, wide[vector : vector + 1], tile)
    first[:, at:] = tile.astype(BF)


def pack_kernel(device, *refs):
    vectors, shards, (first, rest) = refs[:4], refs[4:-2], refs[-2:]
    pack_first(device, vectors, shards[:3], first)
    pack_rest(*shards[3:], rest)


def pack_rest(w_output, gate_attn, gate_ffn, w_in, w_out, rest):
    width = w_output.shape[1]
    tile = lambda k: pl.ds(k * width, width)
    for k, shard in enumerate((w_output, gate_attn, gate_ffn)):
        rest[:, tile(k)] = shard[...]
    order = in_order(width)
    for part in range(4):
        moved = dot(w_in[:, tile(part)], order).astype(BF)
        for group in range(4):
            rest[:, pl.ds((3 + group) * width + part * 128, 128)] = moved[:, group * 128 : (group + 1) * 128]
    for group in range(4):
        rest[:, tile(7 + group)] = w_out[group * ROWS : (group + 1) * ROWS, :]


def pack(device, vectors, *shards):
    vmem = pl.BlockSpec(memory_space=pltpu.VMEM)
    return pl.pallas_call(
        pack_kernel,
        in_specs=[pl.BlockSpec(memory_space=pltpu.SMEM)] + [vmem] * (4 + len(shards)),
        out_shape=[
            jax.ShapeDtypeStruct((ROWS, FIRST), BF),
            jax.ShapeDtypeStruct((ROWS, TILES * shards[0].shape[1]), BF),
        ],
        compiler_params=pltpu.CompilerParams(vmem_limit_bytes=VMEM),
        name="pack",
    )(device, *vectors, *shards)


def per_device(
    tokens, segment, w_query, w_key, w_value, w_output, gate_attn, gate_ffn, w_in, w_out,
    norm_attn, norm_ffn, bias_attn, bias_ffn, out_grad,
):
    wide, narrow = lax.axis_size("wide"), lax.axis_size("narrow")
    devices = wide * narrow
    length, width = tokens.shape
    hidden = w_in.shape[1]
    own_rows = w_query.shape[0]
    device = lax.axis_index("wide") * narrow + lax.axis_index("narrow")
    direct = wide == 8 and narrow == 4 and own_rows == ROWS
    vectors = (norm_attn, norm_ffn, bias_attn, bias_ffn)

    def gather(values):
        return lax.all_gather(values, AXES, axis=0, tiled=True)

    if direct:
        me = device.astype(jnp.int32).reshape(1)
        first, rest = pack(
            me, vectors, w_query, w_key, w_value, w_output, gate_attn, gate_ffn, w_in, w_out
        )
        pieces = both_cores(gather_pieces(first))
        rest_near = gather_pieces(rest)
        order = jnp.concatenate(
            [
                jnp.bitwise_xor(device, (jnp.arange(16) // 4 * 2 + half) * 4 + jnp.arange(16) % 4)
                for half in range(2)
            ]
        ).astype(jnp.int32)
    else:
        full = gather(jnp.stack(vectors, axis=1))
        tile = jnp.zeros((BLOCKS, ROWS, 128), BF).at[0].set(full.T.reshape(ROWS, 128))
        first = jnp.concatenate(
            [gather(w_query), gather(w_key), gather(w_value), tile.reshape(BLOCKS * ROWS, 128)], axis=1
        ).reshape(8, 4 * ROWS, FIRST)
        squares = [gather(w).reshape(BLOCKS, 1, ROWS, width) for w in (w_output, gate_attn, gate_ffn)]
        in_tiles = gather(w_in).reshape(BLOCKS, ROWS, BLOCKS, 4, ROWS).transpose(0, 3, 1, 2, 4)
        packet = jnp.concatenate(
            squares + [in_tiles.reshape(BLOCKS, 4, ROWS, width), gather(w_out).reshape(BLOCKS, 4, ROWS, width)],
            axis=1,
        ).swapaxes(1, 2).reshape(8, 4 * ROWS, TILES * width)
        pieces = [first[k] for k in range(8)]
        rest_pieces = [packet[k] for k in range(8)]
        me = jnp.zeros((1,), jnp.int32)
        order = jnp.arange(BLOCKS, dtype=jnp.int32)

    segment_row = segment.reshape(1, length)
    normed, normed_t, query, key, value, key_t, value_t, weights, small = project(order, tokens, pieces)
    mixed, log_total = attend(segment, segment_row, query, key, value_t)
    if direct:
        rest_pieces = both_cores(rest_near[:1] + list(hold(rest_near[1:], [log_total])))
    result, grad_middle, zeta_one_low, grad_mixed, inner_sum, whole_gate, send, keep = feed_forward(
        me, order, tokens, normed, normed_t, mixed, out_grad, small, rest_pieces
    )
    if direct:
        flat = lambda values: values.reshape(BLOCKS // 2, (TILES + 1) * ROWS, width)
        plane = add_core(flat(send), flat(keep), True, 12, me)
    else:
        plane = [me]
    *grads, late_send, late_keep = attend_back(
        me, segment, segment_row, query, key, value, key_t, grad_mixed, log_total, inner_sum,
        normed_t, plane[0],
    )
    if direct:
        received = swap_plane(plane)
        (late_send,) = hold([late_send], received)
        line = add_split(plane[0], received, True, 12, me)
        late_plane = add_core(late_send, late_keep, False, 12, line[0])
    else:
        late_plane = [me]
    token_grad, finished = finish(
        tokens, zeta_one_low, grad_middle, weights, whole_gate, small, grads, late_plane[0]
    )

    counted = length * devices
    if direct:
        early = along_line(line)
        late = along_line(add_split(late_plane[0], swap_plane(late_plane), False, 12, finished))
        device_and_count = jnp.stack([device, jnp.int32(counted)]).astype(jnp.int32)
        *owned, norm_one, norm_two, bias_one, bias_two, stats = close(
            device_and_count, w_query, w_key, w_value, gate_attn, gate_ffn, w_in, norm_attn, norm_ffn, late, early, finished
        )
        small_grads = [v.reshape(own_rows) for v in (norm_one, norm_two, bias_one, bias_two)]
        return (result, token_grad, *owned, *small_grads, stats)

    def scatter(values):
        return lax.psum_scatter(values, AXES, scatter_dimension=0, tiled=True)

    tile = keep[0, TILES].astype(F32)
    summed = lax.psum(tile[:6] + tile[6:12], AXES)
    whole = natural(send, keep).astype(F32)
    first = scatter(natural(late_send, late_keep).astype(F32).reshape(width, 3 * width))
    owned = [first[:, k * width : (k + 1) * width] for k in range(3)]
    owned += [scatter(whole[:, k].reshape(width, width)) for k in range(3)]
    in_tiles = whole[:, 3:7].reshape(BLOCKS, 4, ROWS, BLOCKS, ROWS).transpose(0, 2, 3, 1, 4)
    owned += [scatter(in_tiles.reshape(width, hidden)), scatter(whole[:, 7:11].reshape(hidden, width))]
    shards = (w_query, w_key, w_value, gate_attn)
    norm_one = sum(row_sum(w, g)[:, 0] for w, g in zip(shards, owned[:3] + owned[4:5]))
    norm_two = (row_sum(gate_ffn, owned[5]) + row_sum(w_in, owned[6]))[:, 0]
    mean = summed[:4] / counted
    gate_stats = jnp.stack([mean[0], mean[1] - mean[0] * mean[0], mean[2], mean[3] - mean[2] * mean[2]])
    own = lax.dynamic_slice(summed, (4, device * own_rows), (2, own_rows))
    return (
        result, token_grad, *owned, norm_one / norm_attn.astype(F32), norm_two / norm_ffn.astype(F32),
        own[0], own[1], gate_stats,
    )


def solution(mesh):
    rows = P(AXES, None)
    flat = P(AXES)
    in_specs = (rows, flat) + (rows,) * 8 + (flat,) * 4 + (rows,)
    out_specs = (rows,) * 10 + (flat,) * 4 + (P(),)
    return jax.shard_map(
        per_device, mesh=mesh, in_specs=in_specs, out_specs=out_specs, check_vma=False
    )
```

time: 221 us -> 211 us (0.955)
  Pallas kernels: 144 us -> 133 us
  local copies, waits for them, and re-layouts: 14.2 us -> 17.4 us
  other arithmetic: 4.4 us -> 1.21 us
    pallas_call x9, Pallas kernels: 79.5 us -> 69 us  [the longest x1 34.7 us: attend_back(): pl.pallas_call(attend_back_kernel, in_specs=[smem, smem, vmem] + [ANYWHER...]
    unnamed x68 -> x74, local copies, waits for them, and re-layouts: 10.6 us -> 16.1 us
  transfers between devices with their start and end apart: 34 -> 34, of which waited for: 10 -> 9; matrix products, arithmetic and copies ran while one was open for 2% -> 2% of each run, Pallas kernels for 40% -> 38%
where the time goes in v2:
time: 211 us; the launch traced here: 210 us
  Pallas kernels  133 us (63%)
  starting transfers between devices  35.9 us (17%)
  waiting for transfers between devices  21.4 us (10%)
  local copies, waits for them, and re-layouts  17.4 us (8%)
    pallas_call x1, Pallas kernels, feed_forward(): pl.pallas_call(feed_kernel, grid=(length // tile,), in_specs=[pl.BlockSpe...  44 us
    ppermute x34, starting transfers between devices, swap(): return lax.ppermute(values, axis, [(i, i ^ bits) for i in range(count)])  35.9 us
    pallas_call x1, Pallas kernels, attend_back(): pl.pallas_call(attend_back_kernel, in_specs=[smem, smem, vmem] + [ANYWHER...  34.7 us
    pallas_call x1, Pallas kernels, attend(): pl.pallas_call(attend_kernel, in_specs=[smem, vmem, ANYWHERE, ANYWHERE, A...  25.8 us
    ppermute x34, waiting for transfers between devices, swap(): return lax.ppermute(values, axis, [(i, i ^ bits) for i in range(count)])  21.4 us
    unnamed x74, local copies, waits for them, and re-layouts  16.1 us
    pallas_call x1, Pallas kernels, finish(): pl.pallas_call(finish_kernel, grid=(length // tile,), in_specs=[by_rows,...  9.5 us
    pallas_call x1, Pallas kernels, project(): pl.pallas_call(project_kernel, grid=(length // tile,), in_specs=[pl.Block...  8.3 us
  transfers between devices with their start and end apart: 34, of which 9 were waited for; matrix products, arithmetic and copies ran while one was open for 2% of the time, Pallas kernels for 38%

profile of v2, /device:TPU:0, one launch (start us, length us, event | category | flops | bytes accessed | tf_op | source)
XLA Modules:
  0.0 210.1 jit_solution(10735480098649199481)
XLA Ops:
  0.7 2.1 pack.1
  2.8 3.0 %collective-permute-start = (bf16[16,1664]{1,0:T(8,128)(2,1)}, bf16[16,1664]{1,0:T(8,128)(2,1)S(1)}, u32[]{:S(2)}, u32[]{:S(2)}) collective-permute-start(bf16[16,1664]{1,0:T(8,128)(2,1)} %get-tuple-element.75), channel_id=1, source_target_pairs={{0,1},{1,0},{2,3},{3,2},{4,5},{5,4},{6,7},{7,6},{8,9},{9,8},{10,11... | collective-permute-start | bytes 159752 | tf_op jit(solution)/shard_map/ppermute | solution.py:734
  5.8 2.6 %collective-permute-start.1 = (bf16[16,1664]{1,0:T(8,128)(2,1)}, bf16[16,1664]{1,0:T(8,128)(2,1)S(1)}, u32[]{:S(2)}, u32[]{:S(2)}) collective-permute-start(bf16[16,1664]{1,0:T(8,128)(2,1)} %get-tuple-element.75), channel_id=1, source_target_pairs={{0,2},{1,3},{2,0},{3,1},{4,6},{5,7},{6,4},{7,5},{8,10},{9,11},{10,... | collective-permute-start | bytes 159752 | tf_op jit(solution)/shard_map/ppermute | solution.py:734
  8.4 0.9 collective-permute-start.10
  9.3 3.5 %collective-permute-start.11 = (bf16[16,5632]{1,0:T(8,128)(2,1)}, bf16[16,5632]{1,0:T(8,128)(2,1)S(1)}, u32[]{:S(2)}, u32[]{:S(2)}) collective-permute-start(bf16[16,5632]{1,0:T(8,128)(2,1)} %get-tuple-element.83), channel_id=1, source_target_pairs={{0,2},{1,3},{2,0},{3,1},{4,6},{5,7},{6,4},{7,5},{8,10},{9,11},{10,... | collective-permute-start | bytes 540680 | tf_op jit(solution)/shard_map/ppermute | solution.py:734
  12.8 0.8 constant_dynamic-update-slice_fusion.3
  13.6 0.9 constant_dynamic-update-slice_fusion.7
  14.5 0.6 pad_add_fusion.order
  15.1 1.3 reshape.55.segment_row
  16.5 1.8 collective-permute-start.3
  18.2 1.5 collective-permute-start.4
  19.8 1.9 collective-permute-start.5
  21.6 4.9 %collective-permute-done.11 = bf16[16,5632]{1,0:T(8,128)(2,1)S(1)} collective-permute-done((bf16[16,5632]{1,0:T(8,128)(2,1)}, bf16[16,5632]{1,0:T(8,128)(2,1)S(1)}, u32[]{:S(2)}, u32[]{:S(2)}) %collective-permute-start.11) | collective-permute-done | bytes 180256 | tf_op jit(solution)/shard_map/ppermute | solution.py:734
  26.5 0.6 collective-permute-start.7
  27.1 1.2 collective-permute-done.4.refs_2_
  28.3 0.5 collective-permute-start.9
  28.8 0.4 collective-permute-start.13
  29.3 2.0 collective-permute-start.14
  31.3 1.1 collective-permute-start.15
  32.4 0.7 copy-done.33
  33.1 8.3 %project.1 = (bf16[1536,512]{1,0:T(8,128)(2,1)}, bf16[512,1536]{1,0:T(8,128)(2,1)}, bf16[1536,512]{1,0:T(8,128)(2,1)}, bf16[1536,512]{1,0:T(8,128)(2,1)}, bf16[1...) custom-call(s32[32]{0:T(128)} %pad_add_fusion.order, ...), custom_call_target="tpu_custom_call" | custom-call | flops 2415919104 | bytes 12582912 | tf_op jit(solution)/shard_map/project/pallas_call | solution.py:104
  41.5 25.8 %attend.1 = (f32[1536,512]{1,0:T(8,128)}, f32[8,1536]{1,0:T(8,128)}) custom-call(s32[1536]{0:T(1024)} %segment.3, s32[1,1536]{1,0:T(1,128)} %reshape.55.segment_row, bf16[1536,512]{1,0:T(8,128)(2,1)} %get-tuple-element.78.query_in, bf16[1536,512]{1,0:T(8,128)(2,1)} %get-tuple-element.79.key_in, bf16[512,1536]{1,0:T(8,128)(2,1)} %get-tuple-element.80.value_t_in), custom_call_target="tpu_custom_call" | custom-call | flops 9663676416 | bytes 6291456 | tf_op jit(solution)/shard_map/attend/pallas_call | solution.py:218
  67.3 0.8 copy-done.15
  68.1 0.3 copy-done.16
  68.4 0.3 copy-done.17
  68.7 0.5 collective-permute-start.18
  69.2 1.9 collective-permute-done.17.refs_5_
  71.1 1.0 collective-permute-done.18.refs_6_
  72.2 1.0 collective-permute-done.19.refs_7_
  73.2 0.9 copy-done.28
  74.1 44.0 %feed_forward.1 = (bf16[1536,512]{1,0:T(8,128)(2,1)}, f32[1536,512]{1,0:T(8,128)}, bf16[1536,512]{1,0:T(8,128)(2,1)}, bf16[1536,512]{1,0:T(8,128)(2,1)}, f32[8,1...) custom-call(s32[1]{0:T(128)} %bitcast.device.me.refs_1_.refs_3_, ...), custom_call_target="tpu_custom_call" | custom-call | flops 26575110144 | bytes 25165824 | tf_op jit(solution)/shard_map/feed_forward/pallas_call | solution.py:555
  118.3 5.7 %collective-permute-done.20.refs_0_ = bf16[16,192,512]{2,1,0:T(8,128)(2,1)S(1)} collective-permute-done((bf16[16,192,512]{2,1,0:T(8,128)(2,1)}, bf16[16,192,512]{2,1,0:T(8,128)(2,1)S(1)}, u32[]{:S(2)}, u32[]{:S(2)}) %collective-permute-start.20) | collective-permute-done | bytes 3145760 | tf_op jit(solution)/shard_map/ppermute | solution.py:734
  124.0 1.9 copy-done
  125.9 2.2 %add_split.4 = (bf16[4,192,512]{2,1,0:T(8,128)(2,1)S(1)}, bf16[4,192,512]{2,1,0:T(8,128)(2,1)}, bf16[4,192,512]{2,1,0:T(8,128)(2,1)}, bf16[4,192,512]{2,1,0:T(8,128)(2,1)S(1)}) custom-call(bf16[16,192,512]{2,1,0:T(8,128)(2,1)S(1)} %bitcast.15, bf16[16,192,512]{2,1,0:T(8,128)(2,1)S(1)} %collective-permute-done.20.refs_0_, s32[1]{0:T(128)} %bitcast.device.me.refs_1_.refs_3_), custom_call_target="tpu_custom_call" | custom-call | tf_op jit(solution)/shard_map/add_split/pallas_call | solution.py:786
  128.1 0.9 copy-done.9
  129.0 2.5 %collective-permute-start.22 = (bf16[4,192,512]{2,1,0:T(8,128)(2,1)}, bf16[4,192,512]{2,1,0:T(8,128)(2,1)S(1)}, u32[]{:S(2)}, u32[]{:S(2)}) collective-permute-start(bf16[4,192,512]{2,1,0:T(8,128)(2,1)} %get-tuple-element.106), channel_id=1, source_target_pairs={{0,16},{4,20},{8,24},{12,28},{16,0},{20,4},{24,8},{28,12},{1,17},{... | collective-permute-start | bytes 2359304 | tf_op jit(solution)/shard_map/ppermute | solution.py:734
  131.5 1.0 collective-permute-start.23
  132.5 34.7 %attend_back.1 = (bf16[1536,512]{1,0:T(8,128)(2,1)}, bf16[1536,512]{1,0:T(8,128)(2,1)}, bf16[1536,512]{1,0:T(8,128)(2,1)}, bf16[16,16,1536]{2,1,0:T(8,128)(2,1)}, bf16[16,16,1536]{2,1,0:T(8,128)(2,1)}) custom-call(s32[1]{0:T(128)} %bitcast.device.me.refs_1_.refs_3_, s32[1536]{0:T(1024)} %segment.3, s32[1,1536]{1,0:T(1,128)} %reshape.55.segment_row, ...), custom_call_target="tpu_custom_call" | custom-call | flops 24159191040 | bytes 8388608 | tf_op jit(solution)/shard_map/attend_back/pallas_call | solution.py:361
  167.3 0.8 copy-done.1
  168.1 0.3 copy-done.3
  168.7 1.1 copy-done.10
  169.8 1.1 copy-done.2
  170.9 1.1 copy-done.4
  172.1 1.1 copy-done.6
  173.2 1.4 add_split.5
  174.6 1.2 add_split.6
  175.9 0.7 copy-done.11
  176.6 3.5 %collective-permute-start.33 = (bf16[1,192,512]{2,1,0:T(8,128)(2,1)S(1)}, bf16[1,192,512]{2,1,0:T(8,128)(2,1)S(1)}, u32[]{:S(2)}, u32[]{:S(2)}) collective-permute-start(bf16[1,192,512]{2,1,0:T(8,128)(2,1)S(1)} %get-tuple-element.121), channel_id=1, source_target_pairs={{0,3},{1,2},{2,1},{3,0},{4,7},{5,6},{6,5},{7,4},{8,11},{9,10},{10,... | collective-permute-start | bytes 589832 | tf_op jit(solution)/shard_map/ppermute | solution.py:734
  180.1 0.4 collective-permute-start.31
  180.5 0.5 collective-permute-start.32
  181.0 1.3 collective-permute-start.26
  182.3 0.5 collective-permute-done.25.refs_0_
  182.7 1.8 collective-permute-start.27
  184.6 9.5 %finish.1 = (f32[1536,512]{1,0:T(8,128)}, f32[8,128]{1,0:T(8,128)}) custom-call(bf16[1536,512]{1,0:T(8,128)(2,1)} %tokens.5, bf16[1536,512]{1,0:T(8,128)(2,1)} %get-tuple-element.89.zeta_one_low, f32[1536,512]{1,0:T(8,128)} %get-tuple-element.90.grad_middle, bf16[512,1536]{1,0:T(8,128)(2,1)} %get-tuple-element.91.weights, ...), custom_call_target="tpu_custom_call" | custom-call | flops 3221225472 | bytes 16777216 | tf_op jit(solution)/shard_map/finish/pallas_call | solution.py:624
  194.1 0.7 copy-done.14
  194.8 0.4 add_split.7
  195.2 0.6 copy-done.13
  195.8 0.5 collective-permute-start.28
  196.3 3.8 %collective-permute-start.29 = (bf16[1,16,1536]{2,1,0:T(8,128)(2,1)S(1)}, bf16[1,16,1536]{2,1,0:T(8,128)(2,1)S(1)}, u32[]{:S(2)}, u32[]{:S(2)}) collective-permute-start(bf16[1,16,1536]{2,1,0:T(8,128)(2,1)S(1)} %get-tuple-element.117), channel_id=1, source_target_pairs={{0,2},{1,3},{2,0},{3,1},{4,6},{5,7},{6,4},{7,5},{8,10},{9,11},{10,... | collective-permute-start | bytes 147464 | tf_op jit(solution)/shard_map/ppermute | solution.py:734
  200.2 0.6 pad_add_fusion.1.device
  200.9 1.9 collective-permute-done.29
  202.7 3.3 %collective-permute-done.30 = bf16[1,16,1536]{2,1,0:T(8,128)(2,1)S(1)} collective-permute-done((bf16[1,16,1536]{2,1,0:T(8,128)(2,1)S(1)}, bf16[1,16,1536]{2,1,0:T(8,128)(2,1)S(1)}, u32[]{:S(2)}, u32[]{:S(2)}) %collective-permute-start.30) | collective-permute-done | bytes 49184 | tf_op jit(solution)/shard_map/ppermute | solution.py:734
  206.0 0.6 copy-done.23
  206.6 3.3 %close.1 = (f32[16,512]{1,0:T(8,128)}, f32[16,512]{1,0:T(8,128)}, f32[16,512]{1,0:T(8,128)}, f32[16,512]{1,0:T(8,128)}, f32[16,512]{1,0:T(8,128)}, /*index=5*/f3...) custom-call(s32[2]{0:T(128)} %pad_add_fusion.1.device, ...), custom_call_target="tpu_custom_call" | custom-call | tf_op jit(solution)/shard_map/close/pallas_call | solution.py:718
  (97 shorter events, 0.9 us)
Async XLA Ops:
  2.8 13.6 %collective-permute-start = (bf16[16,1664]{1,0:T(8,128)(2,1)}, bf16[16,1664]{1,0:T(8,128)(2,1)S(1)}, u32[]{:S(2)}, u32[]{:S(2)}) collective-permute-start(bf16[16,1664]{1,0:T(8,128)(2,1)} %get-tuple-element.75), channel_id=1, source_target_pairs={{0,1},{1,0},{2,3},{3,2},{4,5},{5,4},{6,7},{7,6},{8,9},{9,8},{10,11... | collective-permute-start | bytes 159752 | tf_op jit(solution)/shard_map/ppermute | solution.py:734
  5.8 10.6 %collective-permute-start.1 = (bf16[16,1664]{1,0:T(8,128)(2,1)}, bf16[16,1664]{1,0:T(8,128)(2,1)S(1)}, u32[]{:S(2)}, u32[]{:S(2)}) collective-permute-start(bf16[16,1664]{1,0:T(8,128)(2,1)} %get-tuple-element.75), channel_id=1, source_target_pairs={{0,2},{1,3},{2,0},{3,1},{4,6},{5,7},{6,4},{7,5},{8,10},{9,11},{10,... | collective-permute-start | bytes 159752 | tf_op jit(solution)/shard_map/ppermute | solution.py:734
  8.4 8.1 %collective-permute-start.2 = (bf16[16,1664]{1,0:T(8,128)(2,1)}, bf16[16,1664]{1,0:T(8,128)(2,1)S(1)}, u32[]{:S(2)}, u32[]{:S(2)}) collective-permute-start(bf16[16,1664]{1,0:T(8,128)(2,1)} %get-tuple-element.75), channel_id=1, source_target_pairs={{0,3},{1,2},{2,1},{3,0},{4,7},{5,6},{6,5},{7,4},{8,11},{9,10},{10,... | collective-permute-start | bytes 159752 | tf_op jit(solution)/shard_map/ppermute | solution.py:734
  8.4 11.4 %collective-permute-start.10 = (bf16[16,5632]{1,0:T(8,128)(2,1)}, bf16[16,5632]{1,0:T(8,128)(2,1)S(1)}, u32[]{:S(2)}, u32[]{:S(2)}) collective-permute-start(bf16[16,5632]{1,0:T(8,128)(2,1)} %get-tuple-element.83), channel_id=1, source_target_pairs={{0,1},{1,0},{2,3},{3,2},{4,5},{5,4},{6,7},{7,6},{8,9},{9,8},{10,11... | collective-permute-start | bytes 540680 | tf_op jit(solution)/shard_map/ppermute | solution.py:734
  9.3 17.2 %collective-permute-start.11 = (bf16[16,5632]{1,0:T(8,128)(2,1)}, bf16[16,5632]{1,0:T(8,128)(2,1)S(1)}, u32[]{:S(2)}, u32[]{:S(2)}) collective-permute-start(bf16[16,5632]{1,0:T(8,128)(2,1)} %get-tuple-element.83), channel_id=1, source_target_pairs={{0,2},{1,3},{2,0},{3,1},{4,6},{5,7},{6,4},{7,5},{8,10},{9,11},{10,... | collective-permute-start | bytes 540680 | tf_op jit(solution)/shard_map/ppermute | solution.py:734
  16.4 12.4 %collective-permute-start.12 = (bf16[16,5632]{1,0:T(8,128)(2,1)}, bf16[16,5632]{1,0:T(8,128)(2,1)S(1)}, u32[]{:S(2)}, u32[]{:S(2)}) collective-permute-start(bf16[16,5632]{1,0:T(8,128)(2,1)} %get-tuple-element.83), channel_id=1, source_target_pairs={{0,3},{1,2},{2,1},{3,0},{4,7},{5,6},{6,5},{7,4},{8,11},{9,10},{10,... | collective-permute-start | bytes 540680 | tf_op jit(solution)/shard_map/ppermute | solution.py:734
  16.5 16.6 %copy-start.25 = (bf16[64,1664]{1,0:T(8,128)(2,1)}, bf16[64,1664]{1,0:T(8,128)(2,1)S(1)}, u32[]{:S(2)}) copy-start(bf16[64,1664]{1,0:T(8,128)(2,1)S(1)} %constant_dynamic-update-slice_fusion.refs_0_) | copy-start | bytes 638980
  16.5 10.0 %collective-permute-start.3 = (bf16[64,1664]{1,0:T(8,128)(2,1)S(1)}, bf16[64,1664]{1,0:T(8,128)(2,1)S(1)}, u32[]{:S(2)}, u32[]{:S(2)}) collective-permute-start(bf16[64,1664]{1,0:T(8,128)(2,1)S(1)} %constant_dynamic-update-slice_fusion.refs_0_), channel_id=1, source_target_pairs={{0,8},{4,12},{8,0},{12,4},{16,24},{20,28},{24,16},{28,20},{1,9},{5... | collective-permute-start | bytes 638984 | tf_op jit(solution)/shard_map/ppermute | solution.py:734
  18.2 10.0 %collective-permute-start.4 = (bf16[64,1664]{1,0:T(8,128)(2,1)S(1)}, bf16[64,1664]{1,0:T(8,128)(2,1)S(1)}, u32[]{:S(2)}, u32[]{:S(2)}) collective-permute-start(bf16[64,1664]{1,0:T(8,128)(2,1)S(1)} %constant_dynamic-update-slice_fusion.refs_0_), channel_id=1, source_target_pairs={{0,16},{4,20},{8,24},{12,28},{16,0},{20,4},{24,8},{28,12},{1,17},{... | collective-permute-start | bytes 638984 | tf_op jit(solution)/shard_map/ppermute | solution.py:734
  19.8 8.5 %collective-permute-start.5 = (bf16[64,1664]{1,0:T(8,128)(2,1)S(1)}, bf16[64,1664]{1,0:T(8,128)(2,1)S(1)}, u32[]{:S(2)}, u32[]{:S(2)}) collective-permute-start(bf16[64,1664]{1,0:T(8,128)(2,1)S(1)} %constant_dynamic-update-slice_fusion.refs_0_), channel_id=1, source_target_pairs={{0,24},{4,28},{8,16},{12,20},{16,8},{20,12},{24,0},{28,4},{1,25},{... | collective-permute-start | bytes 638984 | tf_op jit(solution)/shard_map/ppermute | solution.py:734
  26.5 2.8 %collective-permute-start.6 = (bf16[64,1664]{1,0:T(8,128)(2,1)S(1)}, bf16[64,1664]{1,0:T(8,128)(2,1)S(1)}, u32[]{:S(2)}, u32[]{:S(2)}) collective-permute-start(bf16[64,1664]{1,0:T(8,128)(2,1)S(1)} %constant_dynamic-update-slice_fusion.refs_0_), channel_id=1, source_target_pairs={{0,4},{4,0},{8,12},{12,8},{16,20},{20,16},{24,28},{28,24},{1,5},{5... | collective-permute-start | bytes 638984 | tf_op jit(solution)/shard_map/ppermute | solution.py:734
  26.5 6.6 %copy-start.29 = (bf16[64,1664]{1,0:T(8,128)(2,1)}, bf16[64,1664]{1,0:T(8,128)(2,1)S(1)}, u32[]{:S(2)}) copy-start(bf16[64,1664]{1,0:T(8,128)(2,1)S(1)} %collective-permute-done.3.refs_1_) | copy-start | bytes 638980
  26.5 4.8 %collective-permute-start.7 = (bf16[64,1664]{1,0:T(8,128)(2,1)S(1)}, bf16[64,1664]{1,0:T(8,128)(2,1)}, u32[]{:S(2)}, u32[]{:S(2)}) collective-permute-start(bf16[64,1664]{1,0:T(8,128)(2,1)S(1)} %collective-permute-done.3.refs_1_), channel_id=1, source_target_pairs={{0,4},{4,0},{8,12},{12,8},{16,20},{20,16},{24,28},{28,24},{1,5},{5... | collective-permute-start | bytes 638984 | tf_op jit(solution)/shard_map/ppermute | solution.py:734
  28.3 4.8 %copy-start.30 = (bf16[64,1664]{1,0:T(8,128)(2,1)}, bf16[64,1664]{1,0:T(8,128)(2,1)S(1)}, u32[]{:S(2)}) copy-start(bf16[64,1664]{1,0:T(8,128)(2,1)S(1)} %collective-permute-done.4.refs_2_) | copy-start | bytes 638980
  28.3 4.1 %collective-permute-start.8 = (bf16[64,1664]{1,0:T(8,128)(2,1)S(1)}, bf16[64,1664]{1,0:T(8,128)(2,1)S(1)}, u32[]{:S(2)}, u32[]{:S(2)}) collective-permute-start(bf16[64,1664]{1,0:T(8,128)(2,1)S(1)} %collective-permute-done.4.refs_2_), channel_id=1, source_target_pairs={{0,4},{4,0},{8,12},{12,8},{16,20},{20,16},{24,28},{28,24},{1,5},{5... | collective-permute-start | bytes 638984 | tf_op jit(solution)/shard_map/ppermute | solution.py:734
  28.3 4.8 %copy-start.31 = (bf16[64,1664]{1,0:T(8,128)(2,1)}, bf16[64,1664]{1,0:T(8,128)(2,1)S(1)}, u32[]{:S(2)}) copy-start(bf16[64,1664]{1,0:T(8,128)(2,1)S(1)} %collective-permute-done.5.refs_3_) | copy-start | bytes 638980
  28.3 4.8 %collective-permute-start.9 = (bf16[64,1664]{1,0:T(8,128)(2,1)S(1)}, bf16[64,1664]{1,0:T(8,128)(2,1)}, u32[]{:S(2)}, u32[]{:S(2)}) collective-permute-start(bf16[64,1664]{1,0:T(8,128)(2,1)S(1)} %collective-permute-done.5.refs_3_), channel_id=1, source_target_pairs={{0,4},{4,0},{8,12},{12,8},{16,20},{20,16},{24,28},{28,24},{1,5},{5... | collective-permute-start | bytes 638984 | tf_op jit(solution)/shard_map/ppermute | solution.py:734
  28.8 12.6 %copy-start.24 = (bf16[64,5632]{1,0:T(8,128)(2,1)}, bf16[64,5632]{1,0:T(8,128)(2,1)S(1)}, u32[]{:S(2)}) copy-start(bf16[64,5632]{1,0:T(8,128)(2,1)S(1)} %constant_dynamic-update-slice_fusion.4.refs_0_) | copy-start | bytes 2162692
  28.8 38.4 %collective-permute-start.13 = (bf16[64,5632]{1,0:T(8,128)(2,1)S(1)}, bf16[64,5632]{1,0:T(8,128)(2,1)S(1)}, u32[]{:S(2)}, u32[]{:S(2)}) collective-permute-start(bf16[64,5632]{1,0:T(8,128)(2,1)S(1)} %constant_dynamic-update-slice_fusion.4.refs_0_), channel_id=1, source_target_pairs={{0,8},{4,12},{8,0},{12,4},{16,24},{20,28},{24,16},{28,20},{1,9},{5... | collective-permute-start | bytes 2162696 | tf_op jit(solution)/shard_map/ppermute | solution.py:734
  29.3 3.8 %copy-start.32 = (bf16[64,1664]{1,0:T(8,128)(2,1)}, bf16[64,1664]{1,0:T(8,128)(2,1)S(1)}, u32[]{:S(2)}) copy-start(bf16[64,1664]{1,0:T(8,128)(2,1)S(1)} %collective-permute-done.6.refs_4_) | copy-start | bytes 638980
  29.3 38.0 %collective-permute-start.14 = (bf16[64,5632]{1,0:T(8,128)(2,1)S(1)}, bf16[64,5632]{1,0:T(8,128)(2,1)S(1)}, u32[]{:S(2)}, u32[]{:S(2)}) collective-permute-start(bf16[64,5632]{1,0:T(8,128)(2,1)S(1)} %constant_dynamic-update-slice_fusion.4.refs_0_), channel_id=1, source_target_pairs={{0,16},{4,20},{8,24},{12,28},{16,0},{20,4},{24,8},{28,12},{1,17},{... | collective-permute-start | bytes 2162696 | tf_op jit(solution)/shard_map/ppermute | solution.py:734
  31.3 36.0 %collective-permute-start.15 = (bf16[64,5632]{1,0:T(8,128)(2,1)S(1)}, bf16[64,5632]{1,0:T(8,128)(2,1)S(1)}, u32[]{:S(2)}, u32[]{:S(2)}) collective-permute-start(bf16[64,5632]{1,0:T(8,128)(2,1)S(1)} %constant_dynamic-update-slice_fusion.4.refs_0_), channel_id=1, source_target_pairs={{0,24},{4,28},{8,16},{12,20},{16,8},{20,12},{24,0},{28,4},{1,25},{... | collective-permute-start | bytes 2162696 | tf_op jit(solution)/shard_map/ppermute | solution.py:734
  33.1 36.2 %collective-permute-start.16 = (bf16[64,5632]{1,0:T(8,128)(2,1)S(1)}, bf16[64,5632]{1,0:T(8,128)(2,1)}, u32[]{:S(2)}, u32[]{:S(2)}) collective-permute-start(bf16[64,5632]{1,0:T(8,128)(2,1)S(1)} %constant_dynamic-update-slice_fusion.4.refs_0_), channel_id=1, source_target_pairs={{0,4},{4,0},{8,12},{12,8},{16,20},{20,16},{24,28},{28,24},{1,5},{5... | collective-permute-start | bytes 2162696 | tf_op jit(solution)/shard_map/ppermute | solution.py:734
  67.2 0.9 copy-start.15
  67.3 1.1 copy-start.16
  67.3 1.4 copy-start.17
  68.7 2.4 %collective-permute-start.17 = (bf16[64,5632]{1,0:T(8,128)(2,1)}, bf16[64,5632]{1,0:T(8,128)(2,1)S(1)}, u32[]{:S(2)}, u32[]{:S(2)}) collective-permute-start(bf16[64,5632]{1,0:T(8,128)(2,1)} %get-tuple-element.85.refs_1_), channel_id=1, source_target_pairs={{0,4},{4,0},{8,12},{12,8},{16,20},{20,16},{24,28},{28,24},{1,5},{5... | collective-permute-start | bytes 2162696 | tf_op jit(solution)/shard_map/ppermute | solution.py:734
  68.7 3.4 %collective-permute-start.18 = (bf16[64,5632]{1,0:T(8,128)(2,1)}, bf16[64,5632]{1,0:T(8,128)(2,1)S(1)}, u32[]{:S(2)}, u32[]{:S(2)}) collective-permute-start(bf16[64,5632]{1,0:T(8,128)(2,1)} %get-tuple-element.86.refs_2_), channel_id=1, source_target_pairs={{0,4},{4,0},{8,12},{12,8},{16,20},{20,16},{24,28},{28,24},{1,5},{5... | collective-permute-start | bytes 2162696 | tf_op jit(solution)/shard_map/ppermute | solution.py:734
  69.2 4.0 %collective-permute-start.19 = (bf16[64,5632]{1,0:T(8,128)(2,1)}, bf16[64,5632]{1,0:T(8,128)(2,1)S(1)}, u32[]{:S(2)}, u32[]{:S(2)}) collective-permute-start(bf16[64,5632]{1,0:T(8,128)(2,1)} %get-tuple-element.87.refs_3_), channel_id=1, source_target_pairs={{0,4},{4,0},{8,12},{12,8},{16,20},{20,16},{24,28},{28,24},{1,5},{5... | collective-permute-start | bytes 2162696 | tf_op jit(solution)/shard_map/ppermute | solution.py:734
  71.1 2.1 copy-start.26
  72.2 1.0 copy-start.27
  73.2 0.9 copy-start.28
  118.1 5.9 %collective-permute-start.20 = (bf16[16,192,512]{2,1,0:T(8,128)(2,1)}, bf16[16,192,512]{2,1,0:T(8,128)(2,1)S(1)}, u32[]{:S(2)}, u32[]{:S(2)}) collective-permute-start(bf16[16,192,512]{2,1,0:T(8,128)(2,1)} %bitcast.24), channel_id=1, source_target_pairs={{0,4},{4,0},{8,12},{12,8},{16,20},{20,16},{24,28},{28,24},{1,5},{5... | collective-permute-start | bytes 9437192 | tf_op jit(solution)/shard_map/ppermute | solution.py:734
  124.0 1.9 copy-start
  128.1 0.9 copy-start.9
  129.0 38.2 %collective-permute-start.21 = (bf16[4,192,512]{2,1,0:T(8,128)(2,1)}, bf16[4,192,512]{2,1,0:T(8,128)(2,1)S(1)}, u32[]{:S(2)}, u32[]{:S(2)}) collective-permute-start(bf16[4,192,512]{2,1,0:T(8,128)(2,1)} %get-tuple-element.105), channel_id=1, source_target_pairs={{0,8},{4,12},{8,0},{12,4},{16,24},{20,28},{24,16},{28,20},{1,9},{5... | collective-permute-start | bytes 2359304 | tf_op jit(solution)/shard_map/ppermute | solution.py:734
  129.0 38.2 %collective-permute-start.22 = (bf16[4,192,512]{2,1,0:T(8,128)(2,1)}, bf16[4,192,512]{2,1,0:T(8,128)(2,1)S(1)}, u32[]{:S(2)}, u32[]{:S(2)}) collective-permute-start(bf16[4,192,512]{2,1,0:T(8,128)(2,1)} %get-tuple-element.106), channel_id=1, source_target_pairs={{0,16},{4,20},{8,24},{12,28},{16,0},{20,4},{24,8},{28,12},{1,17},{... | collective-permute-start | bytes 2359304 | tf_op jit(solution)/shard_map/ppermute | solution.py:734
  131.5 35.8 %collective-permute-start.23 = (bf16[4,192,512]{2,1,0:T(8,128)(2,1)S(1)}, bf16[4,192,512]{2,1,0:T(8,128)(2,1)S(1)}, u32[]{:S(2)}, u32[]{:S(2)}) collective-permute-start(bf16[4,192,512]{2,1,0:T(8,128)(2,1)S(1)} %get-tuple-element.107), channel_id=1, source_target_pairs={{0,24},{4,28},{8,16},{12,20},{16,8},{20,12},{24,0},{28,4},{1,25},{... | collective-permute-start | bytes 2359304 | tf_op jit(solution)/shard_map/ppermute | solution.py:734
  167.2 0.9 copy-start.1
  167.2 1.1 copy-start.3
  167.3 1.4 copy-start.5
  168.7 1.1 copy-start.10
  168.7 6.0 %collective-permute-start.24 = (bf16[16,16,1536]{2,1,0:T(8,128)(2,1)}, bf16[16,16,1536]{2,1,0:T(8,128)(2,1)S(1)}, u32[]{:S(2)}, u32[]{:S(2)}) collective-permute-start(bf16[16,16,1536]{2,1,0:T(8,128)(2,1)} %hold.3), channel_id=1, source_target_pairs={{0,4},{4,0},{8,12},{12,8},{16,20},{20,16},{24,28},{28,24},{1,5},{5... | collective-permute-start | bytes 2359304 | tf_op jit(solution)/shard_map/ppermute | solution.py:734
  169.8 1.1 copy-start.2
  170.9 1.1 copy-start.4
  172.1 1.1 copy-start.6
  173.2 1.4 copy-start.7
  174.6 19.5 %copy-start.8 = (bf16[1,192,512]{2,1,0:T(8,128)(2,1)}, bf16[1,192,512]{2,1,0:T(8,128)(2,1)S(1)}, u32[]{:S(2)}) copy-start(bf16[1,192,512]{2,1,0:T(8,128)(2,1)S(1)} %get-tuple-element.108.refs_1_) | copy-start | bytes 589828
  176.6 6.2 %collective-permute-start.25 = (bf16[4,16,1536]{2,1,0:T(8,128)(2,1)S(1)}, bf16[4,16,1536]{2,1,0:T(8,128)(2,1)S(1)}, u32[]{:S(2)}, u32[]{:S(2)}) collective-permute-start(bf16[4,16,1536]{2,1,0:T(8,128)(2,1)S(1)} %get-tuple-element.111), channel_id=1, source_target_pairs={{0,8},{4,12},{8,0},{12,4},{16,24},{20,28},{24,16},{28,20},{1,9},{5... | collective-permute-start | bytes 589832 | tf_op jit(solution)/shard_map/ppermute | solution.py:734
  176.6 23.5 %collective-permute-start.33 = (bf16[1,192,512]{2,1,0:T(8,128)(2,1)S(1)}, bf16[1,192,512]{2,1,0:T(8,128)(2,1)S(1)}, u32[]{:S(2)}, u32[]{:S(2)}) collective-permute-start(bf16[1,192,512]{2,1,0:T(8,128)(2,1)S(1)} %get-tuple-element.121), channel_id=1, source_target_pairs={{0,3},{1,2},{2,1},{3,0},{4,7},{5,6},{6,5},{7,4},{8,11},{9,10},{10,... | collective-permute-start | bytes 589832 | tf_op jit(solution)/shard_map/ppermute | solution.py:734
  180.1 20.7 %collective-permute-start.31 = (bf16[1,192,512]{2,1,0:T(8,128)(2,1)S(1)}, bf16[1,192,512]{2,1,0:T(8,128)(2,1)S(1)}, u32[]{:S(2)}, u32[]{:S(2)}) collective-permute-start(bf16[1,192,512]{2,1,0:T(8,128)(2,1)S(1)} %get-tuple-element.119), channel_id=1, source_target_pairs={{0,1},{1,0},{2,3},{3,2},{4,5},{5,4},{6,7},{7,6},{8,9},{9,8},{10,11... | collective-permute-start | bytes 589832 | tf_op jit(solution)/shard_map/ppermute | solution.py:734
  180.5 20.3 %collective-permute-start.32 = (bf16[1,192,512]{2,1,0:T(8,128)(2,1)S(1)}, bf16[1,192,512]{2,1,0:T(8,128)(2,1)S(1)}, u32[]{:S(2)}, u32[]{:S(2)}) collective-permute-start(bf16[1,192,512]{2,1,0:T(8,128)(2,1)S(1)} %get-tuple-element.120), channel_id=1, source_target_pairs={{0,2},{1,3},{2,0},{3,1},{4,6},{5,7},{6,4},{7,5},{8,10},{9,11},{10,... | collective-permute-start | bytes 589832 | tf_op jit(solution)/shard_map/ppermute | solution.py:734
  181.0 13.1 %collective-permute-start.26 = (bf16[4,16,1536]{2,1,0:T(8,128)(2,1)S(1)}, bf16[4,16,1536]{2,1,0:T(8,128)(2,1)S(1)}, u32[]{:S(2)}, u32[]{:S(2)}) collective-permute-start(bf16[4,16,1536]{2,1,0:T(8,128)(2,1)S(1)} %get-tuple-element.112), channel_id=1, source_target_pairs={{0,16},{4,20},{8,24},{12,28},{16,0},{20,4},{24,8},{28,12},{1,17},{... | collective-permute-start | bytes 589832 | tf_op jit(solution)/shard_map/ppermute | solution.py:734
  182.7 11.4 %collective-permute-start.27 = (bf16[4,16,1536]{2,1,0:T(8,128)(2,1)S(1)}, bf16[4,16,1536]{2,1,0:T(8,128)(2,1)S(1)}, u32[]{:S(2)}, u32[]{:S(2)}) collective-permute-start(bf16[4,16,1536]{2,1,0:T(8,128)(2,1)S(1)} %get-tuple-element.113), channel_id=1, source_target_pairs={{0,24},{4,28},{8,16},{12,20},{16,8},{20,12},{24,0},{28,4},{1,25},{... | collective-permute-start | bytes 589832 | tf_op jit(solution)/shard_map/ppermute | solution.py:734
  184.6 9.5 %copy-start.12 = (bf16[4,16,1536]{2,1,0:T(8,128)(2,1)S(1)}, bf16[4,16,1536]{2,1,0:T(8,128)(2,1)}, u32[]{:S(2)}) copy-start(bf16[4,16,1536]{2,1,0:T(8,128)(2,1)} %copy-done.11) | copy-start | bytes 589828
  194.1 0.7 copy-start.14
  195.8 5.0 %collective-permute-start.28 = (bf16[1,16,1536]{2,1,0:T(8,128)(2,1)S(1)}, bf16[1,16,1536]{2,1,0:T(8,128)(2,1)S(1)}, u32[]{:S(2)}, u32[]{:S(2)}) collective-permute-start(bf16[1,16,1536]{2,1,0:T(8,128)(2,1)S(1)} %get-tuple-element.116), channel_id=1, source_target_pairs={{0,1},{1,0},{2,3},{3,2},{4,5},{5,4},{6,7},{7,6},{8,9},{9,8},{10,11... | collective-permute-start | bytes 147464 | tf_op jit(solution)/shard_map/ppermute | solution.py:734
  196.3 6.4 %collective-permute-start.29 = (bf16[1,16,1536]{2,1,0:T(8,128)(2,1)S(1)}, bf16[1,16,1536]{2,1,0:T(8,128)(2,1)S(1)}, u32[]{:S(2)}, u32[]{:S(2)}) collective-permute-start(bf16[1,16,1536]{2,1,0:T(8,128)(2,1)S(1)} %get-tuple-element.117), channel_id=1, source_target_pairs={{0,2},{1,3},{2,0},{3,1},{4,6},{5,7},{6,4},{7,5},{8,10},{9,11},{10,... | collective-permute-start | bytes 147464 | tf_op jit(solution)/shard_map/ppermute | solution.py:734
  200.1 5.9 %copy-start.18 = (bf16[1,192,512]{2,1,0:T(8,128)(2,1)}, bf16[1,192,512]{2,1,0:T(8,128)(2,1)S(1)}, u32[]{:S(2)}) copy-start(bf16[1,192,512]{2,1,0:T(8,128)(2,1)S(1)} %collective-permute-done.33) | copy-start | bytes 589828
  200.1 5.9 %collective-permute-start.30 = (bf16[1,16,1536]{2,1,0:T(8,128)(2,1)S(1)}, bf16[1,16,1536]{2,1,0:T(8,128)(2,1)S(1)}, u32[]{:S(2)}, u32[]{:S(2)}) collective-permute-start(bf16[1,16,1536]{2,1,0:T(8,128)(2,1)S(1)} %get-tuple-element.118), channel_id=1, source_target_pairs={{0,3},{1,2},{2,1},{3,0},{4,7},{5,6},{6,5},{7,4},{8,11},{9,10},{10,... | collective-permute-start | bytes 147464 | tf_op jit(solution)/shard_map/ppermute | solution.py:734
  200.8 5.2 %copy-start.19 = (bf16[1,192,512]{2,1,0:T(8,128)(2,1)}, bf16[1,192,512]{2,1,0:T(8,128)(2,1)S(1)}, u32[]{:S(2)}) copy-start(bf16[1,192,512]{2,1,0:T(8,128)(2,1)S(1)} %collective-permute-done.31) | copy-start | bytes 589828
  200.8 5.2 %copy-start.20 = (bf16[1,192,512]{2,1,0:T(8,128)(2,1)}, bf16[1,192,512]{2,1,0:T(8,128)(2,1)S(1)}, u32[]{:S(2)}) copy-start(bf16[1,192,512]{2,1,0:T(8,128)(2,1)S(1)} %collective-permute-done.32) | copy-start | bytes 589828
  200.8 5.2 %copy-start.21 = (bf16[1,16,1536]{2,1,0:T(8,128)(2,1)}, bf16[1,16,1536]{2,1,0:T(8,128)(2,1)S(1)}, u32[]{:S(2)}) copy-start(bf16[1,16,1536]{2,1,0:T(8,128)(2,1)S(1)} %collective-permute-done.28) | copy-start | bytes 147460
  202.7 3.3 %copy-start.22 = (bf16[1,16,1536]{2,1,0:T(8,128)(2,1)}, bf16[1,16,1536]{2,1,0:T(8,128)(2,1)S(1)}, u32[]{:S(2)}) copy-start(bf16[1,16,1536]{2,1,0:T(8,128)(2,1)S(1)} %collective-permute-done.29) | copy-start | bytes 147460
  (4 other events, 2.6 us)

commit v3 on v2

--- a/solution.py
+++ b/solution.py
@@ -48,7 +48,7 @@
 
 
 def sigmoid(values):
-    return 1.0 / (1.0 + jnp.exp(-values))
+    return 0.5 + 0.5 * jnp.tanh(0.5 * values)
 
 
 def project_kernel(
@@ -375,7 +375,7 @@
             pltpu.SemaphoreType.DMA((4,)),
             pltpu.SemaphoreType.DMA((2,)),
         ],
-        compiler_params=pltpu.CompilerParams(vmem_limit_bytes=VMEM),
+        compiler_params=pltpu.CompilerParams(vmem_limit_bytes=57 * MIB),
         cost_estimate=pl.CostEstimate(
             flops=20 * length * length * width, bytes_accessed=8 * MIB, transcendentals=4 * length * length
         ),
@@ -600,16 +600,12 @@
 
 
 def finish_kernel(tokens, zeta_one_low, grad_middle, weights, gate_attn, small, *refs):
-    *grads, _after, token_grad, finished = refs
+    grads, (token_grad, finished) = refs[:3], refs[-2:]
     finished[...] = jnp.zeros(finished.shape, F32)
-    groups = len(grads) // 3
     width = tokens.shape[1]
-    part = width // groups
     total = dot_t(zeta_one_low[...], gate_attn[...])
-    for at, grad in enumerate(grads):
-        which, group = at % 3, at // 3
-        columns = pl.ds(which * width + group * part, part)
-        total = total + dot_t(grad[...], weights[:, columns])
+    for which, grad in enumerate(grads):
+        total = total + dot_t(grad[...], weights[:, which * width : (which + 1) * width])
     unit, scale = normalise(tokens[...].astype(F32))
     grad_unit = total * small[0:1, :]
     token_grad[...] = grad_middle[...] + scale * (
@@ -617,31 +613,29 @@
     )
 
 
-def finish(tokens, zeta_one_low, grad_middle, weights, gate_attn, small, grads, after):
+def finish(tokens, zeta_one_low, grad_middle, weights, gate_attn, small, grads, after, first, count, before=()):
     length, width = tokens.shape
     tile = 512
-    by_rows = pl.BlockSpec((tile, width), lambda i: (i, 0))
+    by_rows = pl.BlockSpec((tile, width), lambda i: (i + first, 0))
+    whole = lambda *shape: pl.BlockSpec(shape, lambda i: (0, 0))
     return pl.pallas_call(
         finish_kernel,
-        grid=(length // tile,),
-        in_specs=[
-            by_rows, by_rows, by_rows,
-            pl.BlockSpec((width, 3 * width), lambda i: (0, 0)),
-            pl.BlockSpec((width, width), lambda i: (0, 0)),
-            pl.BlockSpec((4, width), lambda i: (0, 0)),
-        ] + [pl.BlockSpec((tile, g.shape[1]), lambda i: (i, 0)) for g in grads]
-        + [pl.BlockSpec(memory_space=pl.ANY)],
-        out_specs=[by_rows, pl.BlockSpec((8, 128), lambda i: (0, 0))],
+        grid=(count,),
+        in_specs=[by_rows] * 3 + [whole(width, 3 * width), whole(width, width), whole(4, width)]
+        + [by_rows] * 3
+        + [ANYWHERE] * (1 + len(before)),
+        out_specs=[by_rows, whole(8, 128)],
         out_shape=[
             jax.ShapeDtypeStruct((length, width), F32),
             jax.ShapeDtypeStruct((8, 128), F32),
         ],
+        input_output_aliases={10: 0} if before else {},
         compiler_params=pltpu.CompilerParams(vmem_limit_bytes=VMEM),
         cost_estimate=pl.CostEstimate(
-            flops=8 * length * width * width, bytes_accessed=16 * MIB, transcendentals=length
+            flops=8 * tile * count * width * width, bytes_accessed=5 * MIB * count, transcendentals=tile
         ),
         name="finish",
-    )(tokens, zeta_one_low, grad_middle, weights, gate_attn, small, *grads, after)
+    )(tokens, zeta_one_low, grad_middle, weights, gate_attn, small, *grads, after, *before)
 
 
 def row_sum(weight, grad):
@@ -755,6 +749,7 @@
         out_specs=[ANYWHERE] * count,
         out_shape=[jax.ShapeDtypeStruct(a.shape, a.dtype) for a in arrays],
         input_output_aliases={k: k for k in range(count)},
+        compiler_params=pltpu.CompilerParams(vmem_limit_bytes=4 * MIB),
         name="hold",
     )(*arrays, *after)
 
@@ -931,14 +926,19 @@
         late_plane = add_core(late_send, late_keep, False, 12, line[0])
     else:
         late_plane = [me]
-    token_grad, finished = finish(
-        tokens, zeta_one_low, grad_middle, weights, whole_gate, small, grads, late_plane[0]
-    )
+    to_finish = (tokens, zeta_one_low, grad_middle, weights, whole_gate, small, grads)
+    tiles = length // 512
+    token_grad, finished = finish(*to_finish, late_plane[0], 0, tiles - 1)
+    if direct:
+        late_line = add_split(late_plane[0], swap_plane(late_plane), False, 12, finished)
+    else:
+        late_line = [me]
+    token_grad, finished = finish(*to_finish, late_line[0], tiles - 1, 1, (token_grad,))
 
     counted = length * devices
     if direct:
         early = along_line(line)
-        late = along_line(add_split(late_plane[0], swap_plane(late_plane), False, 12, finished))
+        late = along_line(late_line)
         device_and_count = jnp.stack([device, jnp.int32(counted)]).astype(jnp.int32)
         *owned, norm_one, norm_two, bias_one, bias_two, stats = close(
             device_and_count, w_query, w_key, w_value, gate_attn, gate_ffn, w_in, norm_attn, norm_ffn, late, early, finished

time: 211 us -> 202 us (0.957)
  Pallas kernels: 133 us -> 105 us
  waiting for transfers between devices: 21.4 us -> 40.9 us
  local copies, waits for them, and re-layouts: 17.4 us -> 12.1 us
  starting transfers between devices: 35.9 us -> 40.1 us
    ppermute x34, waiting for transfers between devices: 21.4 us -> 40.9 us  [swap(): return lax.ppermute(values, axis, [(i, i ^ bits) for i in range(count)])]
    pallas_call x1, Pallas kernels: 34.7 us -> 18.3 us  [attend_back(): pl.pallas_call(attend_back_kernel, in_specs=[smem, smem, vmem] + [ANYWHER...]
    pallas_call x1, Pallas kernels: 25.8 us -> 13 us  [attend(): pl.pallas_call(attend_kernel, in_specs=[smem, vmem, ANYWHERE, ANYWHERE, A...]
    unnamed x74 -> x68, local copies, waits for them, and re-layouts: 16.1 us -> 10.8 us
    ppermute x34, starting transfers between devices: 35.9 us -> 40.1 us  [swap(): return lax.ppermute(values, axis, [(i, i ^ bits) for i in range(count)])]
    pallas_call x1 -> x2, Pallas kernels: 9.5 us -> 12.3 us  [finish(): pl.pallas_call(finish_kernel, grid=(count,), in_specs=[by_rows] * 3 + [wh...]
  transfers between devices with their start and end apart: 34 -> 34, of which waited for: 9 -> 11; matrix products, arithmetic and copies ran while one was open for 2% -> 2% of each run, Pallas kernels for 38% -> 27%
where the time goes in v3:
time: 202 us; the launch traced here: 201 us
  Pallas kernels  105 us (52%)
  waiting for transfers between devices  40.9 us (20%)
  starting transfers between devices  40.1 us (20%)
  local copies, waits for them, and re-layouts  12.1 us (6%)
    pallas_call x1, Pallas kernels, feed_forward(): pl.pallas_call(feed_kernel, grid=(length // tile,), in_specs=[pl.BlockSpe...  43.6 us
    ppermute x34, waiting for transfers between devices, swap(): return lax.ppermute(values, axis, [(i, i ^ bits) for i in range(count)])  40.9 us
    ppermute x34, starting transfers between devices, swap(): return lax.ppermute(values, axis, [(i, i ^ bits) for i in range(count)])  40.1 us
    pallas_call x1, Pallas kernels, attend_back(): pl.pallas_call(attend_back_kernel, in_specs=[smem, smem, vmem] + [ANYWHER...  18.3 us
    pallas_call x1, Pallas kernels, attend(): pl.pallas_call(attend_kernel, in_specs=[smem, vmem, ANYWHERE, ANYWHERE, A...  13 us
    pallas_call x2, Pallas kernels, finish(): pl.pallas_call(finish_kernel, grid=(count,), in_specs=[by_rows] * 3 + [wh...  12.3 us
    unnamed x68, local copies, waits for them, and re-layouts  10.8 us
    pallas_call x1, Pallas kernels, project(): pl.pallas_call(project_kernel, grid=(length // tile,), in_specs=[pl.Block...  8.3 us
  transfers between devices with their start and end apart: 34, of which 11 were waited for; matrix products, arithmetic and copies ran while one was open for 2% of the time, Pallas kernels for 27%

profile of v3, /device:TPU:0, one launch (start us, length us, event | category | flops | bytes accessed | tf_op | source)
XLA Modules:
  0.0 200.5 jit_solution(8641282813500099486)
XLA Ops:
  0.7 2.1 %pack.1 = (bf16[16,1664]{1,0:T(8,128)(2,1)}, bf16[16,5632]{1,0:T(8,128)(2,1)}) custom-call(s32[1]{0:T(128)} %bitcast.device.me.refs_1_.refs_3_, bf16[16]{0:T(256)(128)(2,1)} %gain_one.1, bf16[16]{0:T(256)(128)(2,1)} %gain_two.1, bf16[16]{0:T(256)(128)(2,1)} %refs_2_.1, bf16[16]{0:T(256)(128)(2,1)} %refs_3_.1, bf16[16,512]{1,0:T(8,128)(2,1)} %query.1, ...), custom_call_target="tpu_custom_call" | custom-call | tf_op jit(solution)/shard_map/pack/pallas_call | solution.py:847
  2.8 3.0 %collective-permute-start = (bf16[16,1664]{1,0:T(8,128)(2,1)}, bf16[16,1664]{1,0:T(8,128)(2,1)S(1)}, u32[]{:S(2)}, u32[]{:S(2)}) collective-permute-start(bf16[16,1664]{1,0:T(8,128)(2,1)} %get-tuple-element.77), channel_id=1, source_target_pairs={{0,1},{1,0},{2,3},{3,2},{4,5},{5,4},{6,7},{7,6},{8,9},{9,8},{10,11... | collective-permute-start | bytes 159752 | tf_op jit(solution)/shard_map/ppermute | solution.py:728
  5.8 2.6 %collective-permute-start.1 = (bf16[16,1664]{1,0:T(8,128)(2,1)}, bf16[16,1664]{1,0:T(8,128)(2,1)S(1)}, u32[]{:S(2)}, u32[]{:S(2)}) collective-permute-start(bf16[16,1664]{1,0:T(8,128)(2,1)} %get-tuple-element.77), channel_id=1, source_target_pairs={{0,2},{1,3},{2,0},{3,1},{4,6},{5,7},{6,4},{7,5},{8,10},{9,11},{10,... | collective-permute-start | bytes 159752 | tf_op jit(solution)/shard_map/ppermute | solution.py:728
  8.4 0.9 collective-permute-start.10
  9.3 3.5 %collective-permute-start.11 = (bf16[16,5632]{1,0:T(8,128)(2,1)}, bf16[16,5632]{1,0:T(8,128)(2,1)S(1)}, u32[]{:S(2)}, u32[]{:S(2)}) collective-permute-start(bf16[16,5632]{1,0:T(8,128)(2,1)} %get-tuple-element.85), channel_id=1, source_target_pairs={{0,2},{1,3},{2,0},{3,1},{4,6},{5,7},{6,4},{7,5},{8,10},{9,11},{10,... | collective-permute-start | bytes 540680 | tf_op jit(solution)/shard_map/ppermute | solution.py:728
  12.8 0.8 constant_dynamic-update-slice_fusion.3
  13.6 0.9 constant_dynamic-update-slice_fusion.7
  14.5 0.6 pad_add_fusion.order
  15.1 1.3 reshape.55.segment_row
  16.5 1.8 collective-permute-start.3
  18.2 1.5 collective-permute-start.4
  19.8 1.9 collective-permute-start.5
  21.6 4.9 %collective-permute-done.11 = bf16[16,5632]{1,0:T(8,128)(2,1)S(1)} collective-permute-done((bf16[16,5632]{1,0:T(8,128)(2,1)}, bf16[16,5632]{1,0:T(8,128)(2,1)S(1)}, u32[]{:S(2)}, u32[]{:S(2)}) %collective-permute-start.11) | collective-permute-done | bytes 180256 | tf_op jit(solution)/shard_map/ppermute | solution.py:728
  26.5 0.6 collective-permute-start.7
  27.1 1.2 collective-permute-done.4.refs_2_
  28.3 0.5 collective-permute-start.9
  28.8 0.4 collective-permute-start.13
  29.3 2.0 %collective-permute-start.14 = (bf16[64,5632]{1,0:T(8,128)(2,1)S(1)}, bf16[64,5632]{1,0:T(8,128)(2,1)S(1)}, u32[]{:S(2)}, u32[]{:S(2)}) collective-permute-start(bf16[64,5632]{1,0:T(8,128)(2,1)S(1)} %constant_dynamic-update-slice_fusion.4.refs_0_), channel_id=1, source_target_pairs={{0,16},{4,20},{8,24},{12,28},{16,0},{20,4},{24,8},{28,12},{1,17},{... | collective-permute-start | bytes 2162696 | tf_op jit(solution)/shard_map/ppermute | solution.py:728
  31.3 1.1 collective-permute-start.15
  32.5 0.6 copy-done.30
  33.1 8.3 %project.1 = (bf16[1536,512]{1,0:T(8,128)(2,1)}, bf16[512,1536]{1,0:T(8,128)(2,1)}, bf16[1536,512]{1,0:T(8,128)(2,1)}, bf16[1536,512]{1,0:T(8,128)(2,1)}, bf16[1...) custom-call(s32[32]{0:T(128)} %pad_add_fusion.order, ...), custom_call_target="tpu_custom_call" | custom-call | flops 2415919104 | bytes 12582912 | tf_op jit(solution)/shard_map/project/pallas_call | solution.py:104
  41.5 13.0 %attend.1 = (f32[1536,512]{1,0:T(8,128)}, f32[8,1536]{1,0:T(8,128)}) custom-call(s32[1536]{0:T(1024)} %segment.3, s32[1,1536]{1,0:T(1,128)} %reshape.55.segment_row, bf16[1536,512]{1,0:T(8,128)(2,1)} %get-tuple-element.80.query_in, bf16[1536,512]{1,0:T(8,128)(2,1)} %get-tuple-element.81.key_in, bf16[512,1536]{1,0:T(8,128)(2,1)} %get-tuple-element.82.value_t_in), custom_call_target="tpu_custom_call" | custom-call | flops 9663676416 | bytes 6291456 | tf_op jit(solution)/shard_map/attend/pallas_call | solution.py:218
  54.5 7.6 %collective-permute-done.14.refs_1_ = bf16[64,5632]{1,0:T(8,128)(2,1)S(1)} collective-permute-done((bf16[64,5632]{1,0:T(8,128)(2,1)S(1)}, bf16[64,5632]{1,0:T(8,128)(2,1)S(1)}, u32[]{:S(2)}, u32[]{:S(2)}) %collective-permute-start.14) | collective-permute-done | bytes 720928 | tf_op jit(solution)/shard_map/ppermute | solution.py:728
  62.2 1.1 collective-permute-done.15.refs_2_
  63.3 0.8 copy-done.11
  64.1 0.5 collective-permute-start.18
  64.6 0.1 collective-permute-start.19
  64.7 1.6 collective-permute-done.17.refs_5_
  66.3 1.0 collective-permute-done.18.refs_6_
  67.3 1.0 collective-permute-done.19.refs_7_
  68.4 0.9 copy-done.24
  69.3 43.6 %feed_forward.1 = (bf16[1536,512]{1,0:T(8,128)(2,1)}, f32[1536,512]{1,0:T(8,128)}, bf16[1536,512]{1,0:T(8,128)(2,1)}, bf16[1536,512]{1,0:T(8,128)(2,1)}, f32[8,1...) custom-call(s32[1]{0:T(128)} %bitcast.device.me.refs_1_.refs_3_, ...), custom_call_target="tpu_custom_call" | custom-call | flops 26575110144 | bytes 25165824 | tf_op jit(solution)/shard_map/feed_forward/pallas_call | solution.py:555
  112.9 0.2 collective-permute-start.20
  113.1 5.7 %collective-permute-done.20.refs_0_ = bf16[16,192,512]{2,1,0:T(8,128)(2,1)S(1)} collective-permute-done((bf16[16,192,512]{2,1,0:T(8,128)(2,1)}, bf16[16,192,512]{2,1,0:T(8,128)(2,1)S(1)}, u32[]{:S(2)}, u32[]{:S(2)}) %collective-permute-start.20) | collective-permute-done | bytes 3145760 | tf_op jit(solution)/shard_map/ppermute | solution.py:728
  118.8 1.9 copy-done
  120.7 1.1 add_split.4
  121.9 0.9 copy-done.3
  122.7 1.0 collective-permute-start.21
  123.8 3.8 %collective-permute-start.22 = (bf16[4,192,512]{2,1,0:T(8,128)(2,1)S(1)}, bf16[4,192,512]{2,1,0:T(8,128)(2,1)S(1)}, u32[]{:S(2)}, u32[]{:S(2)}) collective-permute-start(bf16[4,192,512]{2,1,0:T(8,128)(2,1)S(1)} %get-tuple-element.108), channel_id=1, source_target_pairs={{0,16},{4,20},{8,24},{12,28},{16,0},{20,4},{24,8},{28,12},{1,17},{... | collective-permute-start | bytes 2359304 | tf_op jit(solution)/shard_map/ppermute | solution.py:728
  127.6 1.5 collective-permute-start.23
  129.0 18.3 %attend_back.1 = (bf16[1536,512]{1,0:T(8,128)(2,1)}, bf16[1536,512]{1,0:T(8,128)(2,1)}, bf16[1536,512]{1,0:T(8,128)(2,1)}, bf16[16,16,1536]{2,1,0:T(8,128)(2,1)}, bf16[16,16,1536]{2,1,0:T(8,128)(2,1)}) custom-call(s32[1]{0:T(128)} %bitcast.device.me.refs_1_.refs_3_, s32[1536]{0:T(1024)} %segment.3, s32[1,1536]{1,0:T(1,128)} %reshape.55.segment_row, ...), custom_call_target="tpu_custom_call" | custom-call | flops 24159191040 | bytes 8388608 | tf_op jit(solution)/shard_map/attend_back/pallas_call | solution.py:361
  147.4 14.4 %collective-permute-done.22.refs_2_.refs_1_ = bf16[4,192,512]{2,1,0:T(8,128)(2,1)S(1)} collective-permute-done((bf16[4,192,512]{2,1,0:T(8,128)(2,1)S(1)}, bf16[4,192,512]{2,1,0:T(8,128)(2,1)S(1)}, u32[]{:S(2)}, u32[]{:S(2)}) %collective-permute-start.22) | collective-permute-done | bytes 786464 | tf_op jit(solution)/shard_map/ppermute | solution.py:728
  161.8 1.9 collective-permute-done.23.refs_3_.refs_2_
  163.7 1.1 copy-done.4
  164.8 1.4 add_split.5
  166.2 1.2 add_split.6
  167.5 0.7 copy-done.5
  168.2 0.6 collective-permute-start.25
  168.8 0.6 pad_add_fusion.1.device
  169.3 3.7 %collective-permute-start.33 = (bf16[1,192,512]{2,1,0:T(8,128)(2,1)S(1)}, bf16[1,192,512]{2,1,0:T(8,128)(2,1)S(1)}, u32[]{:S(2)}, u32[]{:S(2)}) collective-permute-start(bf16[1,192,512]{2,1,0:T(8,128)(2,1)S(1)} %get-tuple-element.124), channel_id=1, source_target_pairs={{0,3},{1,2},{2,1},{3,0},{4,7},{5,6},{6,5},{7,4},{8,11},{9,10},{10,... | collective-permute-start | bytes 589832 | tf_op jit(solution)/shard_map/ppermute | solution.py:728
  173.1 1.0 collective-permute-start.32
  174.0 1.4 collective-permute-start.26
  175.5 1.4 collective-permute-start.27
  176.9 7.2 %finish.2 = (f32[1536,512]{1,0:T(8,128)}, f32[8,128]{1,0:T(8,128)}) custom-call(bf16[1536,512]{1,0:T(8,128)(2,1)} %tokens.7, bf16[1536,512]{1,0:T(8,128)(2,1)} %get-tuple-element.91.zeta_one_low, f32[1536,512]{1,0:T(8,128)} %get-tuple-element.92.grad_middle, bf16[512,1536]{1,0:T(8,128)(2,1)} %get-tuple-element.93.weights, ...), custom_call_target="tpu_custom_call" | custom-call | flops 2147483648 | bytes 10485760 | tf_op jit(solution)/shard_map/finish/pallas_call | solution.py:621
  184.0 0.3 collective-permute-done.26.refs_1_
  184.3 0.7 copy-done.12
  185.0 0.4 add_split.7
  185.4 0.6 copy-done.10
  186.0 2.6 %collective-permute-start.28 = (bf16[1,16,1536]{2,1,0:T(8,128)(2,1)S(1)}, bf16[1,16,1536]{2,1,0:T(8,128)(2,1)S(1)}, u32[]{:S(2)}, u32[]{:S(2)}) collective-permute-start(bf16[1,16,1536]{2,1,0:T(8,128)(2,1)S(1)} %get-tuple-element.119), channel_id=1, source_target_pairs={{0,1},{1,0},{2,3},{3,2},{4,5},{5,4},{6,7},{7,6},{8,9},{9,8},{10,11... | collective-permute-start | bytes 147464 | tf_op jit(solution)/shard_map/ppermute | solution.py:728
  188.6 1.7 collective-permute-start.29
  190.4 0.7 collective-permute-start.30
  191.0 5.1 %finish.3 = (f32[1536,512]{1,0:T(8,128)}, f32[8,128]{1,0:T(8,128)}) custom-call(bf16[1536,512]{1,0:T(8,128)(2,1)} %tokens.7, bf16[1536,512]{1,0:T(8,128)(2,1)} %get-tuple-element.91.zeta_one_low, f32[1536,512]{1,0:T(8,128)} %get-tuple-element.92.grad_middle, bf16[512,1536]{1,0:T(8,128)(2,1)} %get-tuple-element.93.weights, ...), custom_call_target="tpu_custom_call", output_to_operand_aliasing={{0}: (10, {})} | custom-call | flops 1073741824 | bytes 5242880 | tf_op jit(solution)/shard_map/finish/pallas_call | solution.py:621
  196.3 0.6 copy-done.14
  197.0 3.3 %close.1 = (f32[16,512]{1,0:T(8,128)}, f32[16,512]{1,0:T(8,128)}, f32[16,512]{1,0:T(8,128)}, f32[16,512]{1,0:T(8,128)}, f32[16,512]{1,0:T(8,128)}, /*index=5*/f3...) custom-call(s32[2]{0:T(128)} %pad_add_fusion.1.device, ...), custom_call_target="tpu_custom_call" | custom-call | tf_op jit(solution)/shard_map/close/pallas_call | solution.py:712
  (92 shorter events, 0.5 us)
Async XLA Ops:
  2.8 13.6 %collective-permute-start = (bf16[16,1664]{1,0:T(8,128)(2,1)}, bf16[16,1664]{1,0:T(8,128)(2,1)S(1)}, u32[]{:S(2)}, u32[]{:S(2)}) collective-permute-start(bf16[16,1664]{1,0:T(8,128)(2,1)} %get-tuple-element.77), channel_id=1, source_target_pairs={{0,1},{1,0},{2,3},{3,2},{4,5},{5,4},{6,7},{7,6},{8,9},{9,8},{10,11... | collective-permute-start | bytes 159752 | tf_op jit(solution)/shard_map/ppermute | solution.py:728
  5.8 10.6 %collective-permute-start.1 = (bf16[16,1664]{1,0:T(8,128)(2,1)}, bf16[16,1664]{1,0:T(8,128)(2,1)S(1)}, u32[]{:S(2)}, u32[]{:S(2)}) collective-permute-start(bf16[16,1664]{1,0:T(8,128)(2,1)} %get-tuple-element.77), channel_id=1, source_target_pairs={{0,2},{1,3},{2,0},{3,1},{4,6},{5,7},{6,4},{7,5},{8,10},{9,11},{10,... | collective-permute-start | bytes 159752 | tf_op jit(solution)/shard_map/ppermute | solution.py:728
  8.4 8.1 %collective-permute-start.2 = (bf16[16,1664]{1,0:T(8,128)(2,1)}, bf16[16,1664]{1,0:T(8,128)(2,1)S(1)}, u32[]{:S(2)}, u32[]{:S(2)}) collective-permute-start(bf16[16,1664]{1,0:T(8,128)(2,1)} %get-tuple-element.77), channel_id=1, source_target_pairs={{0,3},{1,2},{2,1},{3,0},{4,7},{5,6},{6,5},{7,4},{8,11},{9,10},{10,... | collective-permute-start | bytes 159752 | tf_op jit(solution)/shard_map/ppermute | solution.py:728
  8.4 11.4 %collective-permute-start.10 = (bf16[16,5632]{1,0:T(8,128)(2,1)}, bf16[16,5632]{1,0:T(8,128)(2,1)S(1)}, u32[]{:S(2)}, u32[]{:S(2)}) collective-permute-start(bf16[16,5632]{1,0:T(8,128)(2,1)} %get-tuple-element.85), channel_id=1, source_target_pairs={{0,1},{1,0},{2,3},{3,2},{4,5},{5,4},{6,7},{7,6},{8,9},{9,8},{10,11... | collective-permute-start | bytes 540680 | tf_op jit(solution)/shard_map/ppermute | solution.py:728
  9.3 17.2 %collective-permute-start.11 = (bf16[16,5632]{1,0:T(8,128)(2,1)}, bf16[16,5632]{1,0:T(8,128)(2,1)S(1)}, u32[]{:S(2)}, u32[]{:S(2)}) collective-permute-start(bf16[16,5632]{1,0:T(8,128)(2,1)} %get-tuple-element.85), channel_id=1, source_target_pairs={{0,2},{1,3},{2,0},{3,1},{4,6},{5,7},{6,4},{7,5},{8,10},{9,11},{10,... | collective-permute-start | bytes 540680 | tf_op jit(solution)/shard_map/ppermute | solution.py:728
  16.4 12.4 %collective-permute-start.12 = (bf16[16,5632]{1,0:T(8,128)(2,1)}, bf16[16,5632]{1,0:T(8,128)(2,1)S(1)}, u32[]{:S(2)}, u32[]{:S(2)}) collective-permute-start(bf16[16,5632]{1,0:T(8,128)(2,1)} %get-tuple-element.85), channel_id=1, source_target_pairs={{0,3},{1,2},{2,1},{3,0},{4,7},{5,6},{6,5},{7,4},{8,11},{9,10},{10,... | collective-permute-start | bytes 540680 | tf_op jit(solution)/shard_map/ppermute | solution.py:728
  16.5 16.7 %copy-start.20 = (bf16[64,1664]{1,0:T(8,128)(2,1)}, bf16[64,1664]{1,0:T(8,128)(2,1)S(1)}, u32[]{:S(2)}) copy-start(bf16[64,1664]{1,0:T(8,128)(2,1)S(1)} %constant_dynamic-update-slice_fusion.refs_0_) | copy-start | bytes 638980
  16.5 10.0 %collective-permute-start.3 = (bf16[64,1664]{1,0:T(8,128)(2,1)S(1)}, bf16[64,1664]{1,0:T(8,128)(2,1)S(1)}, u32[]{:S(2)}, u32[]{:S(2)}) collective-permute-start(bf16[64,1664]{1,0:T(8,128)(2,1)S(1)} %constant_dynamic-update-slice_fusion.refs_0_), channel_id=1, source_target_pairs={{0,8},{4,12},{8,0},{12,4},{16,24},{20,28},{24,16},{28,20},{1,9},{5... | collective-permute-start | bytes 638984 | tf_op jit(solution)/shard_map/ppermute | solution.py:728
  18.2 10.0 %collective-permute-start.4 = (bf16[64,1664]{1,0:T(8,128)(2,1)S(1)}, bf16[64,1664]{1,0:T(8,128)(2,1)S(1)}, u32[]{:S(2)}, u32[]{:S(2)}) collective-permute-start(bf16[64,1664]{1,0:T(8,128)(2,1)S(1)} %constant_dynamic-update-slice_fusion.refs_0_), channel_id=1, source_target_pairs={{0,16},{4,20},{8,24},{12,28},{16,0},{20,4},{24,8},{28,12},{1,17},{... | collective-permute-start | bytes 638984 | tf_op jit(solution)/shard_map/ppermute | solution.py:728
  19.8 8.5 %collective-permute-start.5 = (bf16[64,1664]{1,0:T(8,128)(2,1)S(1)}, bf16[64,1664]{1,0:T(8,128)(2,1)S(1)}, u32[]{:S(2)}, u32[]{:S(2)}) collective-permute-start(bf16[64,1664]{1,0:T(8,128)(2,1)S(1)} %constant_dynamic-update-slice_fusion.refs_0_), channel_id=1, source_target_pairs={{0,24},{4,28},{8,16},{12,20},{16,8},{20,12},{24,0},{28,4},{1,25},{... | collective-permute-start | bytes 638984 | tf_op jit(solution)/shard_map/ppermute | solution.py:728
  26.5 2.8 %collective-permute-start.6 = (bf16[64,1664]{1,0:T(8,128)(2,1)S(1)}, bf16[64,1664]{1,0:T(8,128)(2,1)S(1)}, u32[]{:S(2)}, u32[]{:S(2)}) collective-permute-start(bf16[64,1664]{1,0:T(8,128)(2,1)S(1)} %constant_dynamic-update-slice_fusion.refs_0_), channel_id=1, source_target_pairs={{0,4},{4,0},{8,12},{12,8},{16,20},{20,16},{24,28},{28,24},{1,5},{5... | collective-permute-start | bytes 638984 | tf_op jit(solution)/shard_map/ppermute | solution.py:728
  26.5 6.6 %copy-start.25 = (bf16[64,1664]{1,0:T(8,128)(2,1)}, bf16[64,1664]{1,0:T(8,128)(2,1)S(1)}, u32[]{:S(2)}) copy-start(bf16[64,1664]{1,0:T(8,128)(2,1)S(1)} %collective-permute-done.3.refs_1_) | copy-start | bytes 638980
  26.5 4.8 %collective-permute-start.7 = (bf16[64,1664]{1,0:T(8,128)(2,1)S(1)}, bf16[64,1664]{1,0:T(8,128)(2,1)S(1)}, u32[]{:S(2)}, u32[]{:S(2)}) collective-permute-start(bf16[64,1664]{1,0:T(8,128)(2,1)S(1)} %collective-permute-done.3.refs_1_), channel_id=1, source_target_pairs={{0,4},{4,0},{8,12},{12,8},{16,20},{20,16},{24,28},{28,24},{1,5},{5... | collective-permute-start | bytes 638984 | tf_op jit(solution)/shard_map/ppermute | solution.py:728
  28.3 4.1 %copy-start.26 = (bf16[64,1664]{1,0:T(8,128)(2,1)}, bf16[64,1664]{1,0:T(8,128)(2,1)S(1)}, u32[]{:S(2)}) copy-start(bf16[64,1664]{1,0:T(8,128)(2,1)S(1)} %collective-permute-done.4.refs_2_) | copy-start | bytes 638980
  28.3 4.1 %collective-permute-start.8 = (bf16[64,1664]{1,0:T(8,128)(2,1)S(1)}, bf16[64,1664]{1,0:T(8,128)(2,1)S(1)}, u32[]{:S(2)}, u32[]{:S(2)}) collective-permute-start(bf16[64,1664]{1,0:T(8,128)(2,1)S(1)} %collective-permute-done.4.refs_2_), channel_id=1, source_target_pairs={{0,4},{4,0},{8,12},{12,8},{16,20},{20,16},{24,28},{28,24},{1,5},{5... | collective-permute-start | bytes 638984 | tf_op jit(solution)/shard_map/ppermute | solution.py:728
  28.3 4.1 %copy-start.27 = (bf16[64,1664]{1,0:T(8,128)(2,1)}, bf16[64,1664]{1,0:T(8,128)(2,1)S(1)}, u32[]{:S(2)}) copy-start(bf16[64,1664]{1,0:T(8,128)(2,1)S(1)} %collective-permute-done.5.refs_3_) | copy-start | bytes 638980
  28.3 4.8 %collective-permute-start.9 = (bf16[64,1664]{1,0:T(8,128)(2,1)S(1)}, bf16[64,1664]{1,0:T(8,128)(2,1)}, u32[]{:S(2)}, u32[]{:S(2)}) collective-permute-start(bf16[64,1664]{1,0:T(8,128)(2,1)S(1)} %collective-permute-done.5.refs_3_), channel_id=1, source_target_pairs={{0,4},{4,0},{8,12},{12,8},{16,20},{20,16},{24,28},{28,24},{1,5},{5... | collective-permute-start | bytes 638984 | tf_op jit(solution)/shard_map/ppermute | solution.py:728
  28.8 12.6 %copy-start.19 = (bf16[64,5632]{1,0:T(8,128)(2,1)}, bf16[64,5632]{1,0:T(8,128)(2,1)S(1)}, u32[]{:S(2)}) copy-start(bf16[64,5632]{1,0:T(8,128)(2,1)S(1)} %constant_dynamic-update-slice_fusion.4.refs_0_) | copy-start | bytes 2162692
  28.8 25.7 %collective-permute-start.13 = (bf16[64,5632]{1,0:T(8,128)(2,1)S(1)}, bf16[64,5632]{1,0:T(8,128)(2,1)S(1)}, u32[]{:S(2)}, u32[]{:S(2)}) collective-permute-start(bf16[64,5632]{1,0:T(8,128)(2,1)S(1)} %constant_dynamic-update-slice_fusion.4.refs_0_), channel_id=1, source_target_pairs={{0,8},{4,12},{8,0},{12,4},{16,24},{20,28},{24,16},{28,20},{1,9},{5... | collective-permute-start | bytes 2162696 | tf_op jit(solution)/shard_map/ppermute | solution.py:728
  29.3 3.1 %copy-start.28 = (bf16[64,1664]{1,0:T(8,128)(2,1)}, bf16[64,1664]{1,0:T(8,128)(2,1)S(1)}, u32[]{:S(2)}) copy-start(bf16[64,1664]{1,0:T(8,128)(2,1)S(1)} %collective-permute-done.6.refs_4_) | copy-start | bytes 638980
  29.3 32.9 %collective-permute-start.14 = (bf16[64,5632]{1,0:T(8,128)(2,1)S(1)}, bf16[64,5632]{1,0:T(8,128)(2,1)S(1)}, u32[]{:S(2)}, u32[]{:S(2)}) collective-permute-start(bf16[64,5632]{1,0:T(8,128)(2,1)S(1)} %constant_dynamic-update-slice_fusion.4.refs_0_), channel_id=1, source_target_pairs={{0,16},{4,20},{8,24},{12,28},{16,0},{20,4},{24,8},{28,12},{1,17},{... | collective-permute-start | bytes 2162696 | tf_op jit(solution)/shard_map/ppermute | solution.py:728
  31.3 1.1 copy-start.29
  31.3 32.0 %collective-permute-start.15 = (bf16[64,5632]{1,0:T(8,128)(2,1)S(1)}, bf16[64,5632]{1,0:T(8,128)(2,1)S(1)}, u32[]{:S(2)}, u32[]{:S(2)}) collective-permute-start(bf16[64,5632]{1,0:T(8,128)(2,1)S(1)} %constant_dynamic-update-slice_fusion.4.refs_0_), channel_id=1, source_target_pairs={{0,24},{4,28},{8,16},{12,20},{16,8},{20,12},{24,0},{28,4},{1,25},{... | collective-permute-start | bytes 2162696 | tf_op jit(solution)/shard_map/ppermute | solution.py:728
  32.4 0.7 copy-start.30
  32.4 32.2 %collective-permute-start.16 = (bf16[64,5632]{1,0:T(8,128)(2,1)S(1)}, bf16[64,5632]{1,0:T(8,128)(2,1)S(1)}, u32[]{:S(2)}, u32[]{:S(2)}) collective-permute-start(bf16[64,5632]{1,0:T(8,128)(2,1)S(1)} %constant_dynamic-update-slice_fusion.4.refs_0_), channel_id=1, source_target_pairs={{0,4},{4,0},{8,12},{12,8},{16,20},{20,16},{24,28},{28,24},{1,5},{5... | collective-permute-start | bytes 2162696 | tf_op jit(solution)/shard_map/ppermute | solution.py:728
  63.3 0.8 copy-start.11
  64.1 5.2 %copy-start.7 = (bf16[64,5632]{1,0:T(8,128)(2,1)}, bf16[64,5632]{1,0:T(8,128)(2,1)S(1)}, u32[]{:S(2)}) copy-start(bf16[64,5632]{1,0:T(8,128)(2,1)S(1)} %get-tuple-element.87.refs_1_) | copy-start | bytes 2162692
  64.1 5.2 %copy-start.8 = (bf16[64,5632]{1,0:T(8,128)(2,1)}, bf16[64,5632]{1,0:T(8,128)(2,1)S(1)}, u32[]{:S(2)}) copy-start(bf16[64,5632]{1,0:T(8,128)(2,1)S(1)} %get-tuple-element.88.refs_2_) | copy-start | bytes 2162692
  64.1 5.2 %copy-start.9 = (bf16[64,5632]{1,0:T(8,128)(2,1)}, bf16[64,5632]{1,0:T(8,128)(2,1)S(1)}, u32[]{:S(2)}) copy-start(bf16[64,5632]{1,0:T(8,128)(2,1)S(1)} %get-tuple-element.89.refs_3_) | copy-start | bytes 2162692
  64.1 2.2 %collective-permute-start.17 = (bf16[64,5632]{1,0:T(8,128)(2,1)S(1)}, bf16[64,5632]{1,0:T(8,128)(2,1)S(1)}, u32[]{:S(2)}, u32[]{:S(2)}) collective-permute-start(bf16[64,5632]{1,0:T(8,128)(2,1)S(1)} %get-tuple-element.87.refs_1_), channel_id=1, source_target_pairs={{0,4},{4,0},{8,12},{12,8},{16,20},{20,16},{24,28},{28,24},{1,5},{5... | collective-permute-start | bytes 2162696 | tf_op jit(solution)/shard_map/ppermute | solution.py:728
  64.1 3.2 %collective-permute-start.18 = (bf16[64,5632]{1,0:T(8,128)(2,1)S(1)}, bf16[64,5632]{1,0:T(8,128)(2,1)S(1)}, u32[]{:S(2)}, u32[]{:S(2)}) collective-permute-start(bf16[64,5632]{1,0:T(8,128)(2,1)S(1)} %get-tuple-element.88.refs_2_), channel_id=1, source_target_pairs={{0,4},{4,0},{8,12},{12,8},{16,20},{20,16},{24,28},{28,24},{1,5},{5... | collective-permute-start | bytes 2162696 | tf_op jit(solution)/shard_map/ppermute | solution.py:728
  64.6 3.7 %collective-permute-start.19 = (bf16[64,5632]{1,0:T(8,128)(2,1)S(1)}, bf16[64,5632]{1,0:T(8,128)(2,1)S(1)}, u32[]{:S(2)}, u32[]{:S(2)}) collective-permute-start(bf16[64,5632]{1,0:T(8,128)(2,1)S(1)} %get-tuple-element.89.refs_3_), channel_id=1, source_target_pairs={{0,4},{4,0},{8,12},{12,8},{16,20},{20,16},{24,28},{28,24},{1,5},{5... | collective-permute-start | bytes 2162696 | tf_op jit(solution)/shard_map/ppermute | solution.py:728
  64.7 4.6 %copy-start.21 = (bf16[64,5632]{1,0:T(8,128)(2,1)}, bf16[64,5632]{1,0:T(8,128)(2,1)S(1)}, u32[]{:S(2)}) copy-start(bf16[64,5632]{1,0:T(8,128)(2,1)S(1)} %collective-permute-done.16.refs_4_) | copy-start | bytes 2162692
  66.3 2.1 %copy-start.22 = (bf16[64,5632]{1,0:T(8,128)(2,1)}, bf16[64,5632]{1,0:T(8,128)(2,1)S(1)}, u32[]{:S(2)}) copy-start(bf16[64,5632]{1,0:T(8,128)(2,1)S(1)} %collective-permute-done.17.refs_5_) | copy-start | bytes 2162692
  67.3 1.0 copy-start.23
  68.4 0.9 copy-start.24
  112.9 5.9 %collective-permute-start.20 = (bf16[16,192,512]{2,1,0:T(8,128)(2,1)}, bf16[16,192,512]{2,1,0:T(8,128)(2,1)S(1)}, u32[]{:S(2)}, u32[]{:S(2)}) collective-permute-start(bf16[16,192,512]{2,1,0:T(8,128)(2,1)} %bitcast.24), channel_id=1, source_target_pairs={{0,4},{4,0},{8,12},{12,8},{16,20},{20,16},{24,28},{28,24},{1,5},{5... | collective-permute-start | bytes 9437192 | tf_op jit(solution)/shard_map/ppermute | solution.py:728
  118.8 1.9 copy-start
  121.8 0.9 copy-start.3
  122.7 24.6 %collective-permute-start.21 = (bf16[4,192,512]{2,1,0:T(8,128)(2,1)S(1)}, bf16[4,192,512]{2,1,0:T(8,128)(2,1)S(1)}, u32[]{:S(2)}, u32[]{:S(2)}) collective-permute-start(bf16[4,192,512]{2,1,0:T(8,128)(2,1)S(1)} %get-tuple-element.107), channel_id=1, source_target_pairs={{0,8},{4,12},{8,0},{12,4},{16,24},{20,28},{24,16},{28,20},{1,9},{5... | collective-permute-start | bytes 2359304 | tf_op jit(solution)/shard_map/ppermute | solution.py:728
  123.8 38.0 %collective-permute-start.22 = (bf16[4,192,512]{2,1,0:T(8,128)(2,1)S(1)}, bf16[4,192,512]{2,1,0:T(8,128)(2,1)S(1)}, u32[]{:S(2)}, u32[]{:S(2)}) collective-permute-start(bf16[4,192,512]{2,1,0:T(8,128)(2,1)S(1)} %get-tuple-element.108), channel_id=1, source_target_pairs={{0,16},{4,20},{8,24},{12,28},{16,0},{20,4},{24,8},{28,12},{1,17},{... | collective-permute-start | bytes 2359304 | tf_op jit(solution)/shard_map/ppermute | solution.py:728
  127.6 36.1 %collective-permute-start.23 = (bf16[4,192,512]{2,1,0:T(8,128)(2,1)S(1)}, bf16[4,192,512]{2,1,0:T(8,128)(2,1)S(1)}, u32[]{:S(2)}, u32[]{:S(2)}) collective-permute-start(bf16[4,192,512]{2,1,0:T(8,128)(2,1)S(1)} %get-tuple-element.109), channel_id=1, source_target_pairs={{0,24},{4,28},{8,16},{12,20},{16,8},{20,12},{24,0},{28,4},{1,25},{... | collective-permute-start | bytes 2359304 | tf_op jit(solution)/shard_map/ppermute | solution.py:728
  163.7 1.1 copy-start.4
  163.7 2.6 %copy-start.1 = (bf16[16,16,1536]{2,1,0:T(8,128)(2,1)S(1)}, bf16[16,16,1536]{2,1,0:T(8,128)(2,1)}, u32[]{:S(2)}) copy-start(bf16[16,16,1536]{2,1,0:T(8,128)(2,1)} %get-tuple-element.105.own) | copy-start | bytes 2359300
  163.7 2.6 %collective-permute-start.24 = (bf16[16,16,1536]{2,1,0:T(8,128)(2,1)}, bf16[16,16,1536]{2,1,0:T(8,128)(2,1)S(1)}, u32[]{:S(2)}, u32[]{:S(2)}) collective-permute-start(bf16[16,16,1536]{2,1,0:T(8,128)(2,1)} %hold.3), channel_id=1, source_target_pairs={{0,4},{4,0},{8,12},{12,8},{16,20},{20,16},{24,28},{28,24},{1,5},{5... | collective-permute-start | bytes 2359304 | tf_op jit(solution)/shard_map/ppermute | solution.py:728
  166.2 17.8 %copy-start.2 = (bf16[1,192,512]{2,1,0:T(8,128)(2,1)}, bf16[1,192,512]{2,1,0:T(8,128)(2,1)S(1)}, u32[]{:S(2)}) copy-start(bf16[1,192,512]{2,1,0:T(8,128)(2,1)S(1)} %get-tuple-element.110.refs_1_) | copy-start | bytes 589828
  167.5 0.7 copy-start.5
  168.2 7.3 %collective-permute-start.25 = (bf16[4,16,1536]{2,1,0:T(8,128)(2,1)S(1)}, bf16[4,16,1536]{2,1,0:T(8,128)(2,1)S(1)}, u32[]{:S(2)}, u32[]{:S(2)}) collective-permute-start(bf16[4,16,1536]{2,1,0:T(8,128)(2,1)S(1)} %get-tuple-element.112), channel_id=1, source_target_pairs={{0,8},{4,12},{8,0},{12,4},{16,24},{20,28},{24,16},{28,20},{1,9},{5... | collective-permute-start | bytes 589832 | tf_op jit(solution)/shard_map/ppermute | solution.py:728
  169.3 21.0 %collective-permute-start.33 = (bf16[1,192,512]{2,1,0:T(8,128)(2,1)S(1)}, bf16[1,192,512]{2,1,0:T(8,128)(2,1)S(1)}, u32[]{:S(2)}, u32[]{:S(2)}) collective-permute-start(bf16[1,192,512]{2,1,0:T(8,128)(2,1)S(1)} %get-tuple-element.124), channel_id=1, source_target_pairs={{0,3},{1,2},{2,1},{3,0},{4,7},{5,6},{6,5},{7,4},{8,11},{9,10},{10,... | collective-permute-start | bytes 589832 | tf_op jit(solution)/shard_map/ppermute | solution.py:728
  173.0 23.1 %collective-permute-start.31 = (bf16[1,192,512]{2,1,0:T(8,128)(2,1)S(1)}, bf16[1,192,512]{2,1,0:T(8,128)(2,1)S(1)}, u32[]{:S(2)}, u32[]{:S(2)}) collective-permute-start(bf16[1,192,512]{2,1,0:T(8,128)(2,1)S(1)} %get-tuple-element.122), channel_id=1, source_target_pairs={{0,1},{1,0},{2,3},{3,2},{4,5},{5,4},{6,7},{7,6},{8,9},{9,8},{10,11... | collective-permute-start | bytes 589832 | tf_op jit(solution)/shard_map/ppermute | solution.py:728
  173.1 23.2 %collective-permute-start.32 = (bf16[1,192,512]{2,1,0:T(8,128)(2,1)S(1)}, bf16[1,192,512]{2,1,0:T(8,128)(2,1)S(1)}, u32[]{:S(2)}, u32[]{:S(2)}) collective-permute-start(bf16[1,192,512]{2,1,0:T(8,128)(2,1)S(1)} %get-tuple-element.123), channel_id=1, source_target_pairs={{0,2},{1,3},{2,0},{3,1},{4,6},{5,7},{6,4},{7,5},{8,10},{9,11},{10,... | collective-permute-start | bytes 589832 | tf_op jit(solution)/shard_map/ppermute | solution.py:728
  174.0 10.3 %collective-permute-start.26 = (bf16[4,16,1536]{2,1,0:T(8,128)(2,1)S(1)}, bf16[4,16,1536]{2,1,0:T(8,128)(2,1)S(1)}, u32[]{:S(2)}, u32[]{:S(2)}) collective-permute-start(bf16[4,16,1536]{2,1,0:T(8,128)(2,1)S(1)} %get-tuple-element.113), channel_id=1, source_target_pairs={{0,16},{4,20},{8,24},{12,28},{16,0},{20,4},{24,8},{28,12},{1,17},{... | collective-permute-start | bytes 589832 | tf_op jit(solution)/shard_map/ppermute | solution.py:728
  175.5 8.9 %collective-permute-start.27 = (bf16[4,16,1536]{2,1,0:T(8,128)(2,1)S(1)}, bf16[4,16,1536]{2,1,0:T(8,128)(2,1)S(1)}, u32[]{:S(2)}, u32[]{:S(2)}) collective-permute-start(bf16[4,16,1536]{2,1,0:T(8,128)(2,1)S(1)} %get-tuple-element.114), channel_id=1, source_target_pairs={{0,24},{4,28},{8,16},{12,20},{16,8},{20,12},{24,0},{28,4},{1,25},{... | collective-permute-start | bytes 589832 | tf_op jit(solution)/shard_map/ppermute | solution.py:728
  176.9 7.5 %copy-start.6 = (bf16[4,16,1536]{2,1,0:T(8,128)(2,1)S(1)}, bf16[4,16,1536]{2,1,0:T(8,128)(2,1)}, u32[]{:S(2)}) copy-start(bf16[4,16,1536]{2,1,0:T(8,128)(2,1)} %copy-done.5) | copy-start | bytes 589828
  184.3 0.7 copy-start.12
  186.0 10.2 %collective-permute-start.28 = (bf16[1,16,1536]{2,1,0:T(8,128)(2,1)S(1)}, bf16[1,16,1536]{2,1,0:T(8,128)(2,1)S(1)}, u32[]{:S(2)}, u32[]{:S(2)}) collective-permute-start(bf16[1,16,1536]{2,1,0:T(8,128)(2,1)S(1)} %get-tuple-element.119), channel_id=1, source_target_pairs={{0,1},{1,0},{2,3},{3,2},{4,5},{5,4},{6,7},{7,6},{8,9},{9,8},{10,11... | collective-permute-start | bytes 147464 | tf_op jit(solution)/shard_map/ppermute | solution.py:728
  188.6 7.6 %collective-permute-start.29 = (bf16[1,16,1536]{2,1,0:T(8,128)(2,1)S(1)}, bf16[1,16,1536]{2,1,0:T(8,128)(2,1)S(1)}, u32[]{:S(2)}, u32[]{:S(2)}) collective-permute-start(bf16[1,16,1536]{2,1,0:T(8,128)(2,1)S(1)} %get-tuple-element.120), channel_id=1, source_target_pairs={{0,2},{1,3},{2,0},{3,1},{4,6},{5,7},{6,4},{7,5},{8,10},{9,11},{10,... | collective-permute-start | bytes 147464 | tf_op jit(solution)/shard_map/ppermute | solution.py:728
  190.4 5.8 %copy-start.13 = (bf16[1,192,512]{2,1,0:T(8,128)(2,1)}, bf16[1,192,512]{2,1,0:T(8,128)(2,1)S(1)}, u32[]{:S(2)}) copy-start(bf16[1,192,512]{2,1,0:T(8,128)(2,1)S(1)} %collective-permute-done.33) | copy-start | bytes 589828
  190.4 5.9 %collective-permute-start.30 = (bf16[1,16,1536]{2,1,0:T(8,128)(2,1)S(1)}, bf16[1,16,1536]{2,1,0:T(8,128)(2,1)S(1)}, u32[]{:S(2)}, u32[]{:S(2)}) collective-permute-start(bf16[1,16,1536]{2,1,0:T(8,128)(2,1)S(1)} %get-tuple-element.121), channel_id=1, source_target_pairs={{0,3},{1,2},{2,1},{3,0},{4,7},{5,6},{6,5},{7,4},{8,11},{9,10},{10,... | collective-permute-start | bytes 147464 | tf_op jit(solution)/shard_map/ppermute | solution.py:728
  196.2 0.7 copy-start.14
  196.2 0.7 copy-start.15
  196.2 0.7 copy-start.16
  196.3 0.7 copy-start.17
  196.3 0.8 copy-start.18
  (1 other events, 0.6 us)

commit v4 on v3

--- a/solution.py
+++ b/solution.py
@@ -126,10 +126,19 @@
     )(order, tokens, *pieces)
 
 
-def bias_of(segment_row, key_block, query_block):
-    key_at = key_block * BLOCK + lax.broadcasted_iota(jnp.int32, (BLOCK, BLOCK), 0)
-    query_at = query_block * BLOCK + lax.broadcasted_iota(jnp.int32, (BLOCK, BLOCK), 1)
+def bias_of(segment_row, first_key, first_query, keys):
+    shape = (keys, segment_row.shape[1])
+    key_at = first_key + lax.broadcasted_iota(jnp.int32, shape, 0)
+    query_at = first_query + lax.broadcasted_iota(jnp.int32, shape, 1)
     return jnp.where((key_at >= segment_row) & (key_at <= query_at), 0.0, MASKED)
+
+
+def parts_of(block, step):
+    start = block * BLOCK
+    half = BLOCK // 2
+    if block is step:
+        return [(start, half, 0), (start + half, half, half)]
+    return [(start, BLOCK, 0)]
 
 
 def keep_heads(source, target):
@@ -175,28 +184,44 @@
         seen = segment_row[:, here]
 
         def visit(block, _):
-            bias = bias_of(seen, block, step)
-            rows = pl.ds(pl.multiple_of(block * BLOCK, BLOCK), BLOCK)
-            scores = [dot_t(key[rows, pair(h)], masked_query[h]) + bias for h in heads]
+            parts = parts_of(block, step)
+            rows = [pl.ds(pl.multiple_of(start, keys), keys) for start, keys, _ in parts]
+            bias = [
+                bias_of(seen[:, low:], start, step * BLOCK + low, keys) for start, keys, low in parts
+            ]
+
+            def widen(value, part, fill):
+                low = parts[part][2]
+                return jnp.concatenate([jnp.full((value.shape[0], low), fill, F32), value], axis=1) if low else value
+
+            each = [(h, p) for h in heads for p in range(len(parts))]
+            scores = {
+                (h, p): dot_t(key[rows[p], pair(h)], masked_query[h, parts[p][2] :]) + bias[p] for h, p in each
+            }
             old = [peak[h : h + 1, :] for h in heads]
-            new = [jnp.maximum(o, jnp.max(s, axis=0, keepdims=True)) for o, s in zip(old, scores)]
-            power = [jnp.exp(s - n) for s, n in zip(scores, new)]
+            new = list(old)
+            for h, p in each:
+                highest = jnp.max(scores[h, p], axis=0, keepdims=True)
+                new[h] = jnp.maximum(new[h], widen(highest, p, -1e30))
+            power = {(h, p): jnp.exp(scores[h, p] - new[h][:, parts[p][2] :]) for h, p in each}
             fade = [jnp.exp(o - n) for o, n in zip(old, new)]
-            added = [jnp.sum(p, axis=0, keepdims=True) for p in power]
-            high = [p.astype(BF) for p in power]
-            rest = [(p - x.astype(F32)).astype(BF) for p, x in zip(power, high)]
-            mixes = [
-                mix[own(h), :] * fade[h] + dot(value_t[own(h), rows], high[h]) + dot(value_t[own(h), rows], rest[h])
-                for h in heads
-            ]
+            high = {at: power[at].astype(BF) for at in each}
+            rest = {at: (power[at] - high[at].astype(F32)).astype(BF) for at in each}
+            mixes = [mix[own(h), :] * fade[h] for h in heads]
+            added = [total[h : h + 1, :] * fade[h] for h in heads]
+            for h, p in each:
+                values = value_t[own(h), rows[p]]
+                mixes[h] = mixes[h] + widen(dot(values, high[h, p]) + dot(values, rest[h, p]), p, 0.0)
+                added[h] = added[h] + widen(jnp.sum(power[h, p], axis=0, keepdims=True), p, 0.0)
             for h in heads:
                 peak[h : h + 1, :] = new[h]
-                total[h : h + 1, :] = total[h : h + 1, :] * fade[h] + added[h]
+                total[h : h + 1, :] = added[h]
                 mix[own(h), :] = mixes[h]
             return 0
 
         first = lax.div(segment[step * BLOCK], BLOCK)
-        lax.fori_loop(first, step + 1, visit, 0)
+        lax.fori_loop(first, step, visit, 0)
+        visit(step, 0)
         log_total[:, here] = peak[...] + jnp.log(total[...])
         for head in heads:
             mix[own(head), :] = mix[own(head), :] / total[head : head + 1, :]
@@ -287,26 +312,40 @@
         seen = segment_row[:, here]
 
         def visit(block, _):
-            bias = bias_of(seen, block, step)
-            rows = pl.ds(pl.multiple_of(block * BLOCK, BLOCK), BLOCK)
-            scores = [dot_t(key[rows, pair(h)], masked_query[h]) for h in heads]
-            grad_probs = [dot_t(value[rows, pair(h)], masked_grad[h]) for h in heads]
-            probs = [jnp.exp((scores[h] + bias) - log_total[h : h + 1, here]) for h in heads]
-            grad_scores = [
-                (probs[h] * (grad_probs[h] - inner_sum[h : h + 1, here])).astype(BF) for h in heads
+            parts = parts_of(block, step)
+            rows = [pl.ds(pl.multiple_of(start, keys), keys) for start, keys, _ in parts]
+            bias = [
+                bias_of(seen[:, low:], start, step * BLOCK + low, keys) for start, keys, low in parts
             ]
-            to_value = [dot(probs[h].astype(BF), masked_grad[h]) for h in heads]
-            to_key = [dot(grad_scores[h], masked_query[h]) for h in heads]
-            to_query = [dot(key_t[own(h), rows], grad_scores[h]) for h in heads]
-            for h in heads[::2]:
-                value_sum[rows, pair(h)] += to_value[h] + to_value[h + 1]
-                key_sum[rows, pair(h)] += to_key[h] + to_key[h + 1]
-            for h in heads:
-                query_sum[own(h), :] += to_query[h]
+            lows = [low for _, _, low in parts]
+            each = [(h, p) for h in heads for p in range(len(parts))]
+            queries = {(h, p): masked_query[h, lows[p] :] for h, p in each}
+            grads = {(h, p): masked_grad[h, lows[p] :] for h, p in each}
+            logs = [log_total[h : h + 1, here] for h in heads]
+            inner = [inner_sum[h : h + 1, here] for h in heads]
+            scores = {(h, p): dot_t(key[rows[p], pair(h)], queries[h, p]) for h, p in each}
+            grad_probs = {(h, p): dot_t(value[rows[p], pair(h)], grads[h, p]) for h, p in each}
+            probs = {
+                (h, p): jnp.exp((scores[h, p] + bias[p]) - logs[h][:, lows[p] :]) for h, p in each
+            }
+            grad_scores = {
+                (h, p): (probs[h, p] * (grad_probs[h, p] - inner[h][:, lows[p] :])).astype(BF)
+                for h, p in each
+            }
+            to_value = {at: dot(probs[at].astype(BF), grads[at]) for at in each}
+            to_key = {at: dot(grad_scores[at], queries[at]) for at in each}
+            to_query = {(h, p): dot(key_t[own(h), rows[p]], grad_scores[h, p]) for h, p in each}
+            for p in range(len(parts)):
+                for h in heads[::2]:
+                    value_sum[rows[p], pair(h)] += to_value[h, p] + to_value[h + 1, p]
+                    key_sum[rows[p], pair(h)] += to_key[h, p] + to_key[h + 1, p]
+                for h in heads:
+                    query_sum[own(h), lows[p] :] += to_query[h, p]
             return 0
 
         first = lax.div(segment[step * BLOCK], BLOCK)
-        lax.fori_loop(first, step + 1, visit, 0)
+        lax.fori_loop(first, step, visit, 0)
+        visit(step, 0)
         low_query[here, :] = (query_sum[...] * HEAD_DIM**-0.5).astype(BF).T
         return 0
 

time: 202 us -> 198 us (0.980)
  Pallas kernels: 105 us -> 130 us
  waiting for transfers between devices: 40.9 us -> 16.7 us
  starting transfers between devices: 40.1 us -> 36.5 us
    ppermute x34, waiting for transfers between devices: 40.9 us -> 16.7 us  [swap(): return lax.ppermute(values, axis, [(i, i ^ bits) for i in range(count)])]
    pallas_call x1, Pallas kernels: 18.3 us -> 32.9 us  [attend_back(): pl.pallas_call(attend_back_kernel, in_specs=[smem, smem, vmem] + [ANYWHER...]
    pallas_call x1, Pallas kernels: 13 us -> 23.2 us  [attend(): pl.pallas_call(attend_kernel, in_specs=[smem, vmem, ANYWHERE, ANYWHERE, A...]
    ppermute x34, starting transfers between devices: 40.1 us -> 36.5 us  [swap(): return lax.ppermute(values, axis, [(i, i ^ bits) for i in range(count)])]
  transfers between devices with their start and end apart: 34 -> 34, of which waited for: 11 -> 8; matrix products, arithmetic and copies ran while one was open for 2% -> 2% of each run, Pallas kernels for 27% -> 40%
where the time goes in v4:
time: 198 us; the launch traced here: 197 us
  Pallas kernels  130 us (66%)
  starting transfers between devices  36.5 us (18%)
  waiting for transfers between devices  16.7 us (8%)
  local copies, waits for them, and re-layouts  12 us (6%)
    pallas_call x1, Pallas kernels, feed_forward(): pl.pallas_call(feed_kernel, grid=(length // tile,), in_specs=[pl.BlockSpe...  43.6 us
    ppermute x34, starting transfers between devices, swap(): return lax.ppermute(values, axis, [(i, i ^ bits) for i in range(count)])  36.5 us
    pallas_call x1, Pallas kernels, attend_back(): pl.pallas_call(attend_back_kernel, in_specs=[smem, smem, vmem] + [ANYWHER...  32.9 us
    pallas_call x1, Pallas kernels, attend(): pl.pallas_call(attend_kernel, in_specs=[smem, vmem, ANYWHERE, ANYWHERE, A...  23.2 us
    ppermute x34, waiting for transfers between devices, swap(): return lax.ppermute(values, axis, [(i, i ^ bits) for i in range(count)])  16.7 us
    pallas_call x2, Pallas kernels, finish(): pl.pallas_call(finish_kernel, grid=(count,), in_specs=[by_rows] * 3 + [wh...  12.3 us
    unnamed x68, local copies, waits for them, and re-layouts  10.7 us
    pallas_call x1, Pallas kernels, project(): pl.pallas_call(project_kernel, grid=(length // tile,), in_specs=[pl.Block...  8.3 us
  transfers between devices with their start and end apart: 34, of which 8 were waited for; matrix products, arithmetic and copies ran while one was open for 2% of the time, Pallas kernels for 40%

profile of v4, /device:TPU:0, one launch (start us, length us, event | category | flops | bytes accessed | tf_op | source)
XLA Modules:
  0.0 197.5 jit_solution(14799037108720167830)
XLA Ops:
  0.7 2.1 %pack.1 = (bf16[16,1664]{1,0:T(8,128)(2,1)}, bf16[16,5632]{1,0:T(8,128)(2,1)}) custom-call(s32[1]{0:T(128)} %bitcast.device.me.refs_1_.refs_3_, bf16[16]{0:T(256)(128)(2,1)} %gain_one.1, bf16[16]{0:T(256)(128)(2,1)} %gain_two.1, bf16[16]{0:T(256)(128)(2,1)} %refs_2_.1, bf16[16]{0:T(256)(128)(2,1)} %refs_3_.1, bf16[16,512]{1,0:T(8,128)(2,1)} %query.1, ...), custom_call_target="tpu_custom_call" | custom-call | tf_op jit(solution)/shard_map/pack/pallas_call | solution.py:886
  2.8 3.0 %collective-permute-start = (bf16[16,1664]{1,0:T(8,128)(2,1)}, bf16[16,1664]{1,0:T(8,128)(2,1)S(1)}, u32[]{:S(2)}, u32[]{:S(2)}) collective-permute-start(bf16[16,1664]{1,0:T(8,128)(2,1)} %get-tuple-element.77), channel_id=1, source_target_pairs={{0,1},{1,0},{2,3},{3,2},{4,5},{5,4},{6,7},{7,6},{8,9},{9,8},{10,11... | collective-permute-start | bytes 159752 | tf_op jit(solution)/shard_map/ppermute | solution.py:767
  5.8 2.6 %collective-permute-start.1 = (bf16[16,1664]{1,0:T(8,128)(2,1)}, bf16[16,1664]{1,0:T(8,128)(2,1)S(1)}, u32[]{:S(2)}, u32[]{:S(2)}) collective-permute-start(bf16[16,1664]{1,0:T(8,128)(2,1)} %get-tuple-element.77), channel_id=1, source_target_pairs={{0,2},{1,3},{2,0},{3,1},{4,6},{5,7},{6,4},{7,5},{8,10},{9,11},{10,... | collective-permute-start | bytes 159752 | tf_op jit(solution)/shard_map/ppermute | solution.py:767
  8.4 0.9 collective-permute-start.10
  9.3 3.5 %collective-permute-start.11 = (bf16[16,5632]{1,0:T(8,128)(2,1)}, bf16[16,5632]{1,0:T(8,128)(2,1)S(1)}, u32[]{:S(2)}, u32[]{:S(2)}) collective-permute-start(bf16[16,5632]{1,0:T(8,128)(2,1)} %get-tuple-element.85), channel_id=1, source_target_pairs={{0,2},{1,3},{2,0},{3,1},{4,6},{5,7},{6,4},{7,5},{8,10},{9,11},{10,... | collective-permute-start | bytes 540680 | tf_op jit(solution)/shard_map/ppermute | solution.py:767
  12.8 0.8 constant_dynamic-update-slice_fusion.3
  13.6 0.9 constant_dynamic-update-slice_fusion.7
  14.5 0.6 pad_add_fusion.order
  15.1 1.3 reshape.55.segment_row
  16.5 1.8 collective-permute-start.3
  18.2 1.5 collective-permute-start.4
  19.8 1.9 collective-permute-start.5
  21.6 4.9 %collective-permute-done.11 = bf16[16,5632]{1,0:T(8,128)(2,1)S(1)} collective-permute-done((bf16[16,5632]{1,0:T(8,128)(2,1)}, bf16[16,5632]{1,0:T(8,128)(2,1)S(1)}, u32[]{:S(2)}, u32[]{:S(2)}) %collective-permute-start.11) | collective-permute-done | bytes 180256 | tf_op jit(solution)/shard_map/ppermute | solution.py:767
  26.5 0.6 collective-permute-start.7
  27.1 1.2 collective-permute-done.4.refs_2_
  28.3 0.5 collective-permute-start.9
  28.8 0.4 collective-permute-start.13
  29.3 2.0 %collective-permute-start.14 = (bf16[64,5632]{1,0:T(8,128)(2,1)S(1)}, bf16[64,5632]{1,0:T(8,128)(2,1)S(1)}, u32[]{:S(2)}, u32[]{:S(2)}) collective-permute-start(bf16[64,5632]{1,0:T(8,128)(2,1)S(1)} %constant_dynamic-update-slice_fusion.4.refs_0_), channel_id=1, source_target_pairs={{0,16},{4,20},{8,24},{12,28},{16,0},{20,4},{24,8},{28,12},{1,17},{... | collective-permute-start | bytes 2162696 | tf_op jit(solution)/shard_map/ppermute | solution.py:767
  31.3 1.1 collective-permute-start.15
  32.4 0.1 collective-permute-start.16
  32.5 0.6 copy-done.30
  33.1 8.3 %project.1 = (bf16[1536,512]{1,0:T(8,128)(2,1)}, bf16[512,1536]{1,0:T(8,128)(2,1)}, bf16[1536,512]{1,0:T(8,128)(2,1)}, bf16[1536,512]{1,0:T(8,128)(2,1)}, bf16[1...) custom-call(s32[32]{0:T(128)} %pad_add_fusion.order, ...), custom_call_target="tpu_custom_call" | custom-call | flops 2415919104 | bytes 12582912 | tf_op jit(solution)/shard_map/project/pallas_call | solution.py:104
  41.5 23.2 %attend.1 = (f32[1536,512]{1,0:T(8,128)}, f32[8,1536]{1,0:T(8,128)}) custom-call(s32[1536]{0:T(1024)} %segment.3, s32[1,1536]{1,0:T(1,128)} %reshape.55.segment_row, bf16[1536,512]{1,0:T(8,128)(2,1)} %get-tuple-element.80.query_in, bf16[1536,512]{1,0:T(8,128)(2,1)} %get-tuple-element.81.key_in, bf16[512,1536]{1,0:T(8,128)(2,1)} %get-tuple-element.82.value_t_in), custom_call_target="tpu_custom_call" | custom-call | flops 9663676416 | bytes 6291456 | tf_op jit(solution)/shard_map/attend/pallas_call | solution.py:243
  64.7 0.8 copy-done.11
  65.5 0.5 collective-permute-start.18
  66.0 0.1 collective-permute-start.19
  66.1 1.6 collective-permute-done.17.refs_5_
  67.7 1.0 collective-permute-done.18.refs_6_
  68.8 1.0 collective-permute-done.19.refs_7_
  69.8 0.9 copy-done.24
  70.7 43.6 %feed_forward.1 = (bf16[1536,512]{1,0:T(8,128)(2,1)}, f32[1536,512]{1,0:T(8,128)}, bf16[1536,512]{1,0:T(8,128)(2,1)}, bf16[1536,512]{1,0:T(8,128)(2,1)}, f32[8,1...) custom-call(s32[1]{0:T(128)} %bitcast.device.me.refs_1_.refs_3_, ...), custom_call_target="tpu_custom_call" | custom-call | flops 26575110144 | bytes 25165824 | tf_op jit(solution)/shard_map/feed_forward/pallas_call | solution.py:594
  114.3 0.2 collective-permute-start.20
  114.5 5.7 %collective-permute-done.20.refs_0_ = bf16[16,192,512]{2,1,0:T(8,128)(2,1)S(1)} collective-permute-done((bf16[16,192,512]{2,1,0:T(8,128)(2,1)}, bf16[16,192,512]{2,1,0:T(8,128)(2,1)S(1)}, u32[]{:S(2)}, u32[]{:S(2)}) %collective-permute-start.20) | collective-permute-done | bytes 3145760 | tf_op jit(solution)/shard_map/ppermute | solution.py:767
  120.2 1.9 copy-done
  122.1 1.1 add_split.4
  123.3 0.9 copy-done.3
  124.1 0.1 collective-permute-start.21
  124.3 2.3 %collective-permute-start.22 = (bf16[4,192,512]{2,1,0:T(8,128)(2,1)S(1)}, bf16[4,192,512]{2,1,0:T(8,128)(2,1)S(1)}, u32[]{:S(2)}, u32[]{:S(2)}) collective-permute-start(bf16[4,192,512]{2,1,0:T(8,128)(2,1)S(1)} %get-tuple-element.108), channel_id=1, source_target_pairs={{0,16},{4,20},{8,24},{12,28},{16,0},{20,4},{24,8},{28,12},{1,17},{... | collective-permute-start | bytes 2359304 | tf_op jit(solution)/shard_map/ppermute | solution.py:767
  126.6 1.0 collective-permute-start.23
  127.6 32.9 %attend_back.1 = (bf16[1536,512]{1,0:T(8,128)(2,1)}, bf16[1536,512]{1,0:T(8,128)(2,1)}, bf16[1536,512]{1,0:T(8,128)(2,1)}, bf16[16,16,1536]{2,1,0:T(8,128)(2,1)}, bf16[16,16,1536]{2,1,0:T(8,128)(2,1)}) custom-call(s32[1]{0:T(128)} %bitcast.device.me.refs_1_.refs_3_, s32[1536]{0:T(1024)} %segment.3, s32[1,1536]{1,0:T(1,128)} %reshape.55.segment_row, ...), custom_call_target="tpu_custom_call" | custom-call | flops 24159191040 | bytes 8388608 | tf_op jit(solution)/shard_map/attend_back/pallas_call | solution.py:400
  160.5 0.5 collective-permute-done.22.refs_2_.refs_1_
  161.0 0.1 collective-permute-start.24
  161.1 1.0 copy-done.4
  162.2 1.4 add_split.5
  163.6 1.2 add_split.6
  164.9 0.7 copy-done.5
  165.5 1.5 collective-permute-start.25
  167.0 0.6 pad_add_fusion.1.device
  167.6 2.9 %collective-permute-start.33 = (bf16[1,192,512]{2,1,0:T(8,128)(2,1)S(1)}, bf16[1,192,512]{2,1,0:T(8,128)(2,1)S(1)}, u32[]{:S(2)}, u32[]{:S(2)}) collective-permute-start(bf16[1,192,512]{2,1,0:T(8,128)(2,1)S(1)} %get-tuple-element.124), channel_id=1, source_target_pairs={{0,3},{1,2},{2,1},{3,0},{4,7},{5,6},{6,5},{7,4},{8,11},{9,10},{10,... | collective-permute-start | bytes 589832 | tf_op jit(solution)/shard_map/ppermute | solution.py:767
  170.5 1.5 collective-permute-start.32
  172.0 0.6 collective-permute-start.26
  172.6 1.4 collective-permute-start.27
  174.0 7.2 %finish.2 = (f32[1536,512]{1,0:T(8,128)}, f32[8,128]{1,0:T(8,128)}) custom-call(bf16[1536,512]{1,0:T(8,128)(2,1)} %tokens.7, bf16[1536,512]{1,0:T(8,128)(2,1)} %get-tuple-element.91.zeta_one_low, f32[1536,512]{1,0:T(8,128)} %get-tuple-element.92.grad_middle, bf16[512,1536]{1,0:T(8,128)(2,1)} %get-tuple-element.93.weights, ...), custom_call_target="tpu_custom_call" | custom-call | flops 2147483648 | bytes 10485760 | tf_op jit(solution)/shard_map/finish/pallas_call | solution.py:660
  181.2 0.7 collective-permute-done.26.refs_1_
  181.9 0.7 copy-done.12
  182.6 0.4 add_split.7
  183.0 0.6 copy-done.10
  183.6 1.0 collective-permute-start.28
  184.6 2.6 %collective-permute-start.29 = (bf16[1,16,1536]{2,1,0:T(8,128)(2,1)S(1)}, bf16[1,16,1536]{2,1,0:T(8,128)(2,1)S(1)}, u32[]{:S(2)}, u32[]{:S(2)}) collective-permute-start(bf16[1,16,1536]{2,1,0:T(8,128)(2,1)S(1)} %get-tuple-element.120), channel_id=1, source_target_pairs={{0,2},{1,3},{2,0},{3,1},{4,6},{5,7},{6,4},{7,5},{8,10},{9,11},{10,... | collective-permute-start | bytes 147464 | tf_op jit(solution)/shard_map/ppermute | solution.py:767
  187.2 0.7 collective-permute-start.30
  188.0 5.1 %finish.3 = (f32[1536,512]{1,0:T(8,128)}, f32[8,128]{1,0:T(8,128)}) custom-call(bf16[1536,512]{1,0:T(8,128)(2,1)} %tokens.7, bf16[1536,512]{1,0:T(8,128)(2,1)} %get-tuple-element.91.zeta_one_low, f32[1536,512]{1,0:T(8,128)} %get-tuple-element.92.grad_middle, bf16[512,1536]{1,0:T(8,128)(2,1)} %get-tuple-element.93.weights, ...), custom_call_target="tpu_custom_call", output_to_operand_aliasing={{0}: (10, {})} | custom-call | flops 1073741824 | bytes 5242880 | tf_op jit(solution)/shard_map/finish/pallas_call | solution.py:660
  193.2 0.6 copy-done.14
  193.8 0.1 copy-done.15
  194.0 3.3 %close.1 = (f32[16,512]{1,0:T(8,128)}, f32[16,512]{1,0:T(8,128)}, f32[16,512]{1,0:T(8,128)}, f32[16,512]{1,0:T(8,128)}, f32[16,512]{1,0:T(8,128)}, /*index=5*/f3...) custom-call(s32[2]{0:T(128)} %pad_add_fusion.1.device, ...), custom_call_target="tpu_custom_call" | custom-call | tf_op jit(solution)/shard_map/close/pallas_call | solution.py:751
  (92 shorter events, 0.4 us)
Async XLA Ops:
  2.8 13.6 %collective-permute-start = (bf16[16,1664]{1,0:T(8,128)(2,1)}, bf16[16,1664]{1,0:T(8,128)(2,1)S(1)}, u32[]{:S(2)}, u32[]{:S(2)}) collective-permute-start(bf16[16,1664]{1,0:T(8,128)(2,1)} %get-tuple-element.77), channel_id=1, source_target_pairs={{0,1},{1,0},{2,3},{3,2},{4,5},{5,4},{6,7},{7,6},{8,9},{9,8},{10,11... | collective-permute-start | bytes 159752 | tf_op jit(solution)/shard_map/ppermute | solution.py:767
  5.8 10.6 %collective-permute-start.1 = (bf16[16,1664]{1,0:T(8,128)(2,1)}, bf16[16,1664]{1,0:T(8,128)(2,1)S(1)}, u32[]{:S(2)}, u32[]{:S(2)}) collective-permute-start(bf16[16,1664]{1,0:T(8,128)(2,1)} %get-tuple-element.77), channel_id=1, source_target_pairs={{0,2},{1,3},{2,0},{3,1},{4,6},{5,7},{6,4},{7,5},{8,10},{9,11},{10,... | collective-permute-start | bytes 159752 | tf_op jit(solution)/shard_map/ppermute | solution.py:767
  8.4 8.1 %collective-permute-start.2 = (bf16[16,1664]{1,0:T(8,128)(2,1)}, bf16[16,1664]{1,0:T(8,128)(2,1)S(1)}, u32[]{:S(2)}, u32[]{:S(2)}) collective-permute-start(bf16[16,1664]{1,0:T(8,128)(2,1)} %get-tuple-element.77), channel_id=1, source_target_pairs={{0,3},{1,2},{2,1},{3,0},{4,7},{5,6},{6,5},{7,4},{8,11},{9,10},{10,... | collective-permute-start | bytes 159752 | tf_op jit(solution)/shard_map/ppermute | solution.py:767
  8.4 11.4 %collective-permute-start.10 = (bf16[16,5632]{1,0:T(8,128)(2,1)}, bf16[16,5632]{1,0:T(8,128)(2,1)S(1)}, u32[]{:S(2)}, u32[]{:S(2)}) collective-permute-start(bf16[16,5632]{1,0:T(8,128)(2,1)} %get-tuple-element.85), channel_id=1, source_target_pairs={{0,1},{1,0},{2,3},{3,2},{4,5},{5,4},{6,7},{7,6},{8,9},{9,8},{10,11... | collective-permute-start | bytes 540680 | tf_op jit(solution)/shard_map/ppermute | solution.py:767
  9.3 17.2 %collective-permute-start.11 = (bf16[16,5632]{1,0:T(8,128)(2,1)}, bf16[16,5632]{1,0:T(8,128)(2,1)S(1)}, u32[]{:S(2)}, u32[]{:S(2)}) collective-permute-start(bf16[16,5632]{1,0:T(8,128)(2,1)} %get-tuple-element.85), channel_id=1, source_target_pairs={{0,2},{1,3},{2,0},{3,1},{4,6},{5,7},{6,4},{7,5},{8,10},{9,11},{10,... | collective-permute-start | bytes 540680 | tf_op jit(solution)/shard_map/ppermute | solution.py:767
  16.4 12.4 %collective-permute-start.12 = (bf16[16,5632]{1,0:T(8,128)(2,1)}, bf16[16,5632]{1,0:T(8,128)(2,1)S(1)}, u32[]{:S(2)}, u32[]{:S(2)}) collective-permute-start(bf16[16,5632]{1,0:T(8,128)(2,1)} %get-tuple-element.85), channel_id=1, source_target_pairs={{0,3},{1,2},{2,1},{3,0},{4,7},{5,6},{6,5},{7,4},{8,11},{9,10},{10,... | collective-permute-start | bytes 540680 | tf_op jit(solution)/shard_map/ppermute | solution.py:767
  16.5 16.7 %copy-start.20 = (bf16[64,1664]{1,0:T(8,128)(2,1)}, bf16[64,1664]{1,0:T(8,128)(2,1)S(1)}, u32[]{:S(2)}) copy-start(bf16[64,1664]{1,0:T(8,128)(2,1)S(1)} %constant_dynamic-update-slice_fusion.refs_0_) | copy-start | bytes 638980
  16.5 10.0 %collective-permute-start.3 = (bf16[64,1664]{1,0:T(8,128)(2,1)S(1)}, bf16[64,1664]{1,0:T(8,128)(2,1)S(1)}, u32[]{:S(2)}, u32[]{:S(2)}) collective-permute-start(bf16[64,1664]{1,0:T(8,128)(2,1)S(1)} %constant_dynamic-update-slice_fusion.refs_0_), channel_id=1, source_target_pairs={{0,8},{4,12},{8,0},{12,4},{16,24},{20,28},{24,16},{28,20},{1,9},{5... | collective-permute-start | bytes 638984 | tf_op jit(solution)/shard_map/ppermute | solution.py:767
  18.2 10.0 %collective-permute-start.4 = (bf16[64,1664]{1,0:T(8,128)(2,1)S(1)}, bf16[64,1664]{1,0:T(8,128)(2,1)S(1)}, u32[]{:S(2)}, u32[]{:S(2)}) collective-permute-start(bf16[64,1664]{1,0:T(8,128)(2,1)S(1)} %constant_dynamic-update-slice_fusion.refs_0_), channel_id=1, source_target_pairs={{0,16},{4,20},{8,24},{12,28},{16,0},{20,4},{24,8},{28,12},{1,17},{... | collective-permute-start | bytes 638984 | tf_op jit(solution)/shard_map/ppermute | solution.py:767
  19.8 8.5 %collective-permute-start.5 = (bf16[64,1664]{1,0:T(8,128)(2,1)S(1)}, bf16[64,1664]{1,0:T(8,128)(2,1)S(1)}, u32[]{:S(2)}, u32[]{:S(2)}) collective-permute-start(bf16[64,1664]{1,0:T(8,128)(2,1)S(1)} %constant_dynamic-update-slice_fusion.refs_0_), channel_id=1, source_target_pairs={{0,24},{4,28},{8,16},{12,20},{16,8},{20,12},{24,0},{28,4},{1,25},{... | collective-permute-start | bytes 638984 | tf_op jit(solution)/shard_map/ppermute | solution.py:767
  26.5 2.8 %collective-permute-start.6 = (bf16[64,1664]{1,0:T(8,128)(2,1)S(1)}, bf16[64,1664]{1,0:T(8,128)(2,1)S(1)}, u32[]{:S(2)}, u32[]{:S(2)}) collective-permute-start(bf16[64,1664]{1,0:T(8,128)(2,1)S(1)} %constant_dynamic-update-slice_fusion.refs_0_), channel_id=1, source_target_pairs={{0,4},{4,0},{8,12},{12,8},{16,20},{20,16},{24,28},{28,24},{1,5},{5... | collective-permute-start | bytes 638984 | tf_op jit(solution)/shard_map/ppermute | solution.py:767
  26.5 6.6 %copy-start.25 = (bf16[64,1664]{1,0:T(8,128)(2,1)}, bf16[64,1664]{1,0:T(8,128)(2,1)S(1)}, u32[]{:S(2)}) copy-start(bf16[64,1664]{1,0:T(8,128)(2,1)S(1)} %collective-permute-done.3.refs_1_) | copy-start | bytes 638980
  26.5 4.8 %collective-permute-start.7 = (bf16[64,1664]{1,0:T(8,128)(2,1)S(1)}, bf16[64,1664]{1,0:T(8,128)(2,1)S(1)}, u32[]{:S(2)}, u32[]{:S(2)}) collective-permute-start(bf16[64,1664]{1,0:T(8,128)(2,1)S(1)} %collective-permute-done.3.refs_1_), channel_id=1, source_target_pairs={{0,4},{4,0},{8,12},{12,8},{16,20},{20,16},{24,28},{28,24},{1,5},{5... | collective-permute-start | bytes 638984 | tf_op jit(solution)/shard_map/ppermute | solution.py:767
  28.3 4.1 %copy-start.26 = (bf16[64,1664]{1,0:T(8,128)(2,1)}, bf16[64,1664]{1,0:T(8,128)(2,1)S(1)}, u32[]{:S(2)}) copy-start(bf16[64,1664]{1,0:T(8,128)(2,1)S(1)} %collective-permute-done.4.refs_2_) | copy-start | bytes 638980
  28.3 4.1 %collective-permute-start.8 = (bf16[64,1664]{1,0:T(8,128)(2,1)S(1)}, bf16[64,1664]{1,0:T(8,128)(2,1)S(1)}, u32[]{:S(2)}, u32[]{:S(2)}) collective-permute-start(bf16[64,1664]{1,0:T(8,128)(2,1)S(1)} %collective-permute-done.4.refs_2_), channel_id=1, source_target_pairs={{0,4},{4,0},{8,12},{12,8},{16,20},{20,16},{24,28},{28,24},{1,5},{5... | collective-permute-start | bytes 638984 | tf_op jit(solution)/shard_map/ppermute | solution.py:767
  28.3 4.1 %copy-start.27 = (bf16[64,1664]{1,0:T(8,128)(2,1)}, bf16[64,1664]{1,0:T(8,128)(2,1)S(1)}, u32[]{:S(2)}) copy-start(bf16[64,1664]{1,0:T(8,128)(2,1)S(1)} %collective-permute-done.5.refs_3_) | copy-start | bytes 638980
  28.3 4.8 %collective-permute-start.9 = (bf16[64,1664]{1,0:T(8,128)(2,1)S(1)}, bf16[64,1664]{1,0:T(8,128)(2,1)}, u32[]{:S(2)}, u32[]{:S(2)}) collective-permute-start(bf16[64,1664]{1,0:T(8,128)(2,1)S(1)} %collective-permute-done.5.refs_3_), channel_id=1, source_target_pairs={{0,4},{4,0},{8,12},{12,8},{16,20},{20,16},{24,28},{28,24},{1,5},{5... | collective-permute-start | bytes 638984 | tf_op jit(solution)/shard_map/ppermute | solution.py:767
  28.8 12.6 %copy-start.19 = (bf16[64,5632]{1,0:T(8,128)(2,1)}, bf16[64,5632]{1,0:T(8,128)(2,1)S(1)}, u32[]{:S(2)}) copy-start(bf16[64,5632]{1,0:T(8,128)(2,1)S(1)} %constant_dynamic-update-slice_fusion.4.refs_0_) | copy-start | bytes 2162692
  28.8 35.9 %collective-permute-start.13 = (bf16[64,5632]{1,0:T(8,128)(2,1)S(1)}, bf16[64,5632]{1,0:T(8,128)(2,1)S(1)}, u32[]{:S(2)}, u32[]{:S(2)}) collective-permute-start(bf16[64,5632]{1,0:T(8,128)(2,1)S(1)} %constant_dynamic-update-slice_fusion.4.refs_0_), channel_id=1, source_target_pairs={{0,8},{4,12},{8,0},{12,4},{16,24},{20,28},{24,16},{28,20},{1,9},{5... | collective-permute-start | bytes 2162696 | tf_op jit(solution)/shard_map/ppermute | solution.py:767
  29.3 3.1 %copy-start.28 = (bf16[64,1664]{1,0:T(8,128)(2,1)}, bf16[64,1664]{1,0:T(8,128)(2,1)S(1)}, u32[]{:S(2)}) copy-start(bf16[64,1664]{1,0:T(8,128)(2,1)S(1)} %collective-permute-done.6.refs_4_) | copy-start | bytes 638980
  29.3 35.4 %collective-permute-start.14 = (bf16[64,5632]{1,0:T(8,128)(2,1)S(1)}, bf16[64,5632]{1,0:T(8,128)(2,1)S(1)}, u32[]{:S(2)}, u32[]{:S(2)}) collective-permute-start(bf16[64,5632]{1,0:T(8,128)(2,1)S(1)} %constant_dynamic-update-slice_fusion.4.refs_0_), channel_id=1, source_target_pairs={{0,16},{4,20},{8,24},{12,28},{16,0},{20,4},{24,8},{28,12},{1,17},{... | collective-permute-start | bytes 2162696 | tf_op jit(solution)/shard_map/ppermute | solution.py:767
  31.3 1.1 copy-start.29
  31.3 33.4 %collective-permute-start.15 = (bf16[64,5632]{1,0:T(8,128)(2,1)S(1)}, bf16[64,5632]{1,0:T(8,128)(2,1)S(1)}, u32[]{:S(2)}, u32[]{:S(2)}) collective-permute-start(bf16[64,5632]{1,0:T(8,128)(2,1)S(1)} %constant_dynamic-update-slice_fusion.4.refs_0_), channel_id=1, source_target_pairs={{0,24},{4,28},{8,16},{12,20},{16,8},{20,12},{24,0},{28,4},{1,25},{... | collective-permute-start | bytes 2162696 | tf_op jit(solution)/shard_map/ppermute | solution.py:767
  32.4 0.7 copy-start.30
  32.4 33.7 %collective-permute-start.16 = (bf16[64,5632]{1,0:T(8,128)(2,1)S(1)}, bf16[64,5632]{1,0:T(8,128)(2,1)S(1)}, u32[]{:S(2)}, u32[]{:S(2)}) collective-permute-start(bf16[64,5632]{1,0:T(8,128)(2,1)S(1)} %constant_dynamic-update-slice_fusion.4.refs_0_), channel_id=1, source_target_pairs={{0,4},{4,0},{8,12},{12,8},{16,20},{20,16},{24,28},{28,24},{1,5},{5... | collective-permute-start | bytes 2162696 | tf_op jit(solution)/shard_map/ppermute | solution.py:767
  64.7 0.8 copy-start.11
  65.5 5.2 %copy-start.7 = (bf16[64,5632]{1,0:T(8,128)(2,1)}, bf16[64,5632]{1,0:T(8,128)(2,1)S(1)}, u32[]{:S(2)}) copy-start(bf16[64,5632]{1,0:T(8,128)(2,1)S(1)} %get-tuple-element.87.refs_1_) | copy-start | bytes 2162692
  65.5 5.2 %copy-start.8 = (bf16[64,5632]{1,0:T(8,128)(2,1)}, bf16[64,5632]{1,0:T(8,128)(2,1)S(1)}, u32[]{:S(2)}) copy-start(bf16[64,5632]{1,0:T(8,128)(2,1)S(1)} %get-tuple-element.88.refs_2_) | copy-start | bytes 2162692
  65.5 5.2 %copy-start.9 = (bf16[64,5632]{1,0:T(8,128)(2,1)}, bf16[64,5632]{1,0:T(8,128)(2,1)S(1)}, u32[]{:S(2)}) copy-start(bf16[64,5632]{1,0:T(8,128)(2,1)S(1)} %get-tuple-element.89.refs_3_) | copy-start | bytes 2162692
  65.5 2.2 %collective-permute-start.17 = (bf16[64,5632]{1,0:T(8,128)(2,1)S(1)}, bf16[64,5632]{1,0:T(8,128)(2,1)S(1)}, u32[]{:S(2)}, u32[]{:S(2)}) collective-permute-start(bf16[64,5632]{1,0:T(8,128)(2,1)S(1)} %get-tuple-element.87.refs_1_), channel_id=1, source_target_pairs={{0,4},{4,0},{8,12},{12,8},{16,20},{20,16},{24,28},{28,24},{1,5},{5... | collective-permute-start | bytes 2162696 | tf_op jit(solution)/shard_map/ppermute | solution.py:767
  65.5 3.2 %collective-permute-start.18 = (bf16[64,5632]{1,0:T(8,128)(2,1)S(1)}, bf16[64,5632]{1,0:T(8,128)(2,1)S(1)}, u32[]{:S(2)}, u32[]{:S(2)}) collective-permute-start(bf16[64,5632]{1,0:T(8,128)(2,1)S(1)} %get-tuple-element.88.refs_2_), channel_id=1, source_target_pairs={{0,4},{4,0},{8,12},{12,8},{16,20},{20,16},{24,28},{28,24},{1,5},{5... | collective-permute-start | bytes 2162696 | tf_op jit(solution)/shard_map/ppermute | solution.py:767
  66.0 3.7 %collective-permute-start.19 = (bf16[64,5632]{1,0:T(8,128)(2,1)S(1)}, bf16[64,5632]{1,0:T(8,128)(2,1)S(1)}, u32[]{:S(2)}, u32[]{:S(2)}) collective-permute-start(bf16[64,5632]{1,0:T(8,128)(2,1)S(1)} %get-tuple-element.89.refs_3_), channel_id=1, source_target_pairs={{0,4},{4,0},{8,12},{12,8},{16,20},{20,16},{24,28},{28,24},{1,5},{5... | collective-permute-start | bytes 2162696 | tf_op jit(solution)/shard_map/ppermute | solution.py:767
  66.1 4.6 %copy-start.21 = (bf16[64,5632]{1,0:T(8,128)(2,1)}, bf16[64,5632]{1,0:T(8,128)(2,1)S(1)}, u32[]{:S(2)}) copy-start(bf16[64,5632]{1,0:T(8,128)(2,1)S(1)} %collective-permute-done.16.refs_4_) | copy-start | bytes 2162692
  67.7 2.1 %copy-start.22 = (bf16[64,5632]{1,0:T(8,128)(2,1)}, bf16[64,5632]{1,0:T(8,128)(2,1)S(1)}, u32[]{:S(2)}) copy-start(bf16[64,5632]{1,0:T(8,128)(2,1)S(1)} %collective-permute-done.17.refs_5_) | copy-start | bytes 2162692
  68.8 1.0 copy-start.23
  69.8 0.9 copy-start.24
  114.3 5.9 %collective-permute-start.20 = (bf16[16,192,512]{2,1,0:T(8,128)(2,1)}, bf16[16,192,512]{2,1,0:T(8,128)(2,1)S(1)}, u32[]{:S(2)}, u32[]{:S(2)}) collective-permute-start(bf16[16,192,512]{2,1,0:T(8,128)(2,1)} %bitcast.24), channel_id=1, source_target_pairs={{0,4},{4,0},{8,12},{12,8},{16,20},{20,16},{24,28},{28,24},{1,5},{5... | collective-permute-start | bytes 9437192 | tf_op jit(solution)/shard_map/ppermute | solution.py:767
  120.2 1.9 copy-start
  123.3 0.9 copy-start.3
  124.1 36.4 %collective-permute-start.21 = (bf16[4,192,512]{2,1,0:T(8,128)(2,1)S(1)}, bf16[4,192,512]{2,1,0:T(8,128)(2,1)S(1)}, u32[]{:S(2)}, u32[]{:S(2)}) collective-permute-start(bf16[4,192,512]{2,1,0:T(8,128)(2,1)S(1)} %get-tuple-element.107), channel_id=1, source_target_pairs={{0,8},{4,12},{8,0},{12,4},{16,24},{20,28},{24,16},{28,20},{1,9},{5... | collective-permute-start | bytes 2359304 | tf_op jit(solution)/shard_map/ppermute | solution.py:767
  124.3 36.8 %collective-permute-start.22 = (bf16[4,192,512]{2,1,0:T(8,128)(2,1)S(1)}, bf16[4,192,512]{2,1,0:T(8,128)(2,1)S(1)}, u32[]{:S(2)}, u32[]{:S(2)}) collective-permute-start(bf16[4,192,512]{2,1,0:T(8,128)(2,1)S(1)} %get-tuple-element.108), channel_id=1, source_target_pairs={{0,16},{4,20},{8,24},{12,28},{16,0},{20,4},{24,8},{28,12},{1,17},{... | collective-permute-start | bytes 2359304 | tf_op jit(solution)/shard_map/ppermute | solution.py:767
  126.6 34.4 %collective-permute-start.23 = (bf16[4,192,512]{2,1,0:T(8,128)(2,1)S(1)}, bf16[4,192,512]{2,1,0:T(8,128)(2,1)S(1)}, u32[]{:S(2)}, u32[]{:S(2)}) collective-permute-start(bf16[4,192,512]{2,1,0:T(8,128)(2,1)S(1)} %get-tuple-element.109), channel_id=1, source_target_pairs={{0,24},{4,28},{8,16},{12,20},{16,8},{20,12},{24,0},{28,4},{1,25},{... | collective-permute-start | bytes 2359304 | tf_op jit(solution)/shard_map/ppermute | solution.py:767
  161.0 1.1 copy-start.4
  161.0 2.6 %copy-start.1 = (bf16[16,16,1536]{2,1,0:T(8,128)(2,1)S(1)}, bf16[16,16,1536]{2,1,0:T(8,128)(2,1)}, u32[]{:S(2)}) copy-start(bf16[16,16,1536]{2,1,0:T(8,128)(2,1)} %get-tuple-element.105.own) | copy-start | bytes 2359300
  161.0 2.6 %collective-permute-start.24 = (bf16[16,16,1536]{2,1,0:T(8,128)(2,1)}, bf16[16,16,1536]{2,1,0:T(8,128)(2,1)S(1)}, u32[]{:S(2)}, u32[]{:S(2)}) collective-permute-start(bf16[16,16,1536]{2,1,0:T(8,128)(2,1)} %hold.3), channel_id=1, source_target_pairs={{0,4},{4,0},{8,12},{12,8},{16,20},{20,16},{24,28},{28,24},{1,5},{5... | collective-permute-start | bytes 2359304 | tf_op jit(solution)/shard_map/ppermute | solution.py:767
  163.6 17.6 %copy-start.2 = (bf16[1,192,512]{2,1,0:T(8,128)(2,1)}, bf16[1,192,512]{2,1,0:T(8,128)(2,1)S(1)}, u32[]{:S(2)}) copy-start(bf16[1,192,512]{2,1,0:T(8,128)(2,1)S(1)} %get-tuple-element.110.refs_1_) | copy-start | bytes 589828
  164.9 0.7 copy-start.5
  165.5 7.0 %collective-permute-start.25 = (bf16[4,16,1536]{2,1,0:T(8,128)(2,1)S(1)}, bf16[4,16,1536]{2,1,0:T(8,128)(2,1)S(1)}, u32[]{:S(2)}, u32[]{:S(2)}) collective-permute-start(bf16[4,16,1536]{2,1,0:T(8,128)(2,1)S(1)} %get-tuple-element.112), channel_id=1, source_target_pairs={{0,8},{4,12},{8,0},{12,4},{16,24},{20,28},{24,16},{28,20},{1,9},{5... | collective-permute-start | bytes 589832 | tf_op jit(solution)/shard_map/ppermute | solution.py:767
  167.6 19.7 %collective-permute-start.33 = (bf16[1,192,512]{2,1,0:T(8,128)(2,1)S(1)}, bf16[1,192,512]{2,1,0:T(8,128)(2,1)S(1)}, u32[]{:S(2)}, u32[]{:S(2)}) collective-permute-start(bf16[1,192,512]{2,1,0:T(8,128)(2,1)S(1)} %get-tuple-element.124), channel_id=1, source_target_pairs={{0,3},{1,2},{2,1},{3,0},{4,7},{5,6},{6,5},{7,4},{8,11},{9,10},{10,... | collective-permute-start | bytes 589832 | tf_op jit(solution)/shard_map/ppermute | solution.py:767
  170.5 22.6 %collective-permute-start.31 = (bf16[1,192,512]{2,1,0:T(8,128)(2,1)S(1)}, bf16[1,192,512]{2,1,0:T(8,128)(2,1)S(1)}, u32[]{:S(2)}, u32[]{:S(2)}) collective-permute-start(bf16[1,192,512]{2,1,0:T(8,128)(2,1)S(1)} %get-tuple-element.122), channel_id=1, source_target_pairs={{0,1},{1,0},{2,3},{3,2},{4,5},{5,4},{6,7},{7,6},{8,9},{9,8},{10,11... | collective-permute-start | bytes 589832 | tf_op jit(solution)/shard_map/ppermute | solution.py:767
  170.5 22.6 %collective-permute-start.32 = (bf16[1,192,512]{2,1,0:T(8,128)(2,1)S(1)}, bf16[1,192,512]{2,1,0:T(8,128)(2,1)S(1)}, u32[]{:S(2)}, u32[]{:S(2)}) collective-permute-start(bf16[1,192,512]{2,1,0:T(8,128)(2,1)S(1)} %get-tuple-element.123), channel_id=1, source_target_pairs={{0,2},{1,3},{2,0},{3,1},{4,6},{5,7},{6,4},{7,5},{8,10},{9,11},{10,... | collective-permute-start | bytes 589832 | tf_op jit(solution)/shard_map/ppermute | solution.py:767
  172.0 9.9 %collective-permute-start.26 = (bf16[4,16,1536]{2,1,0:T(8,128)(2,1)S(1)}, bf16[4,16,1536]{2,1,0:T(8,128)(2,1)S(1)}, u32[]{:S(2)}, u32[]{:S(2)}) collective-permute-start(bf16[4,16,1536]{2,1,0:T(8,128)(2,1)S(1)} %get-tuple-element.113), channel_id=1, source_target_pairs={{0,16},{4,20},{8,24},{12,28},{16,0},{20,4},{24,8},{28,12},{1,17},{... | collective-permute-start | bytes 589832 | tf_op jit(solution)/shard_map/ppermute | solution.py:767
  172.6 9.3 %collective-permute-start.27 = (bf16[4,16,1536]{2,1,0:T(8,128)(2,1)S(1)}, bf16[4,16,1536]{2,1,0:T(8,128)(2,1)S(1)}, u32[]{:S(2)}, u32[]{:S(2)}) collective-permute-start(bf16[4,16,1536]{2,1,0:T(8,128)(2,1)S(1)} %get-tuple-element.114), channel_id=1, source_target_pairs={{0,24},{4,28},{8,16},{12,20},{16,8},{20,12},{24,0},{28,4},{1,25},{... | collective-permute-start | bytes 589832 | tf_op jit(solution)/shard_map/ppermute | solution.py:767
  174.0 7.9 %copy-start.6 = (bf16[4,16,1536]{2,1,0:T(8,128)(2,1)S(1)}, bf16[4,16,1536]{2,1,0:T(8,128)(2,1)}, u32[]{:S(2)}) copy-start(bf16[4,16,1536]{2,1,0:T(8,128)(2,1)} %copy-done.5) | copy-start | bytes 589828
  181.9 0.7 copy-start.12
  183.6 9.6 %collective-permute-start.28 = (bf16[1,16,1536]{2,1,0:T(8,128)(2,1)S(1)}, bf16[1,16,1536]{2,1,0:T(8,128)(2,1)S(1)}, u32[]{:S(2)}, u32[]{:S(2)}) collective-permute-start(bf16[1,16,1536]{2,1,0:T(8,128)(2,1)S(1)} %get-tuple-element.119), channel_id=1, source_target_pairs={{0,1},{1,0},{2,3},{3,2},{4,5},{5,4},{6,7},{7,6},{8,9},{9,8},{10,11... | collective-permute-start | bytes 147464 | tf_op jit(solution)/shard_map/ppermute | solution.py:767
  184.6 8.6 %collective-permute-start.29 = (bf16[1,16,1536]{2,1,0:T(8,128)(2,1)S(1)}, bf16[1,16,1536]{2,1,0:T(8,128)(2,1)S(1)}, u32[]{:S(2)}, u32[]{:S(2)}) collective-permute-start(bf16[1,16,1536]{2,1,0:T(8,128)(2,1)S(1)} %get-tuple-element.120), channel_id=1, source_target_pairs={{0,2},{1,3},{2,0},{3,1},{4,6},{5,7},{6,4},{7,5},{8,10},{9,11},{10,... | collective-permute-start | bytes 147464 | tf_op jit(solution)/shard_map/ppermute | solution.py:767
  187.2 5.9 %copy-start.13 = (bf16[1,192,512]{2,1,0:T(8,128)(2,1)}, bf16[1,192,512]{2,1,0:T(8,128)(2,1)S(1)}, u32[]{:S(2)}) copy-start(bf16[1,192,512]{2,1,0:T(8,128)(2,1)S(1)} %collective-permute-done.33) | copy-start | bytes 589828
  187.2 6.0 %collective-permute-start.30 = (bf16[1,16,1536]{2,1,0:T(8,128)(2,1)S(1)}, bf16[1,16,1536]{2,1,0:T(8,128)(2,1)S(1)}, u32[]{:S(2)}, u32[]{:S(2)}) collective-permute-start(bf16[1,16,1536]{2,1,0:T(8,128)(2,1)S(1)} %get-tuple-element.121), channel_id=1, source_target_pairs={{0,3},{1,2},{2,1},{3,0},{4,7},{5,6},{6,5},{7,4},{8,11},{9,10},{10,... | collective-permute-start | bytes 147464 | tf_op jit(solution)/shard_map/ppermute | solution.py:767
  193.1 0.7 copy-start.14
  193.2 0.7 copy-start.15
  193.2 0.7 copy-start.16
  193.2 0.7 copy-start.17
  193.2 0.8 copy-start.18
  (1 other events, 0.6 us)

commit v5 on v4

--- a/solution.py
+++ b/solution.py
@@ -706,13 +706,21 @@
     grad = tile(2)
     grad_gate_ffn[...] = grad
     other = row_sum(gate_ffn[...], grad)
-    order = in_order(width)
     tiles = [tile(3 + k) for k in range(4)]
+    spread = jnp.concatenate(
+        [
+            jnp.concatenate([t[:, part * 128 : (part + 1) * 128] for t in tiles], axis=1)
+            for part in range(4)
+        ],
+        axis=0,
+    )
+    high = spread.astype(BF)
+    low = (spread - high.astype(F32)).astype(BF)
+    moved = dot_t(jnp.concatenate([high, low], axis=0), in_order(width))
+    moved = moved[: 4 * ROWS] + moved[4 * ROWS :]
     for part in range(4):
         columns = pl.ds(part * width, width)
-        grad = jnp.concatenate([t[:, part * 128 : (part + 1) * 128] for t in tiles], axis=1)
-        high = grad.astype(BF)
-        grad = dot_t(high, order) + dot_t((grad - high.astype(F32)).astype(BF), order)
+        grad = moved[part * ROWS : (part + 1) * ROWS]
         grad_in[:, columns] = grad
         other = other + row_sum(w_in[:, columns], grad)
     for group in range(4):
@@ -872,11 +880,13 @@
     tile = lambda k: pl.ds(k * width, width)
     for k, shard in enumerate((w_output, gate_attn, gate_ffn)):
         rest[:, tile(k)] = shard[...]
-    order = in_order(width)
+    moved = dot(jnp.concatenate([w_in[:, tile(part)] for part in range(4)], axis=0), in_order(width))
+    moved = moved.astype(BF)
     for part in range(4):
-        moved = dot(w_in[:, tile(part)], order).astype(BF)
         for group in range(4):
-            rest[:, pl.ds((3 + group) * width + part * 128, 128)] = moved[:, group * 128 : (group + 1) * 128]
+            rest[:, pl.ds((3 + group) * width + part * 128, 128)] = moved[
+                part * ROWS : (part + 1) * ROWS, group * 128 : (group + 1) * 128
+            ]
     for group in range(4):
         rest[:, tile(7 + group)] = w_out[group * ROWS : (group + 1) * ROWS, :]
 

time: 198 us -> 197 us (level)
  Pallas kernels: 130 us -> 99.8 us
  waiting for transfers between devices: 16.7 us -> 44.4 us
    ppermute x34, waiting for transfers between devices: 16.7 us -> 44.4 us  [swap(): return lax.ppermute(values, axis, [(i, i ^ bits) for i in range(count)])]
    pallas_call x1, Pallas kernels: 32.9 us -> 16.4 us  [attend_back(): pl.pallas_call(attend_back_kernel, in_specs=[smem, smem, vmem] + [ANYWHER...]
    pallas_call x1, Pallas kernels: 23.2 us -> 10.6 us  [attend(): pl.pallas_call(attend_kernel, in_specs=[smem, vmem, ANYWHERE, ANYWHERE, A...]
  transfers between devices with their start and end apart: 34 -> 34, of which waited for: 8 -> 12; matrix products, arithmetic and copies ran while one was open for 2% -> 2% of each run, Pallas kernels for 40% -> 25%
where the time goes in v5:
time: 197 us
  Pallas kernels  99.8 us (51%)
  waiting for transfers between devices  44.4 us (23%)
  starting transfers between devices  38.1 us (19%)
  local copies, waits for them, and re-layouts  12 us (6%)
    ppermute x34, waiting for transfers between devices, swap(): return lax.ppermute(values, axis, [(i, i ^ bits) for i in range(count)])  44.4 us
    pallas_call x1, Pallas kernels, feed_forward(): pl.pallas_call(feed_kernel, grid=(length // tile,), in_specs=[pl.BlockSpe...  43.6 us
    ppermute x34, starting transfers between devices, swap(): return lax.ppermute(values, axis, [(i, i ^ bits) for i in range(count)])  38.1 us
    pallas_call x1, Pallas kernels, attend_back(): pl.pallas_call(attend_back_kernel, in_specs=[smem, smem, vmem] + [ANYWHER...  16.4 us
    pallas_call x2, Pallas kernels, finish(): pl.pallas_call(finish_kernel, grid=(count,), in_specs=[by_rows] * 3 + [wh...  12.3 us
    unnamed x68, local copies, waits for them, and re-layouts  10.7 us
    pallas_call x1, Pallas kernels, attend(): pl.pallas_call(attend_kernel, in_specs=[smem, vmem, ANYWHERE, ANYWHERE, A...  10.6 us
    pallas_call x1, Pallas kernels, project(): pl.pallas_call(project_kernel, grid=(length // tile,), in_specs=[pl.Block...  8.3 us
  transfers between devices with their start and end apart: 34, of which 12 were waited for; matrix products, arithmetic and copies ran while one was open for 2% of the time, Pallas kernels for 25%

profile of v5, /device:TPU:0, one launch (start us, length us, event | category | flops | bytes accessed | tf_op | source)
XLA Modules:
  0.0 196.6 jit_solution(397765295686578519)
XLA Ops:
  0.7 1.9 pack.1
  2.6 3.0 %collective-permute-start = (bf16[16,1664]{1,0:T(8,128)(2,1)}, bf16[16,1664]{1,0:T(8,128)(2,1)S(1)}, u32[]{:S(2)}, u32[]{:S(2)}) collective-permute-start(bf16[16,1664]{1,0:T(8,128)(2,1)} %get-tuple-element.77), channel_id=1, source_target_pairs={{0,1},{1,0},{2,3},{3,2},{4,5},{5,4},{6,7},{7,6},{8,9},{9,8},{10,11... | collective-permute-start | bytes 159752 | tf_op jit(solution)/shard_map/ppermute | solution.py:775
  5.6 2.6 %collective-permute-start.1 = (bf16[16,1664]{1,0:T(8,128)(2,1)}, bf16[16,1664]{1,0:T(8,128)(2,1)S(1)}, u32[]{:S(2)}, u32[]{:S(2)}) collective-permute-start(bf16[16,1664]{1,0:T(8,128)(2,1)} %get-tuple-element.77), channel_id=1, source_target_pairs={{0,2},{1,3},{2,0},{3,1},{4,6},{5,7},{6,4},{7,5},{8,10},{9,11},{10,... | collective-permute-start | bytes 159752 | tf_op jit(solution)/shard_map/ppermute | solution.py:775
  8.2 0.9 collective-permute-start.10
  9.1 3.5 %collective-permute-start.11 = (bf16[16,5632]{1,0:T(8,128)(2,1)}, bf16[16,5632]{1,0:T(8,128)(2,1)S(1)}, u32[]{:S(2)}, u32[]{:S(2)}) collective-permute-start(bf16[16,5632]{1,0:T(8,128)(2,1)} %get-tuple-element.85), channel_id=1, source_target_pairs={{0,2},{1,3},{2,0},{3,1},{4,6},{5,7},{6,4},{7,5},{8,10},{9,11},{10,... | collective-permute-start | bytes 540680 | tf_op jit(solution)/shard_map/ppermute | solution.py:775
  12.6 0.8 constant_dynamic-update-slice_fusion.3
  13.4 0.9 constant_dynamic-update-slice_fusion.7
  14.3 0.6 pad_add_fusion.order
  14.9 1.3 reshape.55.segment_row
  16.3 1.8 collective-permute-start.3
  18.1 1.5 collective-permute-start.4
  19.6 1.8 collective-permute-start.5
  21.5 4.9 %collective-permute-done.11 = bf16[16,5632]{1,0:T(8,128)(2,1)S(1)} collective-permute-done((bf16[16,5632]{1,0:T(8,128)(2,1)}, bf16[16,5632]{1,0:T(8,128)(2,1)S(1)}, u32[]{:S(2)}, u32[]{:S(2)}) %collective-permute-start.11) | collective-permute-done | bytes 180256 | tf_op jit(solution)/shard_map/ppermute | solution.py:775
  26.3 0.6 collective-permute-start.7
  26.9 1.2 collective-permute-done.4.refs_2_
  28.1 0.5 collective-permute-start.9
  28.7 0.4 collective-permute-start.13
  29.1 2.0 %collective-permute-start.14 = (bf16[64,5632]{1,0:T(8,128)(2,1)S(1)}, bf16[64,5632]{1,0:T(8,128)(2,1)S(1)}, u32[]{:S(2)}, u32[]{:S(2)}) collective-permute-start(bf16[64,5632]{1,0:T(8,128)(2,1)S(1)} %constant_dynamic-update-slice_fusion.4.refs_0_), channel_id=1, source_target_pairs={{0,16},{4,20},{8,24},{12,28},{16,0},{20,4},{24,8},{28,12},{1,17},{... | collective-permute-start | bytes 2162696 | tf_op jit(solution)/shard_map/ppermute | solution.py:775
  31.1 1.1 collective-permute-start.15
  32.3 0.6 copy-done.30
  33.0 8.3 %project.1 = (bf16[1536,512]{1,0:T(8,128)(2,1)}, bf16[512,1536]{1,0:T(8,128)(2,1)}, bf16[1536,512]{1,0:T(8,128)(2,1)}, bf16[1536,512]{1,0:T(8,128)(2,1)}, bf16[1...) custom-call(s32[32]{0:T(128)} %pad_add_fusion.order, ...), custom_call_target="tpu_custom_call" | custom-call | flops 2415919104 | bytes 12582912 | tf_op jit(solution)/shard_map/project/pallas_call | solution.py:104
  41.3 10.6 %attend.1 = (f32[1536,512]{1,0:T(8,128)}, f32[8,1536]{1,0:T(8,128)}) custom-call(s32[1536]{0:T(1024)} %segment.3, s32[1,1536]{1,0:T(1,128)} %reshape.55.segment_row, bf16[1536,512]{1,0:T(8,128)(2,1)} %get-tuple-element.80.query_in, bf16[1536,512]{1,0:T(8,128)(2,1)} %get-tuple-element.81.key_in, bf16[512,1536]{1,0:T(8,128)(2,1)} %get-tuple-element.82.value_t_in), custom_call_target="tpu_custom_call" | custom-call | flops 9663676416 | bytes 6291456 | tf_op jit(solution)/shard_map/attend/pallas_call | solution.py:243
  51.9 10.1 %collective-permute-done.14.refs_1_ = bf16[64,5632]{1,0:T(8,128)(2,1)S(1)} collective-permute-done((bf16[64,5632]{1,0:T(8,128)(2,1)S(1)}, bf16[64,5632]{1,0:T(8,128)(2,1)S(1)}, u32[]{:S(2)}, u32[]{:S(2)}) %collective-permute-start.14) | collective-permute-done | bytes 720928 | tf_op jit(solution)/shard_map/ppermute | solution.py:775
  62.0 1.1 collective-permute-done.15.refs_2_
  63.1 0.8 copy-done.11
  63.9 1.3 collective-permute-start.17
  65.3 0.4 collective-permute-start.19
  65.8 1.3 collective-permute-done.17.refs_5_
  67.1 1.0 collective-permute-done.18.refs_6_
  68.1 1.0 collective-permute-done.19.refs_7_
  69.1 0.9 copy-done.24
  70.1 43.6 %feed_forward.1 = (bf16[1536,512]{1,0:T(8,128)(2,1)}, f32[1536,512]{1,0:T(8,128)}, bf16[1536,512]{1,0:T(8,128)(2,1)}, bf16[1536,512]{1,0:T(8,128)(2,1)}, f32[8,1...) custom-call(s32[1]{0:T(128)} %bitcast.device.me.refs_1_.refs_3_, ...), custom_call_target="tpu_custom_call" | custom-call | flops 26575110144 | bytes 25165824 | tf_op jit(solution)/shard_map/feed_forward/pallas_call | solution.py:594
  113.6 0.4 collective-permute-start.20
  114.1 5.5 %collective-permute-done.20.refs_0_ = bf16[16,192,512]{2,1,0:T(8,128)(2,1)S(1)} collective-permute-done((bf16[16,192,512]{2,1,0:T(8,128)(2,1)}, bf16[16,192,512]{2,1,0:T(8,128)(2,1)S(1)}, u32[]{:S(2)}, u32[]{:S(2)}) %collective-permute-start.20) | collective-permute-done | bytes 3145760 | tf_op jit(solution)/shard_map/ppermute | solution.py:775
  119.6 1.9 copy-done
  121.5 1.1 add_split.4
  122.6 0.9 copy-done.3
  123.5 0.6 collective-permute-start.21
  124.1 0.8 collective-permute-start.22
  124.9 2.1 %collective-permute-start.23 = (bf16[4,192,512]{2,1,0:T(8,128)(2,1)S(1)}, bf16[4,192,512]{2,1,0:T(8,128)(2,1)S(1)}, u32[]{:S(2)}, u32[]{:S(2)}) collective-permute-start(bf16[4,192,512]{2,1,0:T(8,128)(2,1)S(1)} %get-tuple-element.109), channel_id=1, source_target_pairs={{0,24},{4,28},{8,16},{12,20},{16,8},{20,12},{24,0},{28,4},{1,25},{... | collective-permute-start | bytes 2359304 | tf_op jit(solution)/shard_map/ppermute | solution.py:775
  127.0 16.4 %attend_back.1 = (bf16[1536,512]{1,0:T(8,128)(2,1)}, bf16[1536,512]{1,0:T(8,128)(2,1)}, bf16[1536,512]{1,0:T(8,128)(2,1)}, bf16[16,16,1536]{2,1,0:T(8,128)(2,1)}, bf16[16,16,1536]{2,1,0:T(8,128)(2,1)}) custom-call(s32[1]{0:T(128)} %bitcast.device.me.refs_1_.refs_3_, s32[1536]{0:T(1024)} %segment.3, s32[1,1536]{1,0:T(1,128)} %reshape.55.segment_row, ...), custom_call_target="tpu_custom_call" | custom-call | flops 24159191040 | bytes 8388608 | tf_op jit(solution)/shard_map/attend_back/pallas_call | solution.py:400
  143.4 0.4 collective-permute-done.21.refs_1_.refs_0_
  143.9 17.1 %collective-permute-done.23.refs_3_.refs_2_ = bf16[4,192,512]{2,1,0:T(8,128)(2,1)S(1)} collective-permute-done((bf16[4,192,512]{2,1,0:T(8,128)(2,1)S(1)}, bf16[4,192,512]{2,1,0:T(8,128)(2,1)S(1)}, u32[]{:S(2)}, u32[]{:S(2)}) %collective-permute-start.23) | collective-permute-done | bytes 786464 | tf_op jit(solution)/shard_map/ppermute | solution.py:775
  161.0 1.1 copy-done.4
  162.1 1.4 add_split.5
  163.6 1.2 add_split.6
  164.8 0.7 copy-done.5
  165.5 0.9 collective-permute-start.25
  166.4 0.6 pad_add_fusion.1.device
  167.0 3.8 %collective-permute-start.33 = (bf16[1,192,512]{2,1,0:T(8,128)(2,1)S(1)}, bf16[1,192,512]{2,1,0:T(8,128)(2,1)S(1)}, u32[]{:S(2)}, u32[]{:S(2)}) collective-permute-start(bf16[1,192,512]{2,1,0:T(8,128)(2,1)S(1)} %get-tuple-element.124), channel_id=1, source_target_pairs={{0,3},{1,2},{2,1},{3,0},{4,7},{5,6},{6,5},{7,4},{8,11},{9,10},{10,... | collective-permute-start | bytes 589832 | tf_op jit(solution)/shard_map/ppermute | solution.py:775
  170.9 0.6 collective-permute-start.32
  171.4 1.4 collective-permute-start.26
  172.8 1.4 collective-permute-start.27
  174.2 7.2 %finish.2 = (f32[1536,512]{1,0:T(8,128)}, f32[8,128]{1,0:T(8,128)}) custom-call(bf16[1536,512]{1,0:T(8,128)(2,1)} %tokens.7, bf16[1536,512]{1,0:T(8,128)(2,1)} %get-tuple-element.91.zeta_one_low, f32[1536,512]{1,0:T(8,128)} %get-tuple-element.92.grad_middle, bf16[512,1536]{1,0:T(8,128)(2,1)} %get-tuple-element.93.weights, ...), custom_call_target="tpu_custom_call" | custom-call | flops 2147483648 | bytes 10485760 | tf_op jit(solution)/shard_map/finish/pallas_call | solution.py:660
  181.3 0.3 collective-permute-done.26.refs_1_
  181.6 0.7 copy-done.12
  182.3 0.4 add_split.7
  182.7 0.6 copy-done.10
  183.3 1.5 collective-permute-start.28
  184.8 2.6 %collective-permute-start.29 = (bf16[1,16,1536]{2,1,0:T(8,128)(2,1)S(1)}, bf16[1,16,1536]{2,1,0:T(8,128)(2,1)S(1)}, u32[]{:S(2)}, u32[]{:S(2)}) collective-permute-start(bf16[1,16,1536]{2,1,0:T(8,128)(2,1)S(1)} %get-tuple-element.120), channel_id=1, source_target_pairs={{0,2},{1,3},{2,0},{3,1},{4,6},{5,7},{6,4},{7,5},{8,10},{9,11},{10,... | collective-permute-start | bytes 147464 | tf_op jit(solution)/shard_map/ppermute | solution.py:775
  187.4 0.3 collective-permute-start.30
  187.7 5.1 %finish.3 = (f32[1536,512]{1,0:T(8,128)}, f32[8,128]{1,0:T(8,128)}) custom-call(bf16[1536,512]{1,0:T(8,128)(2,1)} %tokens.7, bf16[1536,512]{1,0:T(8,128)(2,1)} %get-tuple-element.91.zeta_one_low, f32[1536,512]{1,0:T(8,128)} %get-tuple-element.92.grad_middle, bf16[512,1536]{1,0:T(8,128)(2,1)} %get-tuple-element.93.weights, ...), custom_call_target="tpu_custom_call", output_to_operand_aliasing={{0}: (10, {})} | custom-call | flops 1073741824 | bytes 5242880 | tf_op jit(solution)/shard_map/finish/pallas_call | solution.py:660
  192.9 0.4 collective-permute-done.30
  193.9 2.5 %close.1 = (f32[16,512]{1,0:T(8,128)}, f32[16,512]{1,0:T(8,128)}, f32[16,512]{1,0:T(8,128)}, f32[16,512]{1,0:T(8,128)}, f32[16,512]{1,0:T(8,128)}, /*index=5*/f3...) custom-call(s32[2]{0:T(128)} %pad_add_fusion.1.device, ...), custom_call_target="tpu_custom_call" | custom-call | tf_op jit(solution)/shard_map/close/pallas_call | solution.py:759
  (92 shorter events, 1.0 us)
Async XLA Ops:
  2.6 13.6 %collective-permute-start = (bf16[16,1664]{1,0:T(8,128)(2,1)}, bf16[16,1664]{1,0:T(8,128)(2,1)S(1)}, u32[]{:S(2)}, u32[]{:S(2)}) collective-permute-start(bf16[16,1664]{1,0:T(8,128)(2,1)} %get-tuple-element.77), channel_id=1, source_target_pairs={{0,1},{1,0},{2,3},{3,2},{4,5},{5,4},{6,7},{7,6},{8,9},{9,8},{10,11... | collective-permute-start | bytes 159752 | tf_op jit(solution)/shard_map/ppermute | solution.py:775
  5.6 10.6 %collective-permute-start.1 = (bf16[16,1664]{1,0:T(8,128)(2,1)}, bf16[16,1664]{1,0:T(8,128)(2,1)S(1)}, u32[]{:S(2)}, u32[]{:S(2)}) collective-permute-start(bf16[16,1664]{1,0:T(8,128)(2,1)} %get-tuple-element.77), channel_id=1, source_target_pairs={{0,2},{1,3},{2,0},{3,1},{4,6},{5,7},{6,4},{7,5},{8,10},{9,11},{10,... | collective-permute-start | bytes 159752 | tf_op jit(solution)/shard_map/ppermute | solution.py:775
  8.2 8.1 %collective-permute-start.2 = (bf16[16,1664]{1,0:T(8,128)(2,1)}, bf16[16,1664]{1,0:T(8,128)(2,1)S(1)}, u32[]{:S(2)}, u32[]{:S(2)}) collective-permute-start(bf16[16,1664]{1,0:T(8,128)(2,1)} %get-tuple-element.77), channel_id=1, source_target_pairs={{0,3},{1,2},{2,1},{3,0},{4,7},{5,6},{6,5},{7,4},{8,11},{9,10},{10,... | collective-permute-start | bytes 159752 | tf_op jit(solution)/shard_map/ppermute | solution.py:775
  8.2 11.4 %collective-permute-start.10 = (bf16[16,5632]{1,0:T(8,128)(2,1)}, bf16[16,5632]{1,0:T(8,128)(2,1)S(1)}, u32[]{:S(2)}, u32[]{:S(2)}) collective-permute-start(bf16[16,5632]{1,0:T(8,128)(2,1)} %get-tuple-element.85), channel_id=1, source_target_pairs={{0,1},{1,0},{2,3},{3,2},{4,5},{5,4},{6,7},{7,6},{8,9},{9,8},{10,11... | collective-permute-start | bytes 540680 | tf_op jit(solution)/shard_map/ppermute | solution.py:775
  9.1 17.2 %collective-permute-start.11 = (bf16[16,5632]{1,0:T(8,128)(2,1)}, bf16[16,5632]{1,0:T(8,128)(2,1)S(1)}, u32[]{:S(2)}, u32[]{:S(2)}) collective-permute-start(bf16[16,5632]{1,0:T(8,128)(2,1)} %get-tuple-element.85), channel_id=1, source_target_pairs={{0,2},{1,3},{2,0},{3,1},{4,6},{5,7},{6,4},{7,5},{8,10},{9,11},{10,... | collective-permute-start | bytes 540680 | tf_op jit(solution)/shard_map/ppermute | solution.py:775
  16.2 12.4 %collective-permute-start.12 = (bf16[16,5632]{1,0:T(8,128)(2,1)}, bf16[16,5632]{1,0:T(8,128)(2,1)S(1)}, u32[]{:S(2)}, u32[]{:S(2)}) collective-permute-start(bf16[16,5632]{1,0:T(8,128)(2,1)} %get-tuple-element.85), channel_id=1, source_target_pairs={{0,3},{1,2},{2,1},{3,0},{4,7},{5,6},{6,5},{7,4},{8,11},{9,10},{10,... | collective-permute-start | bytes 540680 | tf_op jit(solution)/shard_map/ppermute | solution.py:775
  16.3 16.7 %copy-start.20 = (bf16[64,1664]{1,0:T(8,128)(2,1)}, bf16[64,1664]{1,0:T(8,128)(2,1)S(1)}, u32[]{:S(2)}) copy-start(bf16[64,1664]{1,0:T(8,128)(2,1)S(1)} %constant_dynamic-update-slice_fusion.refs_0_) | copy-start | bytes 638980
  16.3 10.0 %collective-permute-start.3 = (bf16[64,1664]{1,0:T(8,128)(2,1)S(1)}, bf16[64,1664]{1,0:T(8,128)(2,1)S(1)}, u32[]{:S(2)}, u32[]{:S(2)}) collective-permute-start(bf16[64,1664]{1,0:T(8,128)(2,1)S(1)} %constant_dynamic-update-slice_fusion.refs_0_), channel_id=1, source_target_pairs={{0,8},{4,12},{8,0},{12,4},{16,24},{20,28},{24,16},{28,20},{1,9},{5... | collective-permute-start | bytes 638984 | tf_op jit(solution)/shard_map/ppermute | solution.py:775
  18.1 10.0 %collective-permute-start.4 = (bf16[64,1664]{1,0:T(8,128)(2,1)S(1)}, bf16[64,1664]{1,0:T(8,128)(2,1)S(1)}, u32[]{:S(2)}, u32[]{:S(2)}) collective-permute-start(bf16[64,1664]{1,0:T(8,128)(2,1)S(1)} %constant_dynamic-update-slice_fusion.refs_0_), channel_id=1, source_target_pairs={{0,16},{4,20},{8,24},{12,28},{16,0},{20,4},{24,8},{28,12},{1,17},{... | collective-permute-start | bytes 638984 | tf_op jit(solution)/shard_map/ppermute | solution.py:775
  19.6 8.5 %collective-permute-start.5 = (bf16[64,1664]{1,0:T(8,128)(2,1)S(1)}, bf16[64,1664]{1,0:T(8,128)(2,1)S(1)}, u32[]{:S(2)}, u32[]{:S(2)}) collective-permute-start(bf16[64,1664]{1,0:T(8,128)(2,1)S(1)} %constant_dynamic-update-slice_fusion.refs_0_), channel_id=1, source_target_pairs={{0,24},{4,28},{8,16},{12,20},{16,8},{20,12},{24,0},{28,4},{1,25},{... | collective-permute-start | bytes 638984 | tf_op jit(solution)/shard_map/ppermute | solution.py:775
  26.3 2.8 %collective-permute-start.6 = (bf16[64,1664]{1,0:T(8,128)(2,1)S(1)}, bf16[64,1664]{1,0:T(8,128)(2,1)S(1)}, u32[]{:S(2)}, u32[]{:S(2)}) collective-permute-start(bf16[64,1664]{1,0:T(8,128)(2,1)S(1)} %constant_dynamic-update-slice_fusion.refs_0_), channel_id=1, source_target_pairs={{0,4},{4,0},{8,12},{12,8},{16,20},{20,16},{24,28},{28,24},{1,5},{5... | collective-permute-start | bytes 638984 | tf_op jit(solution)/shard_map/ppermute | solution.py:775
  26.3 6.6 %copy-start.25 = (bf16[64,1664]{1,0:T(8,128)(2,1)}, bf16[64,1664]{1,0:T(8,128)(2,1)S(1)}, u32[]{:S(2)}) copy-start(bf16[64,1664]{1,0:T(8,128)(2,1)S(1)} %collective-permute-done.3.refs_1_) | copy-start | bytes 638980
  26.3 4.8 %collective-permute-start.7 = (bf16[64,1664]{1,0:T(8,128)(2,1)S(1)}, bf16[64,1664]{1,0:T(8,128)(2,1)S(1)}, u32[]{:S(2)}, u32[]{:S(2)}) collective-permute-start(bf16[64,1664]{1,0:T(8,128)(2,1)S(1)} %collective-permute-done.3.refs_1_), channel_id=1, source_target_pairs={{0,4},{4,0},{8,12},{12,8},{16,20},{20,16},{24,28},{28,24},{1,5},{5... | collective-permute-start | bytes 638984 | tf_op jit(solution)/shard_map/ppermute | solution.py:775
  28.1 4.1 %copy-start.26 = (bf16[64,1664]{1,0:T(8,128)(2,1)}, bf16[64,1664]{1,0:T(8,128)(2,1)S(1)}, u32[]{:S(2)}) copy-start(bf16[64,1664]{1,0:T(8,128)(2,1)S(1)} %collective-permute-done.4.refs_2_) | copy-start | bytes 638980
  28.1 4.1 %collective-permute-start.8 = (bf16[64,1664]{1,0:T(8,128)(2,1)S(1)}, bf16[64,1664]{1,0:T(8,128)(2,1)S(1)}, u32[]{:S(2)}, u32[]{:S(2)}) collective-permute-start(bf16[64,1664]{1,0:T(8,128)(2,1)S(1)} %collective-permute-done.4.refs_2_), channel_id=1, source_target_pairs={{0,4},{4,0},{8,12},{12,8},{16,20},{20,16},{24,28},{28,24},{1,5},{5... | collective-permute-start | bytes 638984 | tf_op jit(solution)/shard_map/ppermute | solution.py:775
  28.1 4.1 %copy-start.27 = (bf16[64,1664]{1,0:T(8,128)(2,1)}, bf16[64,1664]{1,0:T(8,128)(2,1)S(1)}, u32[]{:S(2)}) copy-start(bf16[64,1664]{1,0:T(8,128)(2,1)S(1)} %collective-permute-done.5.refs_3_) | copy-start | bytes 638980
  28.1 4.8 %collective-permute-start.9 = (bf16[64,1664]{1,0:T(8,128)(2,1)S(1)}, bf16[64,1664]{1,0:T(8,128)(2,1)}, u32[]{:S(2)}, u32[]{:S(2)}) collective-permute-start(bf16[64,1664]{1,0:T(8,128)(2,1)S(1)} %collective-permute-done.5.refs_3_), channel_id=1, source_target_pairs={{0,4},{4,0},{8,12},{12,8},{16,20},{20,16},{24,28},{28,24},{1,5},{5... | collective-permute-start | bytes 638984 | tf_op jit(solution)/shard_map/ppermute | solution.py:775
  28.7 12.6 %copy-start.19 = (bf16[64,5632]{1,0:T(8,128)(2,1)}, bf16[64,5632]{1,0:T(8,128)(2,1)S(1)}, u32[]{:S(2)}) copy-start(bf16[64,5632]{1,0:T(8,128)(2,1)S(1)} %constant_dynamic-update-slice_fusion.4.refs_0_) | copy-start | bytes 2162692
  28.7 23.2 %collective-permute-start.13 = (bf16[64,5632]{1,0:T(8,128)(2,1)S(1)}, bf16[64,5632]{1,0:T(8,128)(2,1)S(1)}, u32[]{:S(2)}, u32[]{:S(2)}) collective-permute-start(bf16[64,5632]{1,0:T(8,128)(2,1)S(1)} %constant_dynamic-update-slice_fusion.4.refs_0_), channel_id=1, source_target_pairs={{0,8},{4,12},{8,0},{12,4},{16,24},{20,28},{24,16},{28,20},{1,9},{5... | collective-permute-start | bytes 2162696 | tf_op jit(solution)/shard_map/ppermute | solution.py:775
  29.1 3.1 %copy-start.28 = (bf16[64,1664]{1,0:T(8,128)(2,1)}, bf16[64,1664]{1,0:T(8,128)(2,1)S(1)}, u32[]{:S(2)}) copy-start(bf16[64,1664]{1,0:T(8,128)(2,1)S(1)} %collective-permute-done.6.refs_4_) | copy-start | bytes 638980
  29.1 32.9 %collective-permute-start.14 = (bf16[64,5632]{1,0:T(8,128)(2,1)S(1)}, bf16[64,5632]{1,0:T(8,128)(2,1)S(1)}, u32[]{:S(2)}, u32[]{:S(2)}) collective-permute-start(bf16[64,5632]{1,0:T(8,128)(2,1)S(1)} %constant_dynamic-update-slice_fusion.4.refs_0_), channel_id=1, source_target_pairs={{0,16},{4,20},{8,24},{12,28},{16,0},{20,4},{24,8},{28,12},{1,17},{... | collective-permute-start | bytes 2162696 | tf_op jit(solution)/shard_map/ppermute | solution.py:775
  31.1 1.1 copy-start.29
  31.1 32.0 %collective-permute-start.15 = (bf16[64,5632]{1,0:T(8,128)(2,1)S(1)}, bf16[64,5632]{1,0:T(8,128)(2,1)S(1)}, u32[]{:S(2)}, u32[]{:S(2)}) collective-permute-start(bf16[64,5632]{1,0:T(8,128)(2,1)S(1)} %constant_dynamic-update-slice_fusion.4.refs_0_), channel_id=1, source_target_pairs={{0,24},{4,28},{8,16},{12,20},{16,8},{20,12},{24,0},{28,4},{1,25},{... | collective-permute-start | bytes 2162696 | tf_op jit(solution)/shard_map/ppermute | solution.py:775
  32.3 0.7 copy-start.30
  32.3 33.5 %collective-permute-start.16 = (bf16[64,5632]{1,0:T(8,128)(2,1)S(1)}, bf16[64,5632]{1,0:T(8,128)(2,1)S(1)}, u32[]{:S(2)}, u32[]{:S(2)}) collective-permute-start(bf16[64,5632]{1,0:T(8,128)(2,1)S(1)} %constant_dynamic-update-slice_fusion.4.refs_0_), channel_id=1, source_target_pairs={{0,4},{4,0},{8,12},{12,8},{16,20},{20,16},{24,28},{28,24},{1,5},{5... | collective-permute-start | bytes 2162696 | tf_op jit(solution)/shard_map/ppermute | solution.py:775
  63.1 0.8 copy-start.11
  63.9 6.1 %copy-start.7 = (bf16[64,5632]{1,0:T(8,128)(2,1)}, bf16[64,5632]{1,0:T(8,128)(2,1)S(1)}, u32[]{:S(2)}) copy-start(bf16[64,5632]{1,0:T(8,128)(2,1)S(1)} %get-tuple-element.87.refs_1_) | copy-start | bytes 2162692
  63.9 6.1 %copy-start.8 = (bf16[64,5632]{1,0:T(8,128)(2,1)}, bf16[64,5632]{1,0:T(8,128)(2,1)S(1)}, u32[]{:S(2)}) copy-start(bf16[64,5632]{1,0:T(8,128)(2,1)S(1)} %get-tuple-element.88.refs_2_) | copy-start | bytes 2162692
  63.9 6.1 %copy-start.9 = (bf16[64,5632]{1,0:T(8,128)(2,1)}, bf16[64,5632]{1,0:T(8,128)(2,1)S(1)}, u32[]{:S(2)}) copy-start(bf16[64,5632]{1,0:T(8,128)(2,1)S(1)} %get-tuple-element.89.refs_3_) | copy-start | bytes 2162692
  63.9 3.1 %collective-permute-start.17 = (bf16[64,5632]{1,0:T(8,128)(2,1)S(1)}, bf16[64,5632]{1,0:T(8,128)(2,1)S(1)}, u32[]{:S(2)}, u32[]{:S(2)}) collective-permute-start(bf16[64,5632]{1,0:T(8,128)(2,1)S(1)} %get-tuple-element.87.refs_1_), channel_id=1, source_target_pairs={{0,4},{4,0},{8,12},{12,8},{16,20},{20,16},{24,28},{28,24},{1,5},{5... | collective-permute-start | bytes 2162696 | tf_op jit(solution)/shard_map/ppermute | solution.py:775
  65.2 2.8 %collective-permute-start.18 = (bf16[64,5632]{1,0:T(8,128)(2,1)S(1)}, bf16[64,5632]{1,0:T(8,128)(2,1)S(1)}, u32[]{:S(2)}, u32[]{:S(2)}) collective-permute-start(bf16[64,5632]{1,0:T(8,128)(2,1)S(1)} %get-tuple-element.88.refs_2_), channel_id=1, source_target_pairs={{0,4},{4,0},{8,12},{12,8},{16,20},{20,16},{24,28},{28,24},{1,5},{5... | collective-permute-start | bytes 2162696 | tf_op jit(solution)/shard_map/ppermute | solution.py:775
  65.3 3.8 %collective-permute-start.19 = (bf16[64,5632]{1,0:T(8,128)(2,1)S(1)}, bf16[64,5632]{1,0:T(8,128)(2,1)S(1)}, u32[]{:S(2)}, u32[]{:S(2)}) collective-permute-start(bf16[64,5632]{1,0:T(8,128)(2,1)S(1)} %get-tuple-element.89.refs_3_), channel_id=1, source_target_pairs={{0,4},{4,0},{8,12},{12,8},{16,20},{20,16},{24,28},{28,24},{1,5},{5... | collective-permute-start | bytes 2162696 | tf_op jit(solution)/shard_map/ppermute | solution.py:775
  65.8 4.3 %copy-start.21 = (bf16[64,5632]{1,0:T(8,128)(2,1)}, bf16[64,5632]{1,0:T(8,128)(2,1)S(1)}, u32[]{:S(2)}) copy-start(bf16[64,5632]{1,0:T(8,128)(2,1)S(1)} %collective-permute-done.16.refs_4_) | copy-start | bytes 2162692
  67.1 2.1 %copy-start.22 = (bf16[64,5632]{1,0:T(8,128)(2,1)}, bf16[64,5632]{1,0:T(8,128)(2,1)S(1)}, u32[]{:S(2)}) copy-start(bf16[64,5632]{1,0:T(8,128)(2,1)S(1)} %collective-permute-done.17.refs_5_) | copy-start | bytes 2162692
  68.1 1.0 copy-start.23
  69.1 0.9 copy-start.24
  113.6 5.9 %collective-permute-start.20 = (bf16[16,192,512]{2,1,0:T(8,128)(2,1)}, bf16[16,192,512]{2,1,0:T(8,128)(2,1)S(1)}, u32[]{:S(2)}, u32[]{:S(2)}) collective-permute-start(bf16[16,192,512]{2,1,0:T(8,128)(2,1)} %bitcast.24), channel_id=1, source_target_pairs={{0,4},{4,0},{8,12},{12,8},{16,20},{20,16},{24,28},{28,24},{1,5},{5... | collective-permute-start | bytes 9437192 | tf_op jit(solution)/shard_map/ppermute | solution.py:775
  119.6 1.9 copy-start
  122.6 0.9 copy-start.3
  123.5 20.4 %collective-permute-start.21 = (bf16[4,192,512]{2,1,0:T(8,128)(2,1)S(1)}, bf16[4,192,512]{2,1,0:T(8,128)(2,1)S(1)}, u32[]{:S(2)}, u32[]{:S(2)}) collective-permute-start(bf16[4,192,512]{2,1,0:T(8,128)(2,1)S(1)} %get-tuple-element.107), channel_id=1, source_target_pairs={{0,8},{4,12},{8,0},{12,4},{16,24},{20,28},{24,16},{28,20},{1,9},{5... | collective-permute-start | bytes 2359304 | tf_op jit(solution)/shard_map/ppermute | solution.py:775
  124.1 19.8 %collective-permute-start.22 = (bf16[4,192,512]{2,1,0:T(8,128)(2,1)S(1)}, bf16[4,192,512]{2,1,0:T(8,128)(2,1)S(1)}, u32[]{:S(2)}, u32[]{:S(2)}) collective-permute-start(bf16[4,192,512]{2,1,0:T(8,128)(2,1)S(1)} %get-tuple-element.108), channel_id=1, source_target_pairs={{0,16},{4,20},{8,24},{12,28},{16,0},{20,4},{24,8},{28,12},{1,17},{... | collective-permute-start | bytes 2359304 | tf_op jit(solution)/shard_map/ppermute | solution.py:775
  124.9 36.1 %collective-permute-start.23 = (bf16[4,192,512]{2,1,0:T(8,128)(2,1)S(1)}, bf16[4,192,512]{2,1,0:T(8,128)(2,1)S(1)}, u32[]{:S(2)}, u32[]{:S(2)}) collective-permute-start(bf16[4,192,512]{2,1,0:T(8,128)(2,1)S(1)} %get-tuple-element.109), channel_id=1, source_target_pairs={{0,24},{4,28},{8,16},{12,20},{16,8},{20,12},{24,0},{28,4},{1,25},{... | collective-permute-start | bytes 2359304 | tf_op jit(solution)/shard_map/ppermute | solution.py:775
  161.0 1.1 copy-start.4
  161.0 2.6 %copy-start.1 = (bf16[16,16,1536]{2,1,0:T(8,128)(2,1)S(1)}, bf16[16,16,1536]{2,1,0:T(8,128)(2,1)}, u32[]{:S(2)}) copy-start(bf16[16,16,1536]{2,1,0:T(8,128)(2,1)} %get-tuple-element.105.own) | copy-start | bytes 2359300
  161.0 2.6 %collective-permute-start.24 = (bf16[16,16,1536]{2,1,0:T(8,128)(2,1)}, bf16[16,16,1536]{2,1,0:T(8,128)(2,1)S(1)}, u32[]{:S(2)}, u32[]{:S(2)}) collective-permute-start(bf16[16,16,1536]{2,1,0:T(8,128)(2,1)} %hold.3), channel_id=1, source_target_pairs={{0,4},{4,0},{8,12},{12,8},{16,20},{20,16},{24,28},{28,24},{1,5},{5... | collective-permute-start | bytes 2359304 | tf_op jit(solution)/shard_map/ppermute | solution.py:775
  163.5 17.8 %copy-start.2 = (bf16[1,192,512]{2,1,0:T(8,128)(2,1)}, bf16[1,192,512]{2,1,0:T(8,128)(2,1)S(1)}, u32[]{:S(2)}) copy-start(bf16[1,192,512]{2,1,0:T(8,128)(2,1)S(1)} %get-tuple-element.110.refs_1_) | copy-start | bytes 589828
  164.8 0.7 copy-start.5
  165.5 7.3 %collective-permute-start.25 = (bf16[4,16,1536]{2,1,0:T(8,128)(2,1)S(1)}, bf16[4,16,1536]{2,1,0:T(8,128)(2,1)S(1)}, u32[]{:S(2)}, u32[]{:S(2)}) collective-permute-start(bf16[4,16,1536]{2,1,0:T(8,128)(2,1)S(1)} %get-tuple-element.112), channel_id=1, source_target_pairs={{0,8},{4,12},{8,0},{12,4},{16,24},{20,28},{24,16},{28,20},{1,9},{5... | collective-permute-start | bytes 589832 | tf_op jit(solution)/shard_map/ppermute | solution.py:775
  167.0 20.4 %collective-permute-start.33 = (bf16[1,192,512]{2,1,0:T(8,128)(2,1)S(1)}, bf16[1,192,512]{2,1,0:T(8,128)(2,1)S(1)}, u32[]{:S(2)}, u32[]{:S(2)}) collective-permute-start(bf16[1,192,512]{2,1,0:T(8,128)(2,1)S(1)} %get-tuple-element.124), channel_id=1, source_target_pairs={{0,3},{1,2},{2,1},{3,0},{4,7},{5,6},{6,5},{7,4},{8,11},{9,10},{10,... | collective-permute-start | bytes 589832 | tf_op jit(solution)/shard_map/ppermute | solution.py:775
  170.9 22.0 %collective-permute-start.31 = (bf16[1,192,512]{2,1,0:T(8,128)(2,1)S(1)}, bf16[1,192,512]{2,1,0:T(8,128)(2,1)S(1)}, u32[]{:S(2)}, u32[]{:S(2)}) collective-permute-start(bf16[1,192,512]{2,1,0:T(8,128)(2,1)S(1)} %get-tuple-element.122), channel_id=1, source_target_pairs={{0,1},{1,0},{2,3},{3,2},{4,5},{5,4},{6,7},{7,6},{8,9},{9,8},{10,11... | collective-permute-start | bytes 589832 | tf_op jit(solution)/shard_map/ppermute | solution.py:775
  170.9 22.0 %collective-permute-start.32 = (bf16[1,192,512]{2,1,0:T(8,128)(2,1)S(1)}, bf16[1,192,512]{2,1,0:T(8,128)(2,1)S(1)}, u32[]{:S(2)}, u32[]{:S(2)}) collective-permute-start(bf16[1,192,512]{2,1,0:T(8,128)(2,1)S(1)} %get-tuple-element.123), channel_id=1, source_target_pairs={{0,2},{1,3},{2,0},{3,1},{4,6},{5,7},{6,4},{7,5},{8,10},{9,11},{10,... | collective-permute-start | bytes 589832 | tf_op jit(solution)/shard_map/ppermute | solution.py:775
  171.4 10.2 %collective-permute-start.26 = (bf16[4,16,1536]{2,1,0:T(8,128)(2,1)S(1)}, bf16[4,16,1536]{2,1,0:T(8,128)(2,1)S(1)}, u32[]{:S(2)}, u32[]{:S(2)}) collective-permute-start(bf16[4,16,1536]{2,1,0:T(8,128)(2,1)S(1)} %get-tuple-element.113), channel_id=1, source_target_pairs={{0,16},{4,20},{8,24},{12,28},{16,0},{20,4},{24,8},{28,12},{1,17},{... | collective-permute-start | bytes 589832 | tf_op jit(solution)/shard_map/ppermute | solution.py:775
  172.8 8.8 %collective-permute-start.27 = (bf16[4,16,1536]{2,1,0:T(8,128)(2,1)S(1)}, bf16[4,16,1536]{2,1,0:T(8,128)(2,1)S(1)}, u32[]{:S(2)}, u32[]{:S(2)}) collective-permute-start(bf16[4,16,1536]{2,1,0:T(8,128)(2,1)S(1)} %get-tuple-element.114), channel_id=1, source_target_pairs={{0,24},{4,28},{8,16},{12,20},{16,8},{20,12},{24,0},{28,4},{1,25},{... | collective-permute-start | bytes 589832 | tf_op jit(solution)/shard_map/ppermute | solution.py:775
  174.2 7.5 %copy-start.6 = (bf16[4,16,1536]{2,1,0:T(8,128)(2,1)S(1)}, bf16[4,16,1536]{2,1,0:T(8,128)(2,1)}, u32[]{:S(2)}) copy-start(bf16[4,16,1536]{2,1,0:T(8,128)(2,1)} %copy-done.5) | copy-start | bytes 589828
  181.6 0.7 copy-start.12
  183.3 9.6 %collective-permute-start.28 = (bf16[1,16,1536]{2,1,0:T(8,128)(2,1)S(1)}, bf16[1,16,1536]{2,1,0:T(8,128)(2,1)S(1)}, u32[]{:S(2)}, u32[]{:S(2)}) collective-permute-start(bf16[1,16,1536]{2,1,0:T(8,128)(2,1)S(1)} %get-tuple-element.119), channel_id=1, source_target_pairs={{0,1},{1,0},{2,3},{3,2},{4,5},{5,4},{6,7},{7,6},{8,9},{9,8},{10,11... | collective-permute-start | bytes 147464 | tf_op jit(solution)/shard_map/ppermute | solution.py:775
  184.8 8.1 %collective-permute-start.29 = (bf16[1,16,1536]{2,1,0:T(8,128)(2,1)S(1)}, bf16[1,16,1536]{2,1,0:T(8,128)(2,1)S(1)}, u32[]{:S(2)}, u32[]{:S(2)}) collective-permute-start(bf16[1,16,1536]{2,1,0:T(8,128)(2,1)S(1)} %get-tuple-element.120), channel_id=1, source_target_pairs={{0,2},{1,3},{2,0},{3,1},{4,6},{5,7},{6,4},{7,5},{8,10},{9,11},{10,... | collective-permute-start | bytes 147464 | tf_op jit(solution)/shard_map/ppermute | solution.py:775
  187.4 5.4 %copy-start.13 = (bf16[1,192,512]{2,1,0:T(8,128)(2,1)}, bf16[1,192,512]{2,1,0:T(8,128)(2,1)S(1)}, u32[]{:S(2)}) copy-start(bf16[1,192,512]{2,1,0:T(8,128)(2,1)S(1)} %collective-permute-done.33) | copy-start | bytes 589828
  187.4 5.9 %collective-permute-start.30 = (bf16[1,16,1536]{2,1,0:T(8,128)(2,1)S(1)}, bf16[1,16,1536]{2,1,0:T(8,128)(2,1)S(1)}, u32[]{:S(2)}, u32[]{:S(2)}) collective-permute-start(bf16[1,16,1536]{2,1,0:T(8,128)(2,1)S(1)} %get-tuple-element.121), channel_id=1, source_target_pairs={{0,3},{1,2},{2,1},{3,0},{4,7},{5,6},{6,5},{7,4},{8,11},{9,10},{10,... | collective-permute-start | bytes 147464 | tf_op jit(solution)/shard_map/ppermute | solution.py:775
  192.9 0.7 copy-start.14
  192.9 0.7 copy-start.15
  192.9 0.7 copy-start.16
  192.9 0.7 copy-start.17
  193.3 0.6 copy-start.18
  (1 other events, 0.6 us)
